TPU v7x, 512 devices: a whole 4x8x8 slice. The times are simulated.
512 devices in a mesh: ctx: 16 (over y, x_lo), fsdp: 32 (over z, x_hi, core).
Axes of the slice: x: 4 (x_hi: 2, x_lo: 2; x = x_hi * 2 + x_lo), y: 8, z: 8, core: 2. Of those that a mesh axis runs over, the one named last changes fastest.
Arguments:
- asking_vectors_stacked: bfloat16 [65536, 2048], P(('ctx', 'fsdp')), may hold values from -10 to 10
- lookup_vectors_stacked: bfloat16 [65536, 256], P(('ctx', 'fsdp')), may hold values from -10 to 10
- content_vectors_stacked: bfloat16 [65536, 256], P(('ctx', 'fsdp')), may hold values from -6 to 6
- passage_label: int32 [65536], P(('ctx', 'fsdp')), may hold values from 0 to 511, never falling along the last dimension, each value on 1 to 256 neighbouring positions
- skip_path_derivative: bfloat16 [65536, 1440], P(('ctx', 'fsdp')), may hold values from -6 to 6
- specialist_entry_activations: bfloat16 [65536, 1440], P(('ctx', 'fsdp')), may hold values from -6 to 6
- merged_activation_derivative: bfloat16 [65536, 1440], P(('ctx', 'fsdp')), may hold values from -6 to 6
- picked_specialist_ids: int32 [65536, 4], P(('ctx', 'fsdp')), may hold values from 0 to 127, all different within a row; in each aligned block of 128 rows (0 to 127, 128 to 255, ...) at most 6 rows name the same one
- dispatcher_mixing_factor: bfloat16 [65536, 4], P(('ctx', 'fsdp')), may hold values from 0.099609375 to 1
- retained_specialist_ids: int32 [96], replicated, may hold values from 0 to 127, as said below
- specialist_linear_map: bfloat16 [16, 1440, 1440], P('ctx', 'fsdp'), may hold values from -0.15625 to 0.15625
- attention_final_linear_map: bfloat16 [2048, 1440], P('fsdp'), may hold values from -0.15625 to 0.15625
Outputs:
- query_grad: bfloat16 [65536, 2048], P(('ctx', 'fsdp'))
- key_grad: bfloat16 [65536, 256], P(('ctx', 'fsdp'))
- value_grad: bfloat16 [65536, 256], P(('ctx', 'fsdp'))
- specialist_source_derivative: bfloat16 [65536, 1440], P(('ctx', 'fsdp'))
- dispatcher_factor_derivative: bfloat16 [65536, 4], P(('ctx', 'fsdp'))
- specialist_map_derivative: bfloat16 [16, 1440, 1440], P('ctx', 'fsdp')
Inputs may be any that keep to these rules, and one draw needn't show every extreme that they name: `passage_label`: document numbers never fall along the sequence; each document holds 1 to 256 positions and one holds exactly 256. `picked_specialist_ids`: each row names 4 different experts; among the 128 rows of one device no expert is named by more than 6 rows, a bound that some block reaches. `retained_specialist_ids`: 96 different expert numbers.
All inputs are finite; a program needn't handle non-finite values.
Results may differ from a plain program's by a relative error of at most 0.024.
Values may be sent and summed in bfloat16 or wider, within the bound.
No kernel may reach another device: no remote copies, remote signals or barrier semaphores. Data moves between devices by JAX's collectives and lax.ppermute only.
A program may use at most 64 MiB of HBM per device.

v0:
```python
import jax
import jax.numpy as jnp
from jax import lax
from jax.sharding import PartitionSpec as P

HEAD_DIM = 64
CAP = 6


def from_behind(value, axis, steps):
    count = lax.axis_size(axis)
    first, last = (max(0, -steps), min(count, count - steps))
    return lax.ppermute(value, axis, [(source, source + steps) for source in range(first, last)])


def group_terms(queries, keys_win, values_win, grads_in, allowed, scale):
    scores = (
        jnp.einsum("tgd,kd->gtk", queries, keys_win, preferred_element_type=jnp.float32) * scale
    )
    scores = jnp.where(allowed[None], scores, -1e30)
    highest = jnp.max(scores, axis=-1, keepdims=True)
    raised = jnp.where(allowed[None], jnp.exp(scores - highest), 0.0)
    shares = raised / jnp.sum(raised, axis=-1, keepdims=True)
    shares_low = shares.astype(jnp.bfloat16)
    attended = jnp.einsum("gtk,kd->tgd", shares_low, values_win, preferred_element_type=jnp.float32)
    centre = jnp.sum(grads_in.astype(jnp.float32) * attended, axis=-1)
    share_grad = jnp.einsum("tgd,kd->gtk", grads_in, values_win, preferred_element_type=jnp.float32)
    score_grad = (shares * (share_grad - centre.T[:, :, None]) * scale).astype(jnp.bfloat16)
    query_part = jnp.einsum("gtk,kd->tgd", score_grad, keys_win, preferred_element_type=jnp.float32)
    key_part = jnp.einsum("gtk,tgd->kd", score_grad, queries, preferred_element_type=jnp.float32)
    value_part = jnp.einsum("gtk,tgd->kd", shares_low, grads_in, preferred_element_type=jnp.float32)
    return (query_part.astype(jnp.bfloat16), key_part, value_part)


def shards(
    asking_vectors_stacked,
    lookup_vectors_stacked,
    content_vectors_stacked,
    passage_label,
    skip_path_derivative,
    specialist_entry_activations,
    merged_activation_derivative,
    picked_specialist_ids,
    dispatcher_mixing_factor,
    retained_specialist_ids,
    specialist_linear_map,
    attention_final_linear_map,
):
    loaded_specialist_total = lax.axis_size("ctx")
    loaded_specialist_map = retained_specialist_ids[:loaded_specialist_total]
    chosen = picked_specialist_ids[:, None, :] == loaded_specialist_map[None, :, None]
    routed = jnp.any(chosen, axis=-1).astype(jnp.int32)
    gating = jnp.sum(
        jnp.where(chosen, dispatcher_mixing_factor.astype(jnp.float32)[:, None, :], 0.0), axis=-1
    )
    ranks = jnp.cumsum(routed, axis=0) - 1
    slots = jnp.arange(CAP, dtype=jnp.int32)
    dispatch = ((ranks.T[:, None, :] == slots[None, :, None]) & (routed.T[:, None, :] == 1)).astype(
        jnp.bfloat16
    )
    send_rows = jnp.einsum(
        "ect,td->ecd", dispatch, specialist_entry_activations, preferred_element_type=jnp.float32
    ).astype(jnp.bfloat16)
    send_grads = jnp.einsum(
        "ect,tn->ecn", dispatch, merged_activation_derivative, preferred_element_type=jnp.float32
    ).astype(jnp.bfloat16)
    send_gates = jnp.einsum("ect,te->ec", dispatch.astype(jnp.float32), gating).astype(jnp.bfloat16)
    got_rows, got_grads, got_gates = (
        lax.all_to_all(send_rows, "ctx", split_axis=0, concat_axis=0, tiled=True),
        lax.all_to_all(send_grads, "ctx", split_axis=0, concat_axis=0, tiled=True),
        lax.all_to_all(send_gates, "ctx", split_axis=0, concat_axis=0, tiled=True),
    )
    in_rows = got_rows.reshape(-1, got_rows.shape[2])
    grad_rows = got_grads.reshape(-1, got_grads.shape[2]).astype(jnp.float32)
    gate_rows = got_gates.reshape(-1).astype(jnp.float32)
    shard = specialist_linear_map[0]
    columns = in_rows
    pre = jnp.dot(
        columns,
        lax.all_gather(shard, "fsdp", axis=0, tiled=True),
        preferred_element_type=jnp.float32,
    )
    activated = jax.nn.silu(pre)
    gate_part = jnp.sum(grad_rows * activated, axis=-1).astype(jnp.bfloat16)
    sigma = jax.nn.sigmoid(pre)
    slope = sigma * (1.0 + pre * (1.0 - sigma))
    pre_grad = (gate_rows[:, None] * grad_rows * slope).astype(jnp.bfloat16)
    row_grads = lax.dot_general(
        pre_grad,
        lax.all_gather(shard, "fsdp", axis=0, tiled=True),
        (((1,), (1,)), ((), ())),
        preferred_element_type=jnp.float32,
    )
    row_grads = row_grads.astype(jnp.bfloat16)
    columns = in_rows
    specialist_map_derivative = lax.psum_scatter(
        lax.dot_general(
            columns, pre_grad, (((0,), (0,)), ((), ())), preferred_element_type=jnp.float32
        ).astype(jnp.bfloat16),
        "fsdp",
        scatter_dimension=0,
        tiled=True,
    )[None]
    back_rows, back_gates = (
        lax.all_to_all(
            row_grads.reshape(loaded_specialist_total, CAP, -1),
            "ctx",
            split_axis=0,
            concat_axis=0,
            tiled=True,
        ),
        lax.all_to_all(
            gate_part.reshape(loaded_specialist_total, CAP),
            "ctx",
            split_axis=0,
            concat_axis=0,
            tiled=True,
        ),
    )
    specialist_source_derivative = jnp.einsum(
        "ect,ecd->td", dispatch, back_rows, preferred_element_type=jnp.float32
    ).astype(jnp.bfloat16)
    per_token = jnp.einsum("ect,ec->te", dispatch, back_gates, preferred_element_type=jnp.float32)
    dispatcher_factor_derivative = jnp.sum(
        jnp.where(chosen, per_token[:, :, None], 0.0), axis=1
    ).astype(jnp.bfloat16)
    hidden_grad = (
        skip_path_derivative.astype(jnp.float32) + specialist_source_derivative.astype(jnp.float32)
    ).astype(jnp.bfloat16)
    attn_cotangent = lax.dot_general(
        hidden_grad,
        lax.all_gather(attention_final_linear_map, "fsdp", axis=0, tiled=True),
        (((1,), (1,)), ((), ())),
        preferred_element_type=jnp.float32,
    ).astype(jnp.bfloat16)
    rows = lookup_vectors_stacked.shape[0]
    kv_width = lookup_vectors_stacked.shape[1]
    kv_heads = kv_width // HEAD_DIM
    group = asking_vectors_stacked.shape[1] // kv_width
    scale = HEAD_DIM ** (-0.5)
    doc_plus = passage_label + 1
    earlier = []
    for distance in (1, 2):
        earlier.append(
            from_behind(
                (lookup_vectors_stacked, content_vectors_stacked, doc_plus),
                ("ctx", "fsdp"),
                distance,
            )
        )
    keys_win = jnp.concatenate([earlier[1][0], earlier[0][0], lookup_vectors_stacked], axis=0)
    values_win = jnp.concatenate([earlier[1][1], earlier[0][1], content_vectors_stacked], axis=0)
    docs_win = jnp.concatenate([earlier[1][2], earlier[0][2], doc_plus], axis=0)
    window_index = jnp.arange(3 * rows, dtype=jnp.int32)
    query_index = jnp.arange(rows, dtype=jnp.int32)
    allowed = (window_index[None, :] <= 2 * rows + query_index[:, None]) & (
        docs_win[None, :] == doc_plus[:, None]
    )
    queries = asking_vectors_stacked.reshape(rows, kv_heads, group, HEAD_DIM).transpose(1, 0, 2, 3)
    grads_in = attn_cotangent.reshape(rows, kv_heads, group, HEAD_DIM).transpose(1, 0, 2, 3)
    keys_split = keys_win.reshape(3 * rows, kv_heads, HEAD_DIM).transpose(1, 0, 2)
    values_split = values_win.reshape(3 * rows, kv_heads, HEAD_DIM).transpose(1, 0, 2)

    def per_group(pieces):
        return group_terms(pieces[0], pieces[1], pieces[2], pieces[3], allowed, scale)

    query_part, key_part, value_part = lax.map(
        per_group, (queries, keys_split, values_split, grads_in)
    )
    query_grad = query_part.transpose(1, 0, 2, 3).reshape(rows, -1)
    key_terms = key_part.transpose(1, 0, 2).reshape(3 * rows, kv_width)
    value_terms = value_part.transpose(1, 0, 2).reshape(3 * rows, kv_width)
    far_keys, near_keys, local_keys = (
        key_terms[:rows],
        key_terms[rows : 2 * rows],
        key_terms[2 * rows :],
    )
    far_values, near_values, local_values = (
        value_terms[:rows],
        value_terms[rows : 2 * rows],
        value_terms[2 * rows :],
    )
    key_total, value_total = (local_keys, local_values)
    for distance, part_keys, part_values in (
        (1, near_keys, near_values),
        (2, far_keys, far_values),
    ):
        got_keys, got_values = (
            from_behind(part_keys.astype(jnp.bfloat16), ("ctx", "fsdp"), -distance).astype(
                part_keys.dtype
            ),
            from_behind(part_values.astype(jnp.bfloat16), ("ctx", "fsdp"), -distance).astype(
                part_values.dtype
            ),
        )
        key_total = key_total + got_keys
        value_total = value_total + got_values
    return (
        query_grad,
        key_total.astype(jnp.bfloat16),
        value_total.astype(jnp.bfloat16),
        specialist_source_derivative,
        dispatcher_factor_derivative,
        specialist_map_derivative,
    )


def solution(mesh):
    return jax.shard_map(
        shards,
        mesh=mesh,
        in_specs=(
            P(("ctx", "fsdp"), None),
            P(("ctx", "fsdp"), None),
            P(("ctx", "fsdp"), None),
            P(("ctx", "fsdp")),
            P(("ctx", "fsdp"), None),
            P(("ctx", "fsdp"), None),
            P(("ctx", "fsdp"), None),
            P(("ctx", "fsdp"), None),
            P(("ctx", "fsdp"), None),
            P(),
            P("ctx", "fsdp", None),
            P("fsdp", None),
        ),
        out_specs=(
            P(("ctx", "fsdp"), None),
            P(("ctx", "fsdp"), None),
            P(("ctx", "fsdp"), None),
            P(("ctx", "fsdp"), None),
            P(("ctx", "fsdp"), None),
            P("ctx", "fsdp", None),
        ),
        check_vma=False,
    )
```

profile of v0, /device:TPU:32, one launch (start us, length us, event | category | flops | bytes accessed | tf_op | source)
XLA Modules:
  0.0 331.1 jit_solution(17898402939602762389)
XLA Ops:
  7.2 1.9 copy.116
  11.3 0.9 copy.114
  12.2 9.0 %all-to-all-start.1 = ((bf16[16,6,1440]{2,1,0:T(8,128)(2,1)}), bf16[16,6,1440]{2,1,0:T(8,128)(2,1)S(1)}, u32[]{:S(2)}, u32[]{:S(2)}) async-start(bf16[16,6,1440]{2,1,0:T(8,128)(2,1)} %copy.114), calls=%async_computation.1 | async-start | bytes 786432 | tf_op jit(solution)/shard_map/all_to_all | solution.py:70
  22.4 8.3 %all-to-all-done.1 = bf16[16,6,1440]{2,1,0:T(8,128)(2,1)S(1)} async-done(((bf16[16,6,1440]{2,1,0:T(8,128)(2,1)}), bf16[16,6,1440]{2,1,0:T(8,128)(2,1)S(1)}, u32[]{:S(2)}, u32[]{:S(2)}) %all-to-all-start.1) | async-done | bytes 276512 | tf_op jit(solution)/shard_map/all_to_all | solution.py:70
  30.7 7.8 %all-to-all-start.2 = ((bf16[16,6,1440]{2,1,0:T(8,128)(2,1)}), bf16[16,6,1440]{2,1,0:T(8,128)(2,1)S(1)}, u32[]{:S(2)}, u32[]{:S(2)}) async-start(bf16[16,6,1440]{2,1,0:T(8,128)(2,1)} %copy.115), calls=%async_computation.2 | async-start | bytes 786432 | tf_op jit(solution)/shard_map/all_to_all | solution.py:69
  38.6 4.5 %collective-permute-start.2 = (s32[128]{0:T(128)S(1)}, s32[128]{0:T(128)S(1)}, u32[]{:S(2)}, u32[]{:S(2)}) collective-permute-start(s32[128]{0:T(128)S(1)} %broadcast_add_fusion), channel_id=1, source_target_pairs={{0,2},{1,3},{2,4},{3,5},{4,6},{5,7},{6,8},{7,9},{8,10},{9,11},{10,... | collective-permute-start | bytes 1544 | tf_op jit(solution)/shard_map/ppermute | solution.py:13
  43.2 1.9 collective-permute-start.3
  45.1 4.5 %collective-permute-start = (bf16[128,256]{1,0:T(8,128)(2,1)S(1)}, bf16[128,256]{1,0:T(8,128)(2,1)S(1)}, u32[]{:S(2)}, u32[]{:S(2)}) collective-permute-start(bf16[128,256]{1,0:T(8,128)(2,1)S(1)} %copy-done.6), channel_id=1, source_target_pairs={{0,2},{1,3},{2,4},{3,5},{4,6},{5,7},{6,8},{7,9},{8,10},{9,11},{10,... | collective-permute-start | bytes 196616 | tf_op jit(solution)/shard_map/ppermute | solution.py:13
  49.6 4.5 %collective-permute-start.1 = (bf16[128,256]{1,0:T(8,128)(2,1)S(1)}, bf16[128,256]{1,0:T(8,128)(2,1)S(1)}, u32[]{:S(2)}, u32[]{:S(2)}) collective-permute-start(bf16[128,256]{1,0:T(8,128)(2,1)S(1)} %copy-done.6), channel_id=1, source_target_pairs={{0,1},{1,2},{2,3},{3,4},{4,5},{5,6},{6,7},{7,8},{8,9},{9,10},{10,1... | collective-permute-start | bytes 196616 | tf_op jit(solution)/shard_map/ppermute | solution.py:13
  54.1 4.5 %collective-permute-start.4 = (bf16[128,256]{1,0:T(8,128)(2,1)S(1)}, bf16[128,256]{1,0:T(8,128)(2,1)S(1)}, u32[]{:S(2)}, u32[]{:S(2)}) collective-permute-start(bf16[128,256]{1,0:T(8,128)(2,1)S(1)} %copy-done.7), channel_id=1, source_target_pairs={{0,2},{1,3},{2,4},{3,5},{4,6},{5,7},{6,8},{7,9},{8,10},{9,11},{10,... | collective-permute-start | bytes 196616 | tf_op jit(solution)/shard_map/ppermute | solution.py:13
  59.4 66.7 %all-gather.6.cloned.1.call-done = bf16[1,1440,1440]{2,0,1:T(2,128)(2,1)} async-done(((bf16[1,45,1440]{2,0,1:T(2,128)(2,1)}), bf16[1,1440,1440]{2,0,1:T(2,128)(2,1)}) %all-gather.6.cloned.1.call-update) | async-done | bytes 4147216 | tf_op jit(solution)/shard_map/all_gather | solution.py:80
  126.1 4.6 %multiply_reduce_fusion = (bf16[96]{0:T(256)(128)(2,1)S(1)}, f32[96,1440]{1,0:T(8,128)S(1)}) fusion(f32[96,1440]{1,0:T(8,128)S(1)} %reshape.100, bf16[96,1440]{1,0:T(8,128)(2,1)S(1)} %reshape.95, bf16[1,1440,1440]{2,0,1:T(2,128)(2,1)} %all-gather.6.cloned.1.call-done), kind=kOutput, calls=%fused_computation.67 | convolution fusion | flops 398960544 | bytes 5529792 | tf_op jit(solution)/shard_map/dot_general | solution.py:78
  131.3 7.5 %all-to-all-start.4 = ((bf16[16,1,6]{2,1,0:T(2,128)(2,1)}), bf16[16,1,6]{2,1,0:T(2,128)(2,1)S(1)}, u32[]{:S(2)}, u32[]{:S(2)}) async-start(bf16[16,1,6]{2,1,0:T(2,128)(2,1)} %convert_element_type.162), calls=%async_computation.4 | async-start | bytes 16384 | tf_op jit(solution)/shard_map/all_to_all | solution.py:112
  138.8 1.3 dynamic-slice.4
  140.7 1.3 all-to-all-done.4
  144.0 8.6 %all-to-all-start = ((bf16[16,1,6]{2,1,0:T(2,128)(2,1)}), bf16[16,1,6]{2,1,0:T(2,128)(2,1)S(1)}, u32[]{:S(2)}, u32[]{:S(2)}) async-start(bf16[16,1,6]{2,1,0:T(2,128)(2,1)} %copy.113), calls=%async_computation | async-start | bytes 16384 | tf_op jit(solution)/shard_map/all_to_all | solution.py:71
  152.6 1.9 collective-permute-start.5
  154.6 1.2 all-to-all-done
  155.9 5.0 %fusion.58 = bf16[96,1440]{1,0:T(8,128)(2,1)S(1)} fusion(bf16[1,1440,1440]{2,0,1:T(2,128)(2,1)} %all-gather.6.cloned.1.call-done, f32[96,1440]{1,0:T(8,128)S(1)} %get-tuple-element.142, f32[96,1440]{1,0:T(8,128)S(1)} %reshape.100, f32[96]{0:T(128)S(1)} %reshape.99), kind=kOutput, calls=%fused_computation.63 | convolution fusion | flops 399651840 | bytes 5529984 | tf_op jit(solution)/shard_map/dot_general | solution.py:88
  161.9 8.7 %all-to-all-start.3 = ((bf16[16,6,1440]{2,1,0:T(8,128)(2,1)}), bf16[16,6,1440]{2,1,0:T(8,128)(2,1)S(1)}, u32[]{:S(2)}, u32[]{:S(2)}) async-start(bf16[16,6,1440]{2,1,0:T(8,128)(2,1)} %reshape.96), calls=%async_computation.3 | async-start | bytes 786432 | tf_op jit(solution)/shard_map/all_to_all | solution.py:105
  170.6 3.4 %convolution_convert_fusion.1 = bf16[1440,1440]{1,0:T(8,128)(2,1)} fusion(bf16[96,1440]{1,0:T(8,128)(2,1)S(1)} %reshape.95, f32[96,1440]{1,0:T(8,128)S(1)} %get-tuple-element.142, f32[96,1440]{1,0:T(8,128)S(1)} %reshape.100, f32[96]{0:T(128)S(1)} %reshape.99), kind=kOutput, calls=%fused_computation.53 | convolution fusion | flops 401587200 | bytes 5529984 | tf_op jit(solution)/shard_map/dot_general | solution.py:97
  174.0 90.7 %fusion.2 = bf16[48,1440]{1,0:T(8,128)(2,1)S(1)} fusion(bf16[1440,1440]{1,0:T(8,128)(2,1)} %convolution_convert_fusion.1), kind=kCustom, calls=%all-reduce-scatter | all-reduce-scatter fusion | flops 2211841 | bytes 4287488
  264.7 1.3 collective-permute-start.10
  266.0 1.5 collective-permute-start.11
  268.8 1.3 collective-permute-done.11
  271.8 5.1 %convolution_convert_fusion.2 = bf16[128,2048]{1,0:T(8,128)(2,1)S(1)} fusion(bf16[2048,1440]{1,0:T(8,128)(2,1)} %all-gather.4.cloned.1.call-done, bf16[128,1440]{0,1:T(8,128)(2,1)S(1)} %fusion.57, bf16[128,1440]{0,1:T(8,128)(2,1)S(1)} %copy-done.4), kind=kOutput, calls=%fused_computation.60 | convolution fusion | flops 755974144 | bytes 7159808 | tf_op jit(solution)/shard_map/dot_general | solution.py:130
  277.1 18.7 %while.15 = (s32[]{:T(128)}, bf16[4,128,8,64]{1,3,2,0:T(8,128)(2,1)}, f32[4,384,64]{1,2,0:T(8,128)}, f32[4,384,64]{1,2,0:T(8,128)}, bf16[4,384,64]{1,2,0:T(8,128...) while((s32[]{:T(128)}, ...), condition=%wide.region_7.8_spmd.clone, body=%wide.region_3.7_spmd.clone.sunk | while | flops 307117440 | bytes 10793589 | solution.py:167
  278.9 0.9 fusion.134
  279.8 1.0 fusion.135
  280.8 1.0 fusion.136
  283.6 0.9 fusion.134
  284.5 1.0 fusion.135
  285.5 1.0 fusion.136
  288.3 0.9 fusion.134
  289.2 1.0 fusion.135
  290.2 1.0 fusion.136
  293.0 0.9 fusion.134
  293.9 1.0 fusion.135
  294.9 1.0 fusion.136
  295.9 1.2 bitcast_convert_fusion.1
  297.1 10.9 %collective-permute-start.8 = (bf16[128,256]{0,1:T(8,128)(2,1)S(1)}, bf16[128,256]{0,1:T(8,128)(2,1)S(1)}, u32[]{:S(2)}, u32[]{:S(2)}) collective-permute-start(bf16[128,256]{0,1:T(8,128)(2,1)S(1)} %bitcast.212), channel_id=1, source_target_pairs={{1,0},{2,1},{3,2},{4,3},{5,4},{6,5},{7,6},{8,7},{9,8},{10,9},{11,1... | collective-permute-start | bytes 196616 | tf_op jit(solution)/shard_map/ppermute | solution.py:13
  308.0 4.7 %collective-permute-start.9 = (bf16[128,256]{0,1:T(8,128)(2,1)S(1)}, bf16[128,256]{0,1:T(8,128)(2,1)S(1)}, u32[]{:S(2)}, u32[]{:S(2)}) collective-permute-start(bf16[128,256]{0,1:T(8,128)(2,1)S(1)} %bitcast.210), channel_id=1, source_target_pairs={{2,0},{3,1},{4,2},{5,3},{6,4},{7,5},{8,6},{9,7},{10,8},{11,9},{12,... | collective-permute-start | bytes 196616 | tf_op jit(solution)/shard_map/ppermute | solution.py:13
  312.7 0.9 slice.47
  313.6 1.9 collective-permute-start.6
  315.6 1.9 collective-permute-start.7
  317.5 0.9 slice.44
  318.4 1.0 copy.121
  320.2 3.2 collective-permute-done.7
  (108 shorter events, 19.4 us)
Async XLA Ops:
  7.2 3.8 %copy-start = (bf16[128,1440]{0,1:T(8,128)(2,1)S(1)}, bf16[128,1440]{0,1:T(8,128)(2,1)}, u32[]{:S(2)}) copy-start(bf16[128,1440]{0,1:T(8,128)(2,1)} %param.20) | copy-start | bytes 1105924
  7.2 118.9 %all-gather.6.cloned.1.call-start = ((), (), s32[]{:S(2)}) async-start(), calls=%async_computation.6 | async-start | bytes 9123840 | tf_op jit(solution)/shard_map/all_gather | solution.py:80
  9.1 12.1 %copy-start.5 = (bf16[128,1440]{0,1:T(8,128)(2,1)S(1)}, bf16[128,1440]{0,1:T(8,128)(2,1)}, u32[]{:S(2)}) copy-start(bf16[128,1440]{0,1:T(8,128)(2,1)} %param.19) | copy-start | bytes 1105924
  9.1 262.6 %all-gather.4.cloned.1.call-start = ((), (), s32[]{:S(2)}) async-start(), calls=%async_computation.5 | async-start | bytes 6488064 | tf_op jit(solution)/shard_map/all_gather | solution.py:132
  12.2 26.4 %copy-start.11 = (s32[128]{0:T(128)S(1)}, s32[128]{0:T(128)}, u32[]{:S(2)}) copy-start(s32[128]{0:T(128)} %param.17) | copy-start | bytes 1540
  12.2 32.9 %copy-start.6 = (bf16[128,256]{1,0:T(8,128)(2,1)S(1)}, bf16[128,256]{1,0:T(8,128)(2,1)}, u32[]{:S(2)}) copy-start(bf16[128,256]{1,0:T(8,128)(2,1)} %param.15) | copy-start | bytes 196612
  12.2 41.9 %copy-start.7 = (bf16[128,256]{1,0:T(8,128)(2,1)S(1)}, bf16[128,256]{1,0:T(8,128)(2,1)}, u32[]{:S(2)}) copy-start(bf16[128,256]{1,0:T(8,128)(2,1)} %param.16) | copy-start | bytes 196612
  12.2 46.4 %copy-start.10 = (bf16[128,4]{0,1:T(4,128)(2,1)S(1)}, bf16[128,4]{0,1:T(4,128)(2,1)}, u32[]{:S(2)}) copy-start(bf16[128,4]{0,1:T(4,128)(2,1)} %param.22) | copy-start | bytes 3076
  12.2 46.5 %copy-start.2 = (bf16[128,2048]{1,0:T(8,128)(2,1)S(1)}, bf16[128,2048]{1,0:T(8,128)(2,1)}, u32[]{:S(2)}) copy-start(bf16[128,2048]{1,0:T(8,128)(2,1)} %param.14) | copy-start | bytes 1572868
  12.2 18.5 %all-to-all-start.1 = ((bf16[16,6,1440]{2,1,0:T(8,128)(2,1)}), bf16[16,6,1440]{2,1,0:T(8,128)(2,1)S(1)}, u32[]{:S(2)}, u32[]{:S(2)}) async-start(bf16[16,6,1440]{2,1,0:T(8,128)(2,1)} %copy.114), calls=%async_computation.1 | async-start | bytes 786432 | tf_op jit(solution)/shard_map/all_to_all | solution.py:70
  30.7 28.4 %all-to-all-start.2 = ((bf16[16,6,1440]{2,1,0:T(8,128)(2,1)}), bf16[16,6,1440]{2,1,0:T(8,128)(2,1)S(1)}, u32[]{:S(2)}, u32[]{:S(2)}) async-start(bf16[16,6,1440]{2,1,0:T(8,128)(2,1)} %copy.115), calls=%async_computation.2 | async-start | bytes 786432 | tf_op jit(solution)/shard_map/all_to_all | solution.py:69
  38.6 114.0 %collective-permute-start.2 = (s32[128]{0:T(128)S(1)}, s32[128]{0:T(128)S(1)}, u32[]{:S(2)}, u32[]{:S(2)}) collective-permute-start(s32[128]{0:T(128)S(1)} %broadcast_add_fusion), channel_id=1, source_target_pairs={{0,2},{1,3},{2,4},{3,5},{4,6},{5,7},{6,8},{7,9},{8,10},{9,11},{10,... | collective-permute-start | bytes 1544 | tf_op jit(solution)/shard_map/ppermute | solution.py:13
  43.2 111.4 %collective-permute-start.3 = (s32[128]{0:T(128)S(1)}, s32[128]{0:T(128)S(1)}, u32[]{:S(2)}, u32[]{:S(2)}) collective-permute-start(s32[128]{0:T(128)S(1)} %broadcast_add_fusion), channel_id=1, source_target_pairs={{0,1},{1,2},{2,3},{3,4},{4,5},{5,6},{6,7},{7,8},{8,9},{9,10},{10,1... | collective-permute-start | bytes 1544 | tf_op jit(solution)/shard_map/ppermute | solution.py:13
  45.1 220.9 %collective-permute-start = (bf16[128,256]{1,0:T(8,128)(2,1)S(1)}, bf16[128,256]{1,0:T(8,128)(2,1)S(1)}, u32[]{:S(2)}, u32[]{:S(2)}) collective-permute-start(bf16[128,256]{1,0:T(8,128)(2,1)S(1)} %copy-done.6), channel_id=1, source_target_pairs={{0,2},{1,3},{2,4},{3,5},{4,6},{5,7},{6,8},{7,9},{8,10},{9,11},{10,... | collective-permute-start | bytes 196616 | tf_op jit(solution)/shard_map/ppermute | solution.py:13
  49.6 217.9 %collective-permute-start.1 = (bf16[128,256]{1,0:T(8,128)(2,1)S(1)}, bf16[128,256]{1,0:T(8,128)(2,1)S(1)}, u32[]{:S(2)}, u32[]{:S(2)}) collective-permute-start(bf16[128,256]{1,0:T(8,128)(2,1)S(1)} %copy-done.6), channel_id=1, source_target_pairs={{0,1},{1,2},{2,3},{3,4},{4,5},{5,6},{6,7},{7,8},{8,9},{9,10},{10,1... | collective-permute-start | bytes 196616 | tf_op jit(solution)/shard_map/ppermute | solution.py:13
  54.1 213.6 %collective-permute-start.4 = (bf16[128,256]{1,0:T(8,128)(2,1)S(1)}, bf16[128,256]{1,0:T(8,128)(2,1)S(1)}, u32[]{:S(2)}, u32[]{:S(2)}) collective-permute-start(bf16[128,256]{1,0:T(8,128)(2,1)S(1)} %copy-done.7), channel_id=1, source_target_pairs={{0,2},{1,3},{2,4},{3,5},{4,6},{5,7},{6,8},{7,9},{8,10},{9,11},{10,... | collective-permute-start | bytes 196616 | tf_op jit(solution)/shard_map/ppermute | solution.py:13
  59.3 83.0 %copy-start.8 = (s32[128,4]{0,1:T(4,128)S(1)}, s32[128,4]{0,1:T(4,128)}, u32[]{:S(2)}) copy-start(s32[128,4]{0,1:T(4,128)} %param.21) | copy-start | bytes 6148
  59.4 83.0 %copy-start.9 = (s32[96]{0:T(128)S(1)}, s32[96]{0:T(128)}, u32[]{:S(2)}) copy-start(s32[96]{0:T(128)} %param.23) | copy-start | bytes 1156
  131.3 10.7 %all-to-all-start.4 = ((bf16[16,1,6]{2,1,0:T(2,128)(2,1)}), bf16[16,1,6]{2,1,0:T(2,128)(2,1)S(1)}, u32[]{:S(2)}, u32[]{:S(2)}) async-start(bf16[16,1,6]{2,1,0:T(2,128)(2,1)} %convert_element_type.162), calls=%async_computation.4 | async-start | bytes 16384 | tf_op jit(solution)/shard_map/all_to_all | solution.py:112
  144.0 11.8 %all-to-all-start = ((bf16[16,1,6]{2,1,0:T(2,128)(2,1)}), bf16[16,1,6]{2,1,0:T(2,128)(2,1)S(1)}, u32[]{:S(2)}, u32[]{:S(2)}) async-start(bf16[16,1,6]{2,1,0:T(2,128)(2,1)} %copy.113), calls=%async_computation | async-start | bytes 16384 | tf_op jit(solution)/shard_map/all_to_all | solution.py:71
  152.6 115.1 %collective-permute-start.5 = (bf16[128,256]{1,0:T(8,128)(2,1)S(1)}, bf16[128,256]{1,0:T(8,128)(2,1)}, u32[]{:S(2)}, u32[]{:S(2)}) collective-permute-start(bf16[128,256]{1,0:T(8,128)(2,1)S(1)} %copy-done.7), channel_id=1, source_target_pairs={{0,1},{1,2},{2,3},{3,4},{4,5},{5,6},{6,7},{7,8},{8,9},{9,10},{10,1... | collective-permute-start | bytes 196616 | tf_op jit(solution)/shard_map/ppermute | solution.py:13
  161.9 109.5 %all-to-all-start.3 = ((bf16[16,6,1440]{2,1,0:T(8,128)(2,1)}), bf16[16,6,1440]{2,1,0:T(8,128)(2,1)S(1)}, u32[]{:S(2)}, u32[]{:S(2)}) async-start(bf16[16,6,1440]{2,1,0:T(8,128)(2,1)} %reshape.96), calls=%async_computation.3 | async-start | bytes 786432 | tf_op jit(solution)/shard_map/all_to_all | solution.py:105
  264.7 5.4 %collective-permute-start.10 = (bf16[48,1440]{1,0:T(8,128)(2,1)S(1)}, bf16[48,1440]{1,0:T(8,128)(2,1)S(1)}, u32[]{:S(2)}, u32[]{:S(2)}) collective-permute-start(bf16[48,1440]{1,0:T(8,128)(2,1)S(1)} %fusion.2), channel_id=1, source_target_pairs={{0,1},{1,2},{2,3},{3,4},{4,5},{5,6},{6,7},{7,8},{8,9},{9,10},{10,1... | collective-permute-start | bytes 414728
  266.0 4.0 %collective-permute-start.11 = (bf16[45,1440]{1,0:T(8,128)(2,1)S(1)}, bf16[45,1440]{1,0:T(8,128)(2,1)S(1)}, u32[]{:S(2)}, u32[]{:S(2)}) collective-permute-start(bf16[45,1440]{1,0:T(8,128)(2,1)S(1)} %slice.50), channel_id=1, source_target_pairs={{0,2},{1,3},{2,4},{3,5},{4,6},{5,7},{6,8},{7,9},{8,10},{9,11},{10,... | collective-permute-start | bytes 388808
  267.5 4.2 %copy-start.4 = (bf16[128,1440]{0,1:T(8,128)(2,1)S(1)}, bf16[128,1440]{0,1:T(8,128)(2,1)}, u32[]{:S(2)}) copy-start(bf16[128,1440]{0,1:T(8,128)(2,1)} %param.18) | copy-start | bytes 1105924
  271.7 5.1 %copy-start.1 = (bf16[128,1440]{0,1:T(8,128)(2,1)}, bf16[128,1440]{0,1:T(8,128)(2,1)S(1)}, u32[]{:S(2)}) copy-start(bf16[128,1440]{0,1:T(8,128)(2,1)S(1)} %fusion.57) | copy-start | bytes 1105924
  295.9 22.6 %copy-start.3 = (bf16[4,128,8,64]{1,3,2,0:T(8,128)(2,1)S(1)}, bf16[4,128,8,64]{1,3,2,0:T(8,128)(2,1)}, u32[]{:S(2)}) copy-start(bf16[4,128,8,64]{1,3,2,0:T(8,128)(2,1)} %get-tuple-element.55) | copy-start | bytes 1572868
  297.1 22.3 %collective-permute-start.8 = (bf16[128,256]{0,1:T(8,128)(2,1)S(1)}, bf16[128,256]{0,1:T(8,128)(2,1)S(1)}, u32[]{:S(2)}, u32[]{:S(2)}) collective-permute-start(bf16[128,256]{0,1:T(8,128)(2,1)S(1)} %bitcast.212), channel_id=1, source_target_pairs={{1,0},{2,1},{3,2},{4,3},{5,4},{6,5},{7,6},{8,7},{9,8},{10,9},{11,1... | collective-permute-start | bytes 196616 | tf_op jit(solution)/shard_map/ppermute | solution.py:13
  308.0 11.5 %collective-permute-start.9 = (bf16[128,256]{0,1:T(8,128)(2,1)S(1)}, bf16[128,256]{0,1:T(8,128)(2,1)S(1)}, u32[]{:S(2)}, u32[]{:S(2)}) collective-permute-start(bf16[128,256]{0,1:T(8,128)(2,1)S(1)} %bitcast.210), channel_id=1, source_target_pairs={{2,0},{3,1},{4,2},{5,3},{6,4},{7,5},{8,6},{9,7},{10,8},{11,9},{12,... | collective-permute-start | bytes 196616 | tf_op jit(solution)/shard_map/ppermute | solution.py:13
  313.6 6.6 %collective-permute-start.6 = (bf16[128,256]{0,1:T(8,128)(2,1)S(1)}, bf16[128,256]{0,1:T(8,128)(2,1)S(1)}, u32[]{:S(2)}, u32[]{:S(2)}) collective-permute-start(bf16[128,256]{0,1:T(8,128)(2,1)S(1)} %bitcast.213), channel_id=1, source_target_pairs={{1,0},{2,1},{3,2},{4,3},{5,4},{6,5},{7,6},{8,7},{9,8},{10,9},{11,1... | collective-permute-start | bytes 196616 | tf_op jit(solution)/shard_map/ppermute | solution.py:13
  315.6 7.9 %collective-permute-start.7 = (bf16[128,256]{0,1:T(8,128)(2,1)S(1)}, bf16[128,256]{0,1:T(8,128)(2,1)S(1)}, u32[]{:S(2)}, u32[]{:S(2)}) collective-permute-start(bf16[128,256]{0,1:T(8,128)(2,1)S(1)} %bitcast.211), channel_id=1, source_target_pairs={{2,0},{3,1},{4,2},{5,3},{6,4},{7,5},{8,6},{9,7},{10,8},{11,9},{12,... | collective-permute-start | bytes 196616 | tf_op jit(solution)/shard_map/ppermute | solution.py:13
Sparse Core Ops, SparseCore 0:
  12.0 114.0 all-gather.5
  129.4 114.9 all-gather.3
where the time goes:
time: 332 us; the launch traced here: 331 us
  blocking collectives  90.7 us (27%)
  starting transfers between devices  85.8 us (26%)
  waiting for transfers between devices  82.8 us (25%)
  matrix products  36.8 us (11%)
  between operations  15.2 us (5%)
  local copies, waits for them, and re-layouts  14.8 us (4%)
  other arithmetic  4.84 us (1%)
    unnamed x1, blocking collectives  90.7 us
    all_gather x1, waiting for transfers between devices, shards(): lax.all_gather(shard, 'fsdp', axis=0, tiled=True)  66.7 us
    ppermute x10, starting transfers between devices, from_behind(): lax.ppermute(value, axis, [(source, source + steps) for source in range(f...  41.3 us
    all_to_all x1, starting transfers between devices, shards(): lax.all_to_all(send_grads, 'ctx', split_axis=0, concat_axis=0, tiled=True)  9.01 us
    all_to_all x1, starting transfers between devices, shards(): lax.all_to_all(row_grads.reshape(loaded_specialist_total, CAP, -1), 'ctx'...  8.7 us
    all_to_all x1, starting transfers between devices, shards(): lax.all_to_all(send_gates, 'ctx', split_axis=0, concat_axis=0, tiled=True)  8.64 us
    all_to_all x1, waiting for transfers between devices, shards(): lax.all_to_all(send_grads, 'ctx', split_axis=0, concat_axis=0, tiled=True)  8.31 us
    all_to_all x1, starting transfers between devices, shards(): lax.all_to_all(send_rows, 'ctx', split_axis=0, concat_axis=0, tiled=True)  7.84 us
  transfers between devices with their start and end apart: 19, of which 6 were waited for; matrix products, arithmetic and copies ran while one was open for 36% of the time, Pallas kernels for 0%

commit v1 on v0

v1 whole, which is shorter than its diff:
```python
import jax
import jax.numpy as jnp
from jax import lax
from jax.experimental import pallas as pl
from jax.experimental.pallas import tpu as pltpu
from jax.sharding import Mesh, PartitionSpec as P

TOK = 128
D = 1440
F = 1440
HEADS = 32
KV_HEADS = 4
HD = 64
CAP = 6
CAPP = 8
EXPERTS = 16
ROWS = EXPERTS * CAPP
SEG = 48
SHARD = 45
DP = 1536
HALF = 768
SEND = 3072
BACK = 1664
KV = 256
WIDE = 640
BF = jnp.bfloat16
F32 = jnp.float32
ALL = ("y", "xl", "z", "xh", "core")
CTX = ("y", "xl")
SWAP = ((0, 1), (1, 0))


def dot(a, b, dims):
    return lax.dot_general(a, b, (dims, ((), ())), preferred_element_type=F32)


def spec_vmem():
    return pl.BlockSpec(memory_space=pltpu.VMEM)


def spec_smem():
    return pl.BlockSpec(memory_space=pltpu.SMEM)


def call(kernel, outs, scratch, flops, nbytes, n_smem, n_vmem):
    return pl.pallas_call(
        kernel,
        out_shape=outs,
        in_specs=[spec_smem()] * n_smem + [spec_vmem()] * n_vmem,
        out_specs=[spec_vmem()] * len(outs),
        scratch_shapes=scratch,
        compiler_params=pltpu.CompilerParams(vmem_limit_bytes=40 * 1024 * 1024),
        cost_estimate=pl.CostEstimate(flops=flops, bytes_accessed=nbytes, transcendentals=0),
    )


def routed_rows(picked_ref, held_ref):
    held = held_ref[...]
    chosen = [picked_ref[s : s + 1, :] == held for s in range(4)]
    routed = chosen[0] | chosen[1] | chosen[2] | chosen[3]
    routed_f = jnp.where(routed, 1.0, 0.0)
    before = lax.broadcasted_iota(jnp.int32, (TOK, TOK), 0) <= lax.broadcasted_iota(
        jnp.int32, (TOK, TOK), 1
    )
    upper = jnp.where(before, 1.0, 0.0).astype(BF)
    rank = dot(routed_f.astype(BF), upper, ((1,), (0,))) - 1.0
    slot = lax.broadcasted_iota(jnp.int32, (ROWS, TOK), 0) % CAPP
    sent = routed & (rank == slot.astype(F32))
    return chosen, sent


def dispatch_kernel(picked_ref, held_ref, gate_ref, place_ref, x_ref, g_ref, out_ref):
    chosen, sent = routed_rows(picked_ref, held_ref)
    sent_bf = jnp.where(sent, 1.0, 0.0).astype(BF)
    gate = jnp.zeros((ROWS, TOK), F32)
    for s in range(4):
        gate = gate + jnp.where(chosen[s] & sent, gate_ref[s : s + 1, :], 0.0)
    gate = jnp.sum(gate, axis=1, keepdims=True)
    rows = dot(sent_bf, x_ref[...], ((1,), (0,))).astype(BF)
    feature = lax.broadcasted_iota(jnp.int32, (D, 256), 0)
    for c in range(DP // 256):
        pick = jnp.where(feature == place_ref[:, c * 256 : (c + 1) * 256], 1.0, 0.0).astype(BF)
        out_ref[:, c * 256 : (c + 1) * 256] = dot(rows, pick, ((1,), (0,))).astype(BF)
    grads = dot(sent_bf, g_ref[...], ((1,), (0,))).astype(BF)
    out_ref[:, DP:] = jnp.concatenate(
        [grads, jnp.broadcast_to(gate, (ROWS, SEND - DP - F)).astype(BF)], axis=1
    )


def expert_kernel(got_ref, wm_ref, wo_ref, back_ref, pg_ref, pre_ref):
    step = 512
    for lo in range(0, F, step):
        hi = min(F, lo + step)
        pre_ref[:, lo:hi] = dot(got_ref[:, :HALF], wm_ref[:, lo:hi], ((1,), (0,))) + dot(
            got_ref[:, HALF:DP], wo_ref[:, lo:hi], ((1,), (0,))
        )
    gate = got_ref[:, DP + F : DP + F + 1].astype(F32)
    total = jnp.zeros((ROWS, 1), F32)
    for lo in range(0, F, step):
        hi = min(F, lo + step)
        pre = pre_ref[:, lo:hi]
        grad = got_ref[:, DP + lo : DP + hi].astype(F32)
        sig = 1.0 / (1.0 + jnp.exp(-pre))
        total = total + jnp.sum(grad * (pre * sig), axis=1, keepdims=True)
        slope = sig * (1.0 + pre * (1.0 - sig))
        pg_ref[:, lo:hi] = (gate * grad * slope).astype(BF)
    pg = pg_ref[...]
    for c in range(HALF // 256):
        r = slice(c * 256, (c + 1) * 256)
        back_ref[:, c * 256 : (c + 1) * 256] = dot(pg, wm_ref[r, :], ((1,), (1,))).astype(BF)
        back_ref[:, HALF + c * 256 : HALF + (c + 1) * 256] = dot(
            pg, wo_ref[r, :], ((1,), (1,))
        ).astype(BF)
    back_ref[:, DP:] = jnp.broadcast_to(total, (ROWS, BACK - DP)).astype(BF)


def attention_kernel(
    core_ref, picked_ref, held_ref, place_ref, back_ref, skip_ref, om_ref, oo_ref,
    q_ref, far_ref, near_ref, own_ref, label_ref,
    src_ref, gate_ref, qg_ref, farg_ref, nearg_ref, owng_ref,
    hidden_s, cot_s, kv_s, bias_s, acck_s, accv_s,
):
    chosen, sent = routed_rows(picked_ref, held_ref)
    sent_bf = jnp.where(sent, 1.0, 0.0).astype(BF)
    gate_part = back_ref[:, DP : DP + 1].astype(F32)
    for s in range(4):
        gate_ref[s : s + 1, :] = jnp.sum(
            jnp.where(chosen[s] & sent, gate_part, 0.0), axis=0, keepdims=True
        )
    src = dot(sent_bf, back_ref[:, :DP], ((0,), (0,))).astype(BF)
    feature = lax.broadcasted_iota(jnp.int32, (D, 256), 0)
    total = jnp.zeros((TOK, D), F32)
    for c in range(DP // 256):
        pick = jnp.where(feature == place_ref[:, c * 256 : (c + 1) * 256], 1.0, 0.0).astype(BF)
        total = total + dot(src[:, c * 256 : (c + 1) * 256], pick, ((1,), (1,)))
    src_ref[...] = total.astype(BF)
    hidden_s[...] = (skip_ref[...].astype(F32) + total).astype(BF)

    first = core_ref[0] == 0

    @pl.loop(0, 8)
    def _(z):
        base = pl.multiple_of(z * 128, 128)
        mine, other = om_ref[pl.ds(base, 128), :], oo_ref[pl.ds(base, 128), :]
        even, odd = jnp.where(first, mine, other), jnp.where(first, other, mine)
        rows = jnp.concatenate([even[:64], odd[:64], even[64:], odd[64:]], axis=0)
        cot_s[:, pl.ds(pl.multiple_of(z * 256, 256), 256)] = dot(
            hidden_s[...], rows, ((1,), (1,))
        ).astype(BF)

    for part, ref in enumerate((far_ref, near_ref, own_ref)):
        kv_s[part * TOK : (part + 1) * TOK, :] = ref[...]
    marks = kv_s[:, 2 * KV :].astype(F32)
    docs = marks[:, 0:1] * 16.0 + marks[:, 1:2]
    r_at = lax.broadcasted_iota(jnp.int32, (3 * TOK, TOK), 0)
    p_at = lax.broadcasted_iota(jnp.int32, (3 * TOK, TOK), 1)
    allowed = (r_at <= 2 * TOK + p_at) & (docs == label_ref[...])
    bias = jnp.where(allowed, 0.0, -1e30)
    bias_s[...] = jnp.concatenate([bias, bias], axis=1)

    low = lax.broadcasted_iota(jnp.int32, (TOK, 128), 1) < HD
    low_win = lax.broadcasted_iota(jnp.int32, (3 * TOK, 128), 1) < HD
    sums = []
    for g in range(KV_HEADS):
        k_one = kv_s[:, g * HD : (g + 1) * HD]
        v_one = kv_s[:, KV + g * HD : KV + (g + 1) * HD]
        k_two = jnp.concatenate([k_one, k_one], axis=1)
        v_two = jnp.concatenate([v_one, v_one], axis=1)
        k_flip = jnp.transpose(k_two.astype(F32))[:HD].astype(BF)
        acck_s[...] = jnp.zeros_like(acck_s)
        accv_s[...] = jnp.zeros_like(accv_s)

        def pair(i, carry, g=g, k_two=k_two, v_two=v_two, k_flip=k_flip):
            at = pl.ds(pl.multiple_of((g * 4 + i) * 128, 128), 128)
            q = q_ref[:, at] * 0.125
            c = cot_s[:, at]
            zero = jnp.zeros_like(q)
            q_st = jnp.concatenate([jnp.where(low, q, zero), jnp.where(low, zero, q)], axis=0)
            c_st = jnp.concatenate([jnp.where(low, c, zero), jnp.where(low, zero, c)], axis=0)
            s = dot(k_two, q_st, ((1,), (1,))) + bias_s[...]
            e = jnp.exp(s - jnp.max(s, axis=0, keepdims=True))
            shares = e * (1.0 / jnp.sum(e, axis=0, keepdims=True))
            shares_low = shares.astype(BF)
            dp = dot(v_two, c_st, ((1,), (1,)))
            centre = jnp.sum(shares_low.astype(F32) * dp, axis=0, keepdims=True)
            sg = (shares * (dp - centre)).astype(BF)
            acck_s[...] += dot(sg, q_st, ((1,), (0,)))
            accv_s[...] += dot(shares_low, c_st, ((1,), (0,)))
            qg = dot(k_flip, sg, ((1,), (0,)))
            both = jnp.concatenate([qg[:, :TOK], qg[:, TOK:]], axis=0) * 0.125
            qg_ref[:, at] = jnp.transpose(both).astype(BF)
            return carry

        lax.fori_loop(0, 4, pair, 0)
        ak, av = acck_s[...], accv_s[...]
        sums.append((ak + pltpu.roll(ak, HD, 1), av + pltpu.roll(av, HD, 1)))
    for kind in range(2):
        for t in range(2):
            tile = jnp.where(low_win, sums[2 * t][kind], sums[2 * t + 1][kind])
            at = slice(kind * KV + t * 128, kind * KV + (t + 1) * 128)
            farg_ref[:, at] = tile[:TOK].astype(BF)
            nearg_ref[:, at] = tile[TOK : 2 * TOK].astype(BF)
            owng_ref[:, at] = tile[2 * TOK :]


def gather_ring(pair):
    rows = pair.shape[0]
    half = rows // 2
    z = lax.axis_index("z")
    up = [(i, (i + 1) % 8) for i in range(8)]
    down = [(i, (i + 7) % 8) for i in range(8)]
    full = jnp.zeros((8 * rows,) + pair.shape[1:], pair.dtype)

    def put(full, piece, at, shift=0):
        return lax.dynamic_update_slice_in_dim(full, piece, (at % 8) * rows + shift, 0)

    full = put(full, pair, z)
    left = right = pair
    for k in range(1, 4):
        right = lax.ppermute(right, "z", up)
        left = lax.ppermute(left, "z", down)
        full = put(full, right, z - k + 8)
        full = put(full, left, z + k)
    last_r = lax.ppermute(right[:half], "z", up)
    last_l = lax.ppermute(left[half:], "z", down)
    full = put(full, last_r, z + 4)
    return put(full, last_l, z + 4, half)


def both_xh(piece):
    got = lax.ppermute(piece, "xh", SWAP)
    first = lax.axis_index("xh") == 0
    return jnp.concatenate([jnp.where(first, piece, got), jnp.where(first, got, piece)], axis=0)


def shift_blocks(value, steps):
    first, last = max(0, -steps), min(512, 512 - steps)
    return lax.ppermute(value, ALL, [(i, i + steps) for i in range(first, last)])


def shards(q, keys, values, label, skip, x, g, picked, mix, retained, weights, out_map):
    core = lax.axis_index("core")
    w_pair = both_xh(jnp.pad(weights[0], ((0, SEG - SHARD), (0, 0))))
    o_pair = both_xh(out_map)
    plus = (label + 1).astype(jnp.int32)
    marks = jnp.stack([plus // 16, plus % 16], axis=1).astype(BF)
    own = jnp.concatenate(
        [keys, values, jnp.pad(marks, ((0, 0), (0, WIDE - 2 * KV - 2)))], axis=1
    )
    near = shift_blocks(own, 1)
    far = shift_blocks(own, 2)

    o_mine = lax.all_gather(o_pair, "z", axis=0, tiled=True)

    picked_t = picked.T
    held = jnp.repeat(retained[:EXPERTS], CAPP)[:, None]
    spot = jnp.arange(DP, dtype=jnp.int32)
    half = spot // HALF
    rest = spot % HALF
    within = rest % SEG
    owner = (rest // SEG) * 2 + (half ^ core)
    place = jnp.where(within < SHARD, owner * SHARD + within, -1)[None, :]
    send = call(
        dispatch_kernel,
        [jax.ShapeDtypeStruct((ROWS, SEND), BF)],
        [],
        2 * TOK * D * (DP + 256),
        3 << 20,
        0,
        6,
    )(picked_t, held, mix.astype(F32).T, place, x, g)[0]
    got = lax.all_to_all(send.reshape(EXPERTS, CAPP, SEND), CTX, 0, 0, tiled=True)
    got = got.reshape(ROWS, SEND)

    w_mine = gather_ring(w_pair)
    w_other = lax.ppermute(w_mine, "core", SWAP)
    o_other = lax.ppermute(o_mine, "core", SWAP)

    x_swapped = lax.ppermute(got[:, HALF:DP], "core", SWAP)
    back, pg = call(
        expert_kernel,
        [jax.ShapeDtypeStruct((ROWS, BACK), BF), jax.ShapeDtypeStruct((ROWS, F), BF)],
        [pltpu.VMEM((ROWS, F), F32)],
        4 * ROWS * DP * F,
        6 << 20,
        0,
        3,
    )(got, w_mine, w_other)
    returned = lax.all_to_all(back.reshape(EXPERTS, CAPP, BACK), CTX, 0, 0, tiled=True)
    returned = returned.reshape(ROWS, BACK)

    pg_swapped = lax.ppermute(pg, "core", SWAP)
    x_rows = jnp.concatenate([got[:, :HALF], x_swapped], axis=0)
    pg_rows = jnp.concatenate([pg, pg_swapped], axis=0)
    partial = dot(x_rows, pg_rows, ((0,), (0,))).astype(BF)
    terms = lax.all_to_all(partial.reshape(16, SEG, F), ("z", "xh"), 0, 0, tiled=True)
    map_grad = jnp.sum(terms.astype(F32), axis=0).astype(BF)[None, :SHARD]

    src, gate_t, q_grad, far_g, near_g, own_g = call(
        attention_kernel,
        [
            jax.ShapeDtypeStruct((TOK, D), BF),
            jax.ShapeDtypeStruct((4, TOK), F32),
            jax.ShapeDtypeStruct((TOK, HEADS * HD), BF),
            jax.ShapeDtypeStruct((TOK, 2 * KV), BF),
            jax.ShapeDtypeStruct((TOK, 2 * KV), BF),
            jax.ShapeDtypeStruct((TOK, 2 * KV), F32),
        ],
        [
            pltpu.VMEM((TOK, D), BF),
            pltpu.VMEM((TOK, HEADS * HD), BF),
            pltpu.VMEM((3 * TOK, WIDE), BF),
            pltpu.VMEM((3 * TOK, 2 * TOK), F32),
            pltpu.VMEM((3 * TOK, 128), F32),
            pltpu.VMEM((3 * TOK, 128), F32),
        ],
        3 << 30,
        9 << 20,
        1,
        12,
    )(
        core[None].astype(jnp.int32), picked_t, held, place, returned, skip, o_mine, o_other,
        q, far, near, own, plus.astype(F32)[None, :],
    )
    got_near = shift_blocks(near_g, -1)
    got_far = shift_blocks(far_g, -2)
    kv_grad = (own_g + got_near.astype(F32) + got_far.astype(F32)).astype(BF)
    return (
        q_grad,
        kv_grad[:, :KV],
        kv_grad[:, KV:],
        src,
        gate_t.T.astype(BF),
        map_grad,
    )


def solution(mesh):
    fine = Mesh(mesh.devices.reshape(8, 2, 8, 2, 2), ALL)
    rows = P(ALL, None)
    fsdp = ("z", "xh", "core")
    return jax.shard_map(
        shards,
        mesh=fine,
        in_specs=(
            rows, rows, rows, P(ALL), rows, rows, rows, rows, rows, P(),
            P(CTX, fsdp, None), P(fsdp, None),
        ),
        out_specs=(rows, rows, rows, rows, rows, P(CTX, fsdp, None)),
        check_vma=False,
    )
```

time: 332 us -> 266 us (0.80)
  blocking collectives: 90.7 us -> 0 us
  matrix products: 36.8 us -> 0.78 us
  Pallas kernels: 0 us -> 25.2 us
  local copies, waits for them, and re-layouts: 14.8 us -> 33.8 us
  waiting for transfers between devices: 82.8 us -> 95.1 us
  starting transfers between devices: 85.8 us -> 89.3 us
    unnamed x1 -> x0, blocking collectives: 90.7 us -> none
    all_gather x2 -> x1, waiting for transfers between devices: 66.7 us -> 0.02 us  [shards(): o_mine = lax.all_gather(o_pair, 'z', axis=0, tiled=True)]
    all_to_all x5 -> x3, waiting for transfers between devices: 10.8 us -> 66.3 us  [the longest x1 51.3 us: shards(): lax.all_to_all(partial.reshape(16, SEG, F), ('z', 'xh'), 0, 0, tiled=True)]
    dot_general x29 -> x1, matrix products: 33.8 us -> 0.78 us  [dot(): return lax.dot_general(a, b, (dims, ((), ())), preferred_element_type=F32)]
    ppermute x10 -> x18, waiting for transfers between devices: 3.25 us -> 28.7 us  [the longest x3 14.7 us: gather_ring(): right = lax.ppermute(right, 'z', up)]
    pallas_call x0 -> x3, Pallas kernels: none -> 25.2 us  [the longest x1 20.6 us: shards(): call(attention_kernel, [jax.ShapeDtypeStruct((TOK, D), BF), jax.ShapeDtyp...]
    ppermute x10 -> x18, starting transfers between devices: 41.3 us -> 64.2 us  [the longest x3 19.3 us: gather_ring(): left = lax.ppermute(left, 'z', down)]
    all_to_all x5 -> x3, starting transfers between devices: 41.7 us -> 25.1 us  [the longest x1 8.79 us: shards(): lax.all_to_all(back.reshape(EXPERTS, CAPP, BACK), CTX, 0, 0, tiled=True)]
  transfers between devices with their start and end apart: 19 -> 22, of which waited for: 6 -> 13; matrix products, arithmetic and copies ran while one was open for 36% -> 11% of each run, Pallas kernels for 0% -> 2%
where the time goes in v1:
time: 266 us; the launch traced here: 264 us
  waiting for transfers between devices  95.1 us (36%)
  starting transfers between devices  89.3 us (34%)
  local copies, waits for them, and re-layouts  33.8 us (13%)
  Pallas kernels  25.2 us (9%)
  between operations  14.7 us (6%)
  other arithmetic  5.49 us (2%)
    all_to_all x1, waiting for transfers between devices, shards(): lax.all_to_all(partial.reshape(16, SEG, F), ('z', 'xh'), 0, 0, tiled=True)  51.3 us
    pallas_call x1, Pallas kernels, shards(): call(attention_kernel, [jax.ShapeDtypeStruct((TOK, D), BF), jax.ShapeDtyp...  20.6 us
    ppermute x3, starting transfers between devices, gather_ring(): left = lax.ppermute(left, 'z', down)  19.3 us
    all_to_all x1, waiting for transfers between devices, shards(): lax.all_to_all(send.reshape(EXPERTS, CAPP, SEND), CTX, 0, 0, tiled=True)  15.1 us
    ppermute x3, waiting for transfers between devices, gather_ring(): right = lax.ppermute(right, 'z', up)  14.7 us
    ppermute x4, starting transfers between devices, shift_blocks(): lax.ppermute(value, ALL, [(i, i + steps) for i in range(first, last)])  14.2 us
    unnamed x42, local copies, waits for them, and re-layouts  12 us
    all_to_all x1, starting transfers between devices, shards(): lax.all_to_all(back.reshape(EXPERTS, CAPP, BACK), CTX, 0, 0, tiled=True)  8.79 us
  transfers between devices with their start and end apart: 22, of which 13 were waited for; matrix products, arithmetic and copies ran while one was open for 11% of the time, Pallas kernels for 2%

profile of v1, /device:TPU:32, one launch (start us, length us, event | category | flops | bytes accessed | tf_op | source)
XLA Modules:
  0.0 264.4 jit_solution(1413745187696387579)
XLA Ops:
  8.2 4.9 %collective-permute-start = (bf16[48,1440]{1,0:T(8,128)(2,1)S(1)}, bf16[48,1440]{1,0:T(8,128)(2,1)S(1)}, u32[]{:S(2)}, u32[]{:S(2)}) collective-permute-start(bf16[48,1440]{1,0:T(8,128)(2,1)S(1)} %pad.8), channel_id=1, source_target_pairs={{0,2},{2,0},{1,3},{3,1},{4,6},{6,4},{5,7},{7,5},{8,10},{10,8},{9,1... | collective-permute-start | bytes 414728 | tf_op jit(solution)/shard_map/ppermute | solution.py:231
  13.1 2.4 collective-permute-start.10
  15.7 1.5 collective-permute-done
  17.2 1.0 broadcast_select_fusion.3
  18.4 4.3 %collective-permute-start.1 = (bf16[96,1440]{1,0:T(8,128)(2,1)S(1)}, bf16[96,1440]{1,0:T(8,128)(2,1)S(1)}, u32[]{:S(2)}, u32[]{:S(2)}) collective-permute-start(bf16[96,1440]{1,0:T(8,128)(2,1)S(1)} %get-tuple-element.46), channel_id=1, source_target_pairs={{0,4},{4,8},{8,12},{12,16},{16,20},{20,24},{24,28},{28,0},{1,5},{5... | collective-permute-start | bytes 829448 | tf_op jit(solution)/shard_map/ppermute | solution.py:220
  22.6 8.6 %collective-permute-start.2 = (bf16[96,1440]{1,0:T(8,128)(2,1)S(1)}, bf16[96,1440]{1,0:T(8,128)(2,1)S(1)}, u32[]{:S(2)}, u32[]{:S(2)}) collective-permute-start(bf16[96,1440]{1,0:T(8,128)(2,1)S(1)} %get-tuple-element.46), channel_id=1, source_target_pairs={{0,28},{4,0},{8,4},{12,8},{16,12},{20,16},{24,20},{28,24},{1,29},{... | collective-permute-start | bytes 829448 | tf_op jit(solution)/shard_map/ppermute | solution.py:221
  33.0 2.4 collective-permute-done.1
  35.4 1.9 collective-permute-start.3
  37.4 5.1 %collective-permute-start.4 = (bf16[96,1440]{1,0:T(8,128)(2,1)S(1)}, bf16[96,1440]{1,0:T(8,128)(2,1)S(1)}, u32[]{:S(2)}, u32[]{:S(2)}) collective-permute-start(bf16[96,1440]{1,0:T(8,128)(2,1)S(1)} %collective-permute-done.2), channel_id=1, source_target_pairs={{0,28},{4,0},{8,4},{12,8},{16,12},{20,16},{24,20},{28,24},{1,29},{... | collective-permute-start | bytes 829448 | tf_op jit(solution)/shard_map/ppermute | solution.py:221
  42.6 3.2 %collective-permute-done.3 = bf16[96,1440]{1,0:T(8,128)(2,1)S(1)} collective-permute-done((bf16[96,1440]{1,0:T(8,128)(2,1)S(1)}, bf16[96,1440]{1,0:T(8,128)(2,1)S(1)}, u32[]{:S(2)}, u32[]{:S(2)}) %collective-permute-start.3) | collective-permute-done | bytes 276512 | tf_op jit(solution)/shard_map/ppermute | solution.py:220
  45.8 1.9 collective-permute-start.5
  48.1 5.6 %collective-permute-start.6 = (bf16[96,1440]{1,0:T(8,128)(2,1)S(1)}, bf16[96,1440]{1,0:T(8,128)(2,1)S(1)}, u32[]{:S(2)}, u32[]{:S(2)}) collective-permute-start(bf16[96,1440]{1,0:T(8,128)(2,1)S(1)} %collective-permute-done.4), channel_id=1, source_target_pairs={{0,28},{4,0},{8,4},{12,8},{16,12},{20,16},{24,20},{28,24},{1,29},{... | collective-permute-start | bytes 829448 | tf_op jit(solution)/shard_map/ppermute | solution.py:221
  53.7 9.2 %collective-permute-done.5 = bf16[96,1440]{1,0:T(8,128)(2,1)S(1)} collective-permute-done((bf16[96,1440]{1,0:T(8,128)(2,1)S(1)}, bf16[96,1440]{1,0:T(8,128)(2,1)S(1)}, u32[]{:S(2)}, u32[]{:S(2)}) %collective-permute-start.5) | collective-permute-done | bytes 276512 | tf_op jit(solution)/shard_map/ppermute | solution.py:220
  62.9 1.9 collective-permute-start.7
  64.9 5.1 %collective-permute-start.8 = (bf16[48,1440]{1,0:T(8,128)(2,1)S(1)}, bf16[48,1440]{1,0:T(8,128)(2,1)S(1)}, u32[]{:S(2)}, u32[]{:S(2)}) collective-permute-start(bf16[48,1440]{1,0:T(8,128)(2,1)S(1)} %slice.33), channel_id=1, source_target_pairs={{0,28},{4,0},{8,4},{12,8},{16,12},{20,16},{24,20},{28,24},{1,29},{... | collective-permute-start | bytes 414728 | tf_op jit(solution)/shard_map/ppermute | solution.py:225
  70.1 4.2 %collective-permute-done.7 = bf16[48,1440]{1,0:T(8,128)(2,1)S(1)} collective-permute-done((bf16[48,1440]{1,0:T(8,128)(2,1)S(1)}, bf16[48,1440]{1,0:T(8,128)(2,1)S(1)}, u32[]{:S(2)}, u32[]{:S(2)}) %collective-permute-start.7) | collective-permute-done | bytes 138272 | tf_op jit(solution)/shard_map/ppermute | solution.py:224
  74.3 1.3 collective-permute-done.8
  75.6 2.6 copy.38
  78.2 1.9 collective-permute-start.9
  80.5 1.2 copy.37.g_ref
  81.8 1.4 shard_map.163
  84.2 8.2 %all-to-all-start = ((bf16[16,8,3072]{2,1,0:T(8,128)(2,1)}), bf16[16,8,3072]{2,1,0:T(8,128)(2,1)S(1)}, u32[]{:S(2)}, u32[]{:S(2)}) async-start(bf16[16,8,3072]{2,1,0:T(8,128)(2,1)} %bitcast.23), calls=%async_computation | async-start | bytes 1572864 | tf_op jit(solution)/shard_map/all_to_all | solution.py:272
  92.3 4.3 %copy.39.wo_ref = bf16[768,1440]{1,0:T(8,128)(2,1)} copy(bf16[768,1440]{0,1:T(8,128)(2,1)} %collective-permute-done.9) | data formatting | bytes 4423680 | tf_op jit(solution)/shard_map/ppermute | solution.py:276
  96.6 15.1 %all-to-all-done = bf16[16,8,3072]{2,1,0:T(8,128)(2,1)S(1)} async-done(((bf16[16,8,3072]{2,1,0:T(8,128)(2,1)}), bf16[16,8,3072]{2,1,0:T(8,128)(2,1)S(1)}, u32[]{:S(2)}, u32[]{:S(2)}) %all-to-all-start) | async-done | bytes 786464 | tf_op jit(solution)/shard_map/all_to_all | solution.py:272
  111.6 1.7 copy-done
  113.3 3.2 %shard_map.164 = (bf16[128,1664]{1,0:T(8,128)(2,1)}, bf16[128,1440]{1,0:T(8,128)(2,1)S(1)}) custom-call(bf16[128,3072]{1,0:T(8,128)(2,1)S(1)} %bitcast.21, bf16[768,1440]{1,0:T(8,128)(2,1)S(1)} %constant_dynamic-update-slice_fusion.wm_ref, bf16[768,1440]{1,0:T(8,128)(2,1)S(1)} %copy-done), custom_call_target="tpu_custom_call" | custom-call | flops 1132462080 | bytes 6291456 | tf_op jit(solution)/shard_map/pallas_call | solution.py:280
  116.5 1.9 collective-permute-start.17
  118.5 2.4 collective-permute-start.16
  120.9 1.0 collective-permute-done.16
  122.7 2.5 copy.45
  125.2 8.1 %all-to-all-start.2 = ((bf16[16,48,1440]{2,1,0:T(8,128)(2,1)}), bf16[16,48,1440]{2,1,0:T(8,128)(2,1)S(1)}, u32[]{:S(2)}, u32[]{:S(2)}) async-start(bf16[16,48,1440]{2,1,0:T(8,128)(2,1)} %bitcast.26), calls=%async_computation.2 | async-start | bytes 4718592 | tf_op jit(solution)/shard_map/all_to_all | solution.py:296
  133.4 4.8 %copy.40 = bf16[1024,1440]{0,1:T(8,128)(2,1)} copy(bf16[1024,1440]{1,0:T(8,128)(2,1)} %all-gather.2.cloned.1.call-done.om_ref) | data formatting | bytes 5898240 | tf_op jit(solution)/shard_map/all_gather | solution.py:253
  138.2 2.0 collective-permute-start.11
  140.2 51.3 %all-to-all-done.2 = bf16[16,48,1440]{2,1,0:T(8,128)(2,1)S(1)} async-done(((bf16[16,48,1440]{2,1,0:T(8,128)(2,1)}), bf16[16,48,1440]{2,1,0:T(8,128)(2,1)S(1)}, u32[]{:S(2)}, u32[]{:S(2)}) %all-to-all-start.2) | async-done | bytes 2211872 | tf_op jit(solution)/shard_map/all_to_all | solution.py:296
  191.5 8.8 %all-to-all-start.1 = ((bf16[16,8,1664]{2,1,0:T(8,128)(2,1)}), bf16[16,8,1664]{2,1,0:T(8,128)(2,1)}, u32[]{:S(2)}, u32[]{:S(2)}) async-start(bf16[16,8,1664]{2,1,0:T(8,128)(2,1)} %bitcast.6), calls=%async_computation.1 | async-start | bytes 851968 | tf_op jit(solution)/shard_map/all_to_all | solution.py:289
  201.1 2.5 collective-permute-start.12
  203.6 2.1 collective-permute-start.13
  207.0 4.7 %copy.44.oo_ref = bf16[1024,1440]{1,0:T(8,128)(2,1)} copy(bf16[1024,1440]{0,1:T(8,128)(2,1)} %collective-permute-done.11) | data formatting | bytes 5898240 | tf_op jit(solution)/shard_map/ppermute | solution.py:277
  211.7 2.3 collective-permute-done.12.far_ref
  214.1 1.9 collective-permute-done.13.near_ref
  216.0 1.9 copy-done.2
  218.8 1.0 copy-done.8
  220.5 20.6 %shard_map.165 = (bf16[128,1440]{1,0:T(8,128)(2,1)S(1)}, f32[4,128]{1,0:T(4,128)S(1)}, bf16[128,2048]{1,0:T(8,128)(2,1)}, bf16[128,512]{1,0:T(8,128)(2,1)}, bf16...) custom-call(s32[1]{0:T(128)} %bitcast.core_ref, s32[4,128]{1,0:T(4,128)S(1)} %bitcast.25, s32[128,1]{1,0:T(8,128)S(1)} %copy-done.7, ...), custom_call_target="tpu_custom_call" | custom-call | flops 3221225472 | bytes 9437184 | tf_op jit(solution)/shard_map/pallas_call | solution.py:299
  242.5 4.8 %collective-permute-start.14 = (bf16[128,512]{1,0:T(8,128)(2,1)}, bf16[128,512]{1,0:T(8,128)(2,1)S(1)}, u32[]{:S(2)}, u32[]{:S(2)}) collective-permute-start(bf16[128,512]{1,0:T(8,128)(2,1)} %get-tuple-element.17), channel_id=1, source_target_pairs={{1,0},{2,1},{3,2},{4,3},{5,4},{6,5},{7,6},{8,7},{9,8},{10,9},{11,1... | collective-permute-start | bytes 393224 | tf_op jit(solution)/shard_map/ppermute | solution.py:238
  247.3 4.8 %collective-permute-start.15 = (bf16[128,512]{1,0:T(8,128)(2,1)}, bf16[128,512]{1,0:T(8,128)(2,1)S(1)}, u32[]{:S(2)}, u32[]{:S(2)}) collective-permute-start(bf16[128,512]{1,0:T(8,128)(2,1)} %get-tuple-element.18), channel_id=1, source_target_pairs={{2,0},{3,1},{4,2},{5,3},{6,4},{7,5},{8,6},{9,7},{10,8},{11,9},{12,... | collective-permute-start | bytes 393224 | tf_op jit(solution)/shard_map/ppermute | solution.py:238
  252.1 1.9 copy.46
  254.6 1.2 collective-permute-done.15
  255.9 1.0 add_convert_fusion
  (79 shorter events, 12.1 us)
Async XLA Ops:
  7.2 24.1 %copy-start.13 = (bf16[64,1440]{1,0:T(8,128)(2,1)S(1)}, bf16[64,1440]{1,0:T(8,128)(2,1)}, u32[]{:S(2)}) copy-start(bf16[64,1440]{1,0:T(8,128)(2,1)} %param.23) | copy-start | bytes 552964
  7.2 126.2 %all-gather.2.cloned.1.call-start = ((), (), s32[]{:S(2)}) async-start(), calls=%async_computation.3 | async-start | bytes 3538944 | tf_op jit(solution)/shard_map/all_gather | solution.py:253
  8.2 9.0 %collective-permute-start = (bf16[48,1440]{1,0:T(8,128)(2,1)S(1)}, bf16[48,1440]{1,0:T(8,128)(2,1)S(1)}, u32[]{:S(2)}, u32[]{:S(2)}) collective-permute-start(bf16[48,1440]{1,0:T(8,128)(2,1)S(1)} %pad.8), channel_id=1, source_target_pairs={{0,2},{2,0},{1,3},{3,1},{4,6},{6,4},{5,7},{7,5},{8,10},{10,8},{9,1... | collective-permute-start | bytes 414728 | tf_op jit(solution)/shard_map/ppermute | solution.py:231
  13.1 18.1 %collective-permute-start.10 = (bf16[64,1440]{1,0:T(8,128)(2,1)}, bf16[64,1440]{1,0:T(8,128)(2,1)}, u32[]{:S(2)}, u32[]{:S(2)}) collective-permute-start(bf16[64,1440]{1,0:T(8,128)(2,1)} %param.23), channel_id=1, source_target_pairs={{0,2},{2,0},{1,3},{3,1},{4,6},{6,4},{5,7},{7,5},{8,10},{10,8},{9,1... | collective-permute-start | bytes 552968 | tf_op jit(solution)/shard_map/ppermute | solution.py:231
  18.4 17.1 %collective-permute-start.1 = (bf16[96,1440]{1,0:T(8,128)(2,1)S(1)}, bf16[96,1440]{1,0:T(8,128)(2,1)S(1)}, u32[]{:S(2)}, u32[]{:S(2)}) collective-permute-start(bf16[96,1440]{1,0:T(8,128)(2,1)S(1)} %get-tuple-element.46), channel_id=1, source_target_pairs={{0,4},{4,8},{8,12},{12,16},{16,20},{20,24},{24,28},{28,0},{1,5},{5... | collective-permute-start | bytes 829448 | tf_op jit(solution)/shard_map/ppermute | solution.py:220
  22.6 14.7 %collective-permute-start.2 = (bf16[96,1440]{1,0:T(8,128)(2,1)S(1)}, bf16[96,1440]{1,0:T(8,128)(2,1)S(1)}, u32[]{:S(2)}, u32[]{:S(2)}) collective-permute-start(bf16[96,1440]{1,0:T(8,128)(2,1)S(1)} %get-tuple-element.46), channel_id=1, source_target_pairs={{0,28},{4,0},{8,4},{12,8},{16,12},{20,16},{24,20},{28,24},{1,29},{... | collective-permute-start | bytes 829448 | tf_op jit(solution)/shard_map/ppermute | solution.py:221
  35.4 10.3 %collective-permute-start.3 = (bf16[96,1440]{1,0:T(8,128)(2,1)S(1)}, bf16[96,1440]{1,0:T(8,128)(2,1)S(1)}, u32[]{:S(2)}, u32[]{:S(2)}) collective-permute-start(bf16[96,1440]{1,0:T(8,128)(2,1)S(1)} %collective-permute-done.1), channel_id=1, source_target_pairs={{0,4},{4,8},{8,12},{12,16},{16,20},{20,24},{24,28},{28,0},{1,5},{5... | collective-permute-start | bytes 829448 | tf_op jit(solution)/shard_map/ppermute | solution.py:220
  37.4 10.7 %collective-permute-start.4 = (bf16[96,1440]{1,0:T(8,128)(2,1)S(1)}, bf16[96,1440]{1,0:T(8,128)(2,1)S(1)}, u32[]{:S(2)}, u32[]{:S(2)}) collective-permute-start(bf16[96,1440]{1,0:T(8,128)(2,1)S(1)} %collective-permute-done.2), channel_id=1, source_target_pairs={{0,28},{4,0},{8,4},{12,8},{16,12},{20,16},{24,20},{28,24},{1,29},{... | collective-permute-start | bytes 829448 | tf_op jit(solution)/shard_map/ppermute | solution.py:221
  45.8 17.1 %collective-permute-start.5 = (bf16[96,1440]{1,0:T(8,128)(2,1)S(1)}, bf16[96,1440]{1,0:T(8,128)(2,1)S(1)}, u32[]{:S(2)}, u32[]{:S(2)}) collective-permute-start(bf16[96,1440]{1,0:T(8,128)(2,1)S(1)} %collective-permute-done.3), channel_id=1, source_target_pairs={{0,4},{4,8},{8,12},{12,16},{16,20},{20,24},{24,28},{28,0},{1,5},{5... | collective-permute-start | bytes 829448 | tf_op jit(solution)/shard_map/ppermute | solution.py:220
  48.1 16.8 %collective-permute-start.6 = (bf16[96,1440]{1,0:T(8,128)(2,1)S(1)}, bf16[96,1440]{1,0:T(8,128)(2,1)S(1)}, u32[]{:S(2)}, u32[]{:S(2)}) collective-permute-start(bf16[96,1440]{1,0:T(8,128)(2,1)S(1)} %collective-permute-done.4), channel_id=1, source_target_pairs={{0,28},{4,0},{8,4},{12,8},{16,12},{20,16},{24,20},{28,24},{1,29},{... | collective-permute-start | bytes 829448 | tf_op jit(solution)/shard_map/ppermute | solution.py:221
  62.9 11.4 %collective-permute-start.7 = (bf16[48,1440]{1,0:T(8,128)(2,1)S(1)}, bf16[48,1440]{1,0:T(8,128)(2,1)S(1)}, u32[]{:S(2)}, u32[]{:S(2)}) collective-permute-start(bf16[48,1440]{1,0:T(8,128)(2,1)S(1)} %slice.32), channel_id=1, source_target_pairs={{0,4},{4,8},{8,12},{12,16},{16,20},{20,24},{24,28},{28,0},{1,5},{5... | collective-permute-start | bytes 414728 | tf_op jit(solution)/shard_map/ppermute | solution.py:224
  64.9 10.7 %collective-permute-start.8 = (bf16[48,1440]{1,0:T(8,128)(2,1)S(1)}, bf16[48,1440]{1,0:T(8,128)(2,1)S(1)}, u32[]{:S(2)}, u32[]{:S(2)}) collective-permute-start(bf16[48,1440]{1,0:T(8,128)(2,1)S(1)} %slice.33), channel_id=1, source_target_pairs={{0,28},{4,0},{8,4},{12,8},{16,12},{20,16},{24,20},{28,24},{1,29},{... | collective-permute-start | bytes 414728 | tf_op jit(solution)/shard_map/ppermute | solution.py:225
  75.6 4.6 %copy-start.17 = (s32[96]{0:T(128)S(1)}, s32[96]{0:T(128)}, u32[]{:S(2)}) copy-start(s32[96]{0:T(128)} %param.21) | copy-start | bytes 1156
  75.6 4.7 %copy-start.11 = (bf16[128,1440]{0,1:T(8,128)(2,1)S(1)}, bf16[128,1440]{0,1:T(8,128)(2,1)}, u32[]{:S(2)}) copy-start(bf16[128,1440]{0,1:T(8,128)(2,1)} %param.17) | copy-start | bytes 1105924
  75.6 6.1 %copy-start.16 = (bf16[128,4]{0,1:T(4,128)(2,1)S(1)}, bf16[128,4]{0,1:T(4,128)(2,1)}, u32[]{:S(2)}) copy-start(bf16[128,4]{0,1:T(4,128)(2,1)} %param.20) | copy-start | bytes 3076
  75.6 6.2 %copy-start.9 = (s32[128,4]{0,1:T(4,128)S(1)}, s32[128,4]{0,1:T(4,128)}, u32[]{:S(2)}) copy-start(s32[128,4]{0,1:T(4,128)} %param.19) | copy-start | bytes 6148
  78.2 14.1 %collective-permute-start.9 = (bf16[768,1440]{0,1:T(8,128)(2,1)}, bf16[768,1440]{0,1:T(8,128)(2,1)}, u32[]{:S(2)}, u32[]{:S(2)}) collective-permute-start(bf16[768,1440]{0,1:T(8,128)(2,1)} %copy.38), channel_id=1, source_target_pairs={{0,1},{1,0},{2,3},{3,2},{4,5},{5,4},{6,7},{7,6},{8,9},{9,8},{10,11... | collective-permute-start | bytes 6635528 | tf_op jit(solution)/shard_map/ppermute | solution.py:276
  80.3 3.8 %copy-start.6 = (s32[128,1]{1,0:T(8,128)}, s32[128,1]{1,0:T(8,128)S(1)}, u32[]{:S(2)}) copy-start(s32[128,1]{1,0:T(8,128)S(1)} %broadcast_in_dim_reshape.4.held_ref) | copy-start | bytes 1540
  83.2 0.9 copy-start.3
  84.2 27.5 %all-to-all-start = ((bf16[16,8,3072]{2,1,0:T(8,128)(2,1)}), bf16[16,8,3072]{2,1,0:T(8,128)(2,1)S(1)}, u32[]{:S(2)}, u32[]{:S(2)}) async-start(bf16[16,8,3072]{2,1,0:T(8,128)(2,1)} %bitcast.23), calls=%async_computation | async-start | bytes 1572864 | tf_op jit(solution)/shard_map/all_to_all | solution.py:272
  111.6 1.7 copy-start
  116.5 5.4 %collective-permute-start.17 = (bf16[128,1440]{1,0:T(8,128)(2,1)S(1)}, bf16[128,1440]{1,0:T(8,128)(2,1)S(1)}, u32[]{:S(2)}, u32[]{:S(2)}) collective-permute-start(bf16[128,1440]{1,0:T(8,128)(2,1)S(1)} %get-tuple-element.21), channel_id=1, source_target_pairs={{0,1},{1,0},{2,3},{3,2},{4,5},{5,4},{6,7},{7,6},{8,9},{9,8},{10,11... | collective-permute-start | bytes 1105928 | tf_op jit(solution)/shard_map/ppermute | solution.py:292
  118.5 3.5 %collective-permute-start.16 = (bf16[128,768]{1,0:T(8,128)(2,1)S(1)}, bf16[128,768]{1,0:T(8,128)(2,1)S(1)}, u32[]{:S(2)}, u32[]{:S(2)}) collective-permute-start(bf16[128,768]{1,0:T(8,128)(2,1)S(1)} %get-tuple-element.43), channel_id=1, source_target_pairs={{0,1},{1,0},{2,3},{3,2},{4,5},{5,4},{6,7},{7,6},{8,9},{9,8},{10,11... | collective-permute-start | bytes 589832 | tf_op jit(solution)/shard_map/ppermute | solution.py:279
  125.2 66.3 %all-to-all-start.2 = ((bf16[16,48,1440]{2,1,0:T(8,128)(2,1)}), bf16[16,48,1440]{2,1,0:T(8,128)(2,1)S(1)}, u32[]{:S(2)}, u32[]{:S(2)}) async-start(bf16[16,48,1440]{2,1,0:T(8,128)(2,1)} %bitcast.26), calls=%async_computation.2 | async-start | bytes 4718592 | tf_op jit(solution)/shard_map/all_to_all | solution.py:296
  133.3 6.9 %copy-start.18 = (s32[128]{0:T(128)S(1)}, s32[128]{0:T(128)}, u32[]{:S(2)}) copy-start(s32[128]{0:T(128)} %param.15) | copy-start | bytes 1540
  133.3 67.1 %copy-start.14 = (bf16[128,256]{1,0:T(8,128)(2,1)S(1)}, bf16[128,256]{1,0:T(8,128)(2,1)}, u32[]{:S(2)}) copy-start(bf16[128,256]{1,0:T(8,128)(2,1)} %param.14) | copy-start | bytes 196612
  133.3 67.1 %copy-start.15 = (bf16[128,256]{1,0:T(8,128)(2,1)S(1)}, bf16[128,256]{1,0:T(8,128)(2,1)}, u32[]{:S(2)}) copy-start(bf16[128,256]{1,0:T(8,128)(2,1)} %param.13) | copy-start | bytes 196612
  133.3 72.4 %copy-start.12 = (bf16[128,1440]{0,1:T(8,128)(2,1)S(1)}, bf16[128,1440]{0,1:T(8,128)(2,1)}, u32[]{:S(2)}) copy-start(bf16[128,1440]{0,1:T(8,128)(2,1)} %param.16) | copy-start | bytes 1105924
  138.2 68.8 %collective-permute-start.11 = (bf16[1024,1440]{0,1:T(8,128)(2,1)}, bf16[1024,1440]{0,1:T(8,128)(2,1)}, u32[]{:S(2)}, u32[]{:S(2)}) collective-permute-start(bf16[1024,1440]{0,1:T(8,128)(2,1)} %copy.40), channel_id=1, source_target_pairs={{0,1},{1,0},{2,3},{3,2},{4,5},{5,4},{6,7},{7,6},{8,9},{9,8},{10,11... | collective-permute-start | bytes 8847368 | tf_op jit(solution)/shard_map/ppermute | solution.py:277
  191.5 24.5 %all-to-all-start.1 = ((bf16[16,8,1664]{2,1,0:T(8,128)(2,1)}), bf16[16,8,1664]{2,1,0:T(8,128)(2,1)}, u32[]{:S(2)}, u32[]{:S(2)}) async-start(bf16[16,8,1664]{2,1,0:T(8,128)(2,1)} %bitcast.6), calls=%async_computation.1 | async-start | bytes 851968 | tf_op jit(solution)/shard_map/all_to_all | solution.py:289
  201.1 12.9 %collective-permute-start.12 = (bf16[128,640]{1,0:T(8,128)(2,1)}, bf16[128,640]{1,0:T(8,128)(2,1)}, u32[]{:S(2)}, u32[]{:S(2)}) collective-permute-start(bf16[128,640]{1,0:T(8,128)(2,1)} %fusion.7.own_ref), channel_id=1, source_target_pairs={{0,2},{1,3},{2,4},{3,5},{4,6},{5,7},{6,8},{7,9},{8,10},{9,11},{10,... | collective-permute-start | bytes 491528 | tf_op jit(solution)/shard_map/ppermute | solution.py:238
  203.6 12.4 %collective-permute-start.13 = (bf16[128,640]{1,0:T(8,128)(2,1)}, bf16[128,640]{1,0:T(8,128)(2,1)}, u32[]{:S(2)}, u32[]{:S(2)}) collective-permute-start(bf16[128,640]{1,0:T(8,128)(2,1)} %fusion.7.own_ref), channel_id=1, source_target_pairs={{0,1},{1,2},{2,3},{3,4},{4,5},{5,6},{6,7},{7,8},{8,9},{9,10},{10,1... | collective-permute-start | bytes 491528 | tf_op jit(solution)/shard_map/ppermute | solution.py:238
  207.0 9.1 %copy-start.1 = (bf16[1024,1440]{1,0:T(8,128)(2,1)S(1)}, bf16[1024,1440]{1,0:T(8,128)(2,1)}, u32[]{:S(2)}) copy-start(bf16[1024,1440]{1,0:T(8,128)(2,1)} %all-gather.2.cloned.1.call-done.om_ref) | copy-start | bytes 8847364
  216.0 1.9 copy-start.2
  217.9 0.8 copy-start.7
  218.8 1.0 copy-start.8
  219.8 0.7 copy-start.10
  241.1 0.7 copy-start.4
  241.8 0.7 copy-start.5
  242.5 12.1 %collective-permute-start.14 = (bf16[128,512]{1,0:T(8,128)(2,1)}, bf16[128,512]{1,0:T(8,128)(2,1)S(1)}, u32[]{:S(2)}, u32[]{:S(2)}) collective-permute-start(bf16[128,512]{1,0:T(8,128)(2,1)} %get-tuple-element.17), channel_id=1, source_target_pairs={{1,0},{2,1},{3,2},{4,3},{5,4},{6,5},{7,6},{8,7},{9,8},{10,9},{11,1... | collective-permute-start | bytes 393224 | tf_op jit(solution)/shard_map/ppermute | solution.py:238
  247.3 8.6 %collective-permute-start.15 = (bf16[128,512]{1,0:T(8,128)(2,1)}, bf16[128,512]{1,0:T(8,128)(2,1)S(1)}, u32[]{:S(2)}, u32[]{:S(2)}) collective-permute-start(bf16[128,512]{1,0:T(8,128)(2,1)} %get-tuple-element.18), channel_id=1, source_target_pairs={{2,0},{3,1},{4,2},{5,3},{6,4},{7,5},{8,6},{9,7},{10,8},{11,9},{12,... | collective-permute-start | bytes 393224 | tf_op jit(solution)/shard_map/ppermute | solution.py:238
Sparse Core Ops, SparseCore 0:
  33.2 55.8 all-gather.1

commit v2 on v1

v2 whole, which is shorter than its diff:
```python
import jax
import jax.numpy as jnp
from jax import lax
from jax.experimental import pallas as pl
from jax.experimental.pallas import tpu as pltpu
from jax.sharding import Mesh, PartitionSpec as P

TOK = 128
D = 1440
F = 1440
HEADS = 32
KV_HEADS = 4
HD = 64
CAP = 6
CAPP = 8
EXPERTS = 16
ROWS = EXPERTS * CAPP
SEG = 48
SHARD = 45
DP = 1536
HALF = 768
SEND = 3072
BACK = 1664
KV = 256
WIDE = 640
BF = jnp.bfloat16
F32 = jnp.float32
ALL = ("y", "xl", "z", "xh", "core")
CTX = ("y", "xl")
SWAP = ((0, 1), (1, 0))


def dot(a, b, dims):
    return lax.dot_general(a, b, (dims, ((), ())), preferred_element_type=F32)


def spec_vmem():
    return pl.BlockSpec(memory_space=pltpu.VMEM)


def spec_smem():
    return pl.BlockSpec(memory_space=pltpu.SMEM)


def out(shape, dtype=BF):
    return jax.ShapeDtypeStruct(shape, dtype)


def call(kernel, outs, scratch, weight_us, n_smem, n_vmem, n_any=0):
    return pl.pallas_call(
        kernel,
        out_shape=outs,
        in_specs=[spec_smem()] * n_smem
        + [spec_vmem()] * n_vmem
        + [pl.BlockSpec(memory_space=pl.ANY)] * n_any,
        out_specs=[spec_vmem()] * len(outs),
        scratch_shapes=scratch,
        compiler_params=pltpu.CompilerParams(vmem_limit_bytes=26 * 1024 * 1024),
        cost_estimate=pl.CostEstimate(
            flops=0, bytes_accessed=int(weight_us * 3690000), transcendentals=0
        ),
    )


def order(value, *ties):
    return lax.optimization_barrier((value, *ties))[0]


def dispatch_kernel(picked_ref, held_ref, gate_ref, place_ref, x_ref, g_ref, out_ref, sent_ref):
    held = held_ref[...]
    chosen = [picked_ref[s : s + 1, :] == held for s in range(4)]
    routed = chosen[0] | chosen[1] | chosen[2] | chosen[3]
    routed_f = jnp.where(routed, 1.0, 0.0)
    before = lax.broadcasted_iota(jnp.int32, (TOK, TOK), 0) <= lax.broadcasted_iota(
        jnp.int32, (TOK, TOK), 1
    )
    upper = jnp.where(before, 1.0, 0.0).astype(BF)
    rank = dot(routed_f.astype(BF), upper, ((1,), (0,))) - 1.0
    slot = lax.broadcasted_iota(jnp.int32, (ROWS, TOK), 0) % CAPP
    sent = routed & (rank == slot.astype(F32))
    sent_bf = jnp.where(sent, 1.0, 0.0).astype(BF)
    sent_ref[...] = sent_bf
    gate = jnp.zeros((ROWS, TOK), F32)
    for s in range(4):
        gate = gate + jnp.where(chosen[s] & sent, gate_ref[s : s + 1, :], 0.0)
    gate = jnp.sum(gate, axis=1, keepdims=True)
    rows = dot(sent_bf, x_ref[...], ((1,), (1,))).astype(BF)
    feature = lax.broadcasted_iota(jnp.int32, (D, 256), 0)
    for c in range(DP // 256):
        pick = jnp.where(feature == place_ref[:, c * 256 : (c + 1) * 256], 1.0, 0.0).astype(BF)
        out_ref[:, c * 256 : (c + 1) * 256] = dot(rows, pick, ((1,), (0,))).astype(BF)
    grads = dot(sent_bf, g_ref[...], ((1,), (1,))).astype(BF)
    out_ref[:, DP:] = jnp.concatenate(
        [grads, jnp.broadcast_to(gate, (ROWS, SEND - DP - F)).astype(BF)], axis=1
    )


def shares_kernel(q_ref, far_ref, near_ref, own_ref, label_ref, shares_ref, qt_ref, kt_ref, v_ref, kv_s, bias_s):
    for part, ref in enumerate((far_ref, near_ref, own_ref)):
        kv_s[part * TOK : (part + 1) * TOK, :] = ref[...]
    marks = kv_s[:, 2 * KV :].astype(F32)
    docs = marks[:, 0:1] * 16.0 + marks[:, 1:2]
    r_at = lax.broadcasted_iota(jnp.int32, (3 * TOK, TOK), 0)
    p_at = lax.broadcasted_iota(jnp.int32, (3 * TOK, TOK), 1)
    allowed = (r_at <= 2 * TOK + p_at) & (docs == label_ref[...])
    bias = jnp.where(allowed, 0.0, -1e30)
    bias_s[...] = jnp.concatenate([bias, bias], axis=1)
    v_ref[...] = kv_s[:, KV : 2 * KV]
    for t in range(2):
        kt_ref[t * 128 : (t + 1) * 128, :] = jnp.transpose(
            kv_s[:, t * 128 : (t + 1) * 128].astype(F32)
        ).astype(BF)
    for g in range(KV_HEADS):
        k_one = kv_s[:, g * HD : (g + 1) * HD]

        def pair(i, carry, g=g, k_one=k_one):
            at = pl.multiple_of((g * 4 + i) * 128, 128)
            flipped = jnp.transpose(q_ref[:, pl.ds(at, 128)].astype(F32) * 0.125).astype(BF)
            qt_ref[pl.ds(at, 128), :] = flipped
            q_two = jnp.concatenate([flipped[:HD], flipped[HD:]], axis=1)
            s = dot(k_one, q_two, ((1,), (0,))) + bias_s[...]
            e = jnp.exp(s - jnp.max(s, axis=0, keepdims=True))
            shares = e * (1.0 / jnp.sum(e, axis=0, keepdims=True))
            shares_ref[:, pl.ds(pl.multiple_of(2 * at, 256), 256)] = shares.astype(BF)
            return carry

        lax.fori_loop(0, 4, pair, 0)


def expert_kernel(got_ref, wm_ref, wo_ref, back_ref, pg_ref, pre_ref):
    step = 512
    for lo in range(0, DP, step):
        at = slice(lo, lo + step)
        pre_ref[:, at] = dot(got_ref[:, :HALF], wm_ref[:, at], ((1,), (0,))) + dot(
            got_ref[:, HALF:DP], wo_ref[:, at], ((1,), (0,))
        )
    gate = got_ref[:, DP + F : DP + F + 1].astype(F32)
    total = jnp.zeros((ROWS, 1), F32)
    for lo in range(0, DP, step):
        pre = pre_ref[:, lo : lo + step]
        grad = got_ref[:, DP + lo : DP + lo + step].astype(F32)
        sig = 1.0 / (1.0 + jnp.exp(-pre))
        total = total + jnp.sum(grad * (pre * sig), axis=1, keepdims=True)
        slope = sig * (1.0 + pre * (1.0 - sig))
        pg_ref[:, lo : lo + step] = (gate * grad * slope).astype(BF)
    pg = pg_ref[...]
    for c in range(HALF // 256):
        r = slice(c * 256, (c + 1) * 256)
        back_ref[:, c * 256 : (c + 1) * 256] = dot(pg, wm_ref[r, :], ((1,), (1,))).astype(BF)
        back_ref[:, HALF + c * 256 : HALF + (c + 1) * 256] = dot(
            pg, wo_ref[r, :], ((1,), (1,))
        ).astype(BF)
    back_ref[:, DP:] = jnp.broadcast_to(total, (ROWS, BACK - DP)).astype(BF)


def map_kernel(x_ref, x2_ref, pg_ref, pg2_ref, out_ref):
    pg = jnp.concatenate([pg_ref[...], pg2_ref[...]], axis=0)
    for c in range(HALF // 256):
        at = slice(c * 256, (c + 1) * 256)
        rows = jnp.concatenate([x_ref[:, at], x2_ref[:, at]], axis=0)
        out_ref[at, :] = dot(rows, pg, ((0,), (0,))).astype(BF)


def late_kernel(
    core_ref, picked_ref, held_ref, sent_ref, place_ref, back_ref, v_ref,
    skip_any, om_any, oo_any, qt_any, shares_any,
    src_ref, gate_ref, sg_ref, farg_ref, nearg_ref, owng_ref,
    hidden_s, cot_s, acck_s, accv_s, skip_ref, om_ref, oo_ref, qt_ref, shares_ref, sems,
):
    pairs = (
        (skip_any, skip_ref), (om_any, om_ref), (oo_any, oo_ref),
        (qt_any, qt_ref), (shares_any, shares_ref),
    )
    copies = [
        pltpu.make_async_copy(source, target, sems.at[i])
        for i, (source, target) in enumerate(pairs)
    ]
    for copy in copies:
        copy.start()
    sent_bf = sent_ref[...]
    sent = sent_bf.astype(F32) > 0.5
    held = held_ref[...]
    gate_part = back_ref[:, DP : DP + 1].astype(F32)
    for s in range(4):
        mine = (picked_ref[s : s + 1, :] == held) & sent
        gate_ref[s : s + 1, :] = jnp.sum(jnp.where(mine, gate_part, 0.0), axis=0, keepdims=True)
    src = dot(sent_bf, back_ref[:, :DP], ((0,), (0,))).astype(BF)
    feature = lax.broadcasted_iota(jnp.int32, (D, 256), 0)
    total = jnp.zeros((D, TOK), F32)
    for c in range(DP // 256):
        pick = jnp.where(feature == place_ref[:, c * 256 : (c + 1) * 256], 1.0, 0.0).astype(BF)
        total = total + dot(pick, src[:, c * 256 : (c + 1) * 256], ((1,), (1,)))
    src_ref[...] = total.astype(BF)
    copies[0].wait()
    hidden_s[:D, :] = (skip_ref[...].astype(F32) + total).astype(BF)
    hidden_s[D:, :] = jnp.zeros((DP - D, TOK), BF)

    core = core_ref[0]
    for ref, place, copy in (
        (om_ref, core * HD, copies[1]),
        (oo_ref, HD - core * HD, copies[2]),
    ):
        copy.wait()
        for c in range(4):
            block = dot(ref[c * 256 : (c + 1) * 256, :], hidden_s[...], ((1,), (0,))).astype(BF)
            for j in range(4):
                at = pl.multiple_of((c * 4 + j) * 128 + place, HD)
                cot_s[pl.ds(at, HD), :] = block[j * HD : (j + 1) * HD]

    copies[3].wait()
    copies[4].wait()
    for t in range(2):
        sums = []
        for g in (2 * t, 2 * t + 1):
            v_one = v_ref[:, g * HD : (g + 1) * HD]
            for i in range(4):
                n = g * 4 + i
                rows = slice(n * 128, n * 128 + HD), slice(n * 128 + HD, (n + 1) * 128)
                q_two = jnp.concatenate([qt_ref[rows[0], :], qt_ref[rows[1], :]], axis=1)
                c_two = jnp.concatenate([cot_s[rows[0], :], cot_s[rows[1], :]], axis=1)
                low = shares_ref[:, n * 256 : (n + 1) * 256]
                dp = dot(v_one, c_two, ((1,), (0,)))
                shares = low.astype(F32)
                centre = jnp.sum(shares * dp, axis=0, keepdims=True)
                sg = (shares * (dp - centre)).astype(BF)
                sg_ref[:, n * 256 : (n + 1) * 256] = sg
                ak = dot(sg, q_two, ((1,), (1,)))
                av = dot(low, c_two, ((1,), (1,)))
                if i == 0:
                    acck_s[...] = ak
                    accv_s[...] = av
                else:
                    acck_s[...] += ak
                    accv_s[...] += av
            sums.append((acck_s[...], accv_s[...]))
        for kind in range(2):
            tile = jnp.concatenate([sums[0][kind], sums[1][kind]], axis=1)
            at = slice(kind * KV + t * 128, kind * KV + (t + 1) * 128)
            farg_ref[:, at] = tile[:TOK].astype(BF)
            nearg_ref[:, at] = tile[TOK : 2 * TOK].astype(BF)
            owng_ref[:, at] = tile[2 * TOK :]


def query_kernel(sg_ref, kt_ref, qg_ref):
    for n in range(16):
        g = n // 4
        qg = dot(kt_ref[g * HD : (g + 1) * HD, :], sg_ref[:, n * 256 : (n + 1) * 256], ((1,), (0,)))
        both = jnp.concatenate([qg[:, :TOK], qg[:, TOK:]], axis=0) * 0.125
        qg_ref[:, n * 128 : (n + 1) * 128] = jnp.transpose(both).astype(BF)


RIGHT = [(i, (i + 1) % 8) for i in range(8)]
LEFT = [(i, (i + 7) % 8) for i in range(8)]


def reduce_start(parts, returned):
    half = parts.shape[1] // 2
    z = lax.axis_index("z")

    def chunk(k):
        return lax.dynamic_index_in_dim(parts, (z + k) % 8, 0, keepdims=False)

    right = lax.ppermute(chunk(4)[:half], "z", RIGHT)
    left = lax.ppermute(chunk(4)[half:], "z", LEFT)
    right, left = lax.optimization_barrier((right, left))
    right = jnp.pad(right, ((0, half), (0, 0)))
    left = jnp.pad(left, ((half, 0), (0, 0)))
    for k in (3, 2):
        right = (chunk(k).astype(F32) + right.astype(F32)).astype(BF)
        left = (chunk(8 - k).astype(F32) + left.astype(F32)).astype(BF)
        ties = (returned,) if k == 2 else ()
        right, left = lax.optimization_barrier((right, left, *ties))[:2]
        right = lax.ppermute(right, "z", RIGHT)
        left = lax.ppermute(left, "z", LEFT)
        right, left = lax.optimization_barrier((right, left))
    right = (chunk(1).astype(F32) + right.astype(F32)).astype(BF)
    left = (chunk(7).astype(F32) + left.astype(F32)).astype(BF)
    return right, left, chunk(0)


def reduce_end(right, left, mine, late):
    right, left = lax.optimization_barrier((right, left, late))[:2]
    right = lax.ppermute(right, "z", RIGHT)
    left = lax.ppermute(left, "z", LEFT)
    return mine.astype(F32) + right.astype(F32) + left.astype(F32)


def both_xh(piece):
    other = lax.ppermute(piece, "xh", SWAP)
    lower = lax.axis_index("xh") == 0
    return jnp.concatenate(
        [jnp.where(lower, piece, other), jnp.where(lower, other, piece)], axis=0
    )


def shift_blocks(value, steps):
    first, last = max(0, -steps), min(512, 512 - steps)
    return lax.ppermute(value, ALL, [(i, i + steps) for i in range(first, last)])


def shards(q, keys, values, label, skip, x, g, picked, mix, retained, weights, out_map):
    core = lax.axis_index("core")
    w_pad = jnp.pad(weights[0], ((0, SEG - SHARD), (0, DP - F)))
    o_pad = jnp.pad(out_map, ((0, 0), (0, DP - D)))
    w_pair = both_xh(w_pad)
    w_mine = lax.all_gather(w_pair, "z", axis=0, tiled=True)

    plus = (label + 1).astype(jnp.int32)
    marks = jnp.stack([plus // 16, plus % 16], axis=1).astype(BF)
    own = jnp.concatenate(
        [keys, values, jnp.pad(marks, ((0, 0), (0, WIDE - 2 * KV - 2)))], axis=1
    )
    picked_t = order(picked.T, w_pair)
    held = jnp.repeat(retained[:EXPERTS], CAPP)[:, None]
    spot = jnp.arange(DP, dtype=jnp.int32)
    half = spot // HALF
    rest = spot % HALF
    within = rest % SEG
    owner = (rest // SEG) * 2 + (half ^ core)
    place = jnp.where(within < SHARD, owner * SHARD + within, -1)[None, :]
    send, sent = call(dispatch_kernel, [out((ROWS, SEND)), out((ROWS, TOK))], [], 2, 0, 6)(
        picked_t, held, mix.astype(F32).T, place, x.T, g.T
    )
    o_pair = both_xh(order(o_pad, send))
    o_mine = lax.all_gather(o_pair, "z", axis=0, tiled=True)
    got = lax.all_to_all(send.reshape(EXPERTS, CAPP, SEND), CTX, 0, 0, tiled=True)
    got = got.reshape(ROWS, SEND)
    x_swapped = lax.ppermute(got[:, HALF:DP], "core", SWAP)
    own = order(own, send)
    near = shift_blocks(own, 1)
    far = shift_blocks(own, 2)

    shares, q_t, k_t, v_win = call(
        shares_kernel,
        [
            out((3 * TOK, HEADS * TOK)),
            out((HEADS * HD, TOK)),
            out((KV, 3 * TOK)),
            out((3 * TOK, KV)),
        ],
        [pltpu.VMEM((3 * TOK, WIDE), BF), pltpu.VMEM((3 * TOK, 2 * TOK), F32)],
        8,
        0,
        5,
    )(q, far, near, own, plus.astype(F32)[None, :])

    w_mine = order(w_mine, v_win, x_swapped, o_pair)
    w_other = lax.ppermute(w_mine, "core", SWAP)
    back, pg = call(
        expert_kernel,
        [out((ROWS, BACK)), out((ROWS, DP))],
        [pltpu.VMEM((ROWS, DP), F32)],
        3,
        0,
        3,
    )(got, w_mine, w_other)
    returned = lax.all_to_all(back.reshape(EXPERTS, CAPP, BACK), CTX, 0, 0, tiled=True)
    returned = returned.reshape(ROWS, BACK)

    pg_swapped = lax.ppermute(pg, "core", SWAP)
    partial = call(map_kernel, [out((HALF, DP))], [], 2, 0, 4)(
        got[:, :HALF], x_swapped, pg, pg_swapped
    )[0]
    right, left, mine = reduce_start(partial.reshape(8, 2 * SEG, DP), returned)
    o_mine = order(o_mine, right, left)
    o_other = lax.ppermute(o_mine, "core", SWAP)
    src_t, gate_t, sg, far_g, near_g, own_g = call(
        late_kernel,
        [
            out((D, TOK)),
            out((4, TOK), F32),
            out((3 * TOK, HEADS * TOK)),
            out((TOK, 2 * KV)),
            out((TOK, 2 * KV)),
            out((TOK, 2 * KV), F32),
        ],
        [
            pltpu.VMEM((DP, TOK), BF),
            pltpu.VMEM((HEADS * HD, TOK), BF),
            pltpu.VMEM((3 * TOK, HD), F32),
            pltpu.VMEM((3 * TOK, HD), F32),
            pltpu.VMEM((D, TOK), BF),
            pltpu.VMEM((16 * HD, DP), BF),
            pltpu.VMEM((16 * HD, DP), BF),
            pltpu.VMEM((HEADS * HD, TOK), BF),
            pltpu.VMEM((3 * TOK, HEADS * TOK), BF),
            pltpu.SemaphoreType.DMA((5,)),
        ],
        8,
        1,
        6,
        5,
    )(
        core[None].astype(jnp.int32), picked_t, held, sent, place, returned, v_win,
        skip.T, o_mine, o_other, q_t, shares,
    )
    merged = reduce_end(right, left, mine, near_g)
    xh = lax.axis_index("xh")
    away = lax.dynamic_slice_in_dim(merged, (1 - xh) * SEG, SEG, 0).astype(BF)
    kept = lax.dynamic_slice_in_dim(merged, xh * SEG, SEG, 0)
    map_grad = (kept + lax.ppermute(away, "xh", SWAP).astype(F32)).astype(BF)
    map_grad = map_grad[None, :SHARD, :F]

    got_near = shift_blocks(near_g, -1)
    got_far = shift_blocks(far_g, -2)
    q_grad = call(query_kernel, [out((TOK, HEADS * HD))], [], 3, 0, 2)(sg, k_t)[0]
    kv_grad = (own_g + got_near.astype(F32) + got_far.astype(F32)).astype(BF)
    return (
        q_grad,
        kv_grad[:, :KV],
        kv_grad[:, KV:],
        src_t.T,
        gate_t.T.astype(BF),
        map_grad,
    )


def solution(mesh):
    fine = Mesh(mesh.devices.reshape(8, 2, 8, 2, 2), ALL)
    rows = P(ALL, None)
    fsdp = ("z", "xh", "core")
    return jax.shard_map(
        shards,
        mesh=fine,
        in_specs=(
            rows, rows, rows, P(ALL), rows, rows, rows, rows, rows, P(),
            P(CTX, fsdp, None), P(fsdp, None),
        ),
        out_specs=(rows, rows, rows, rows, rows, P(CTX, fsdp, None)),
        check_vma=False,
    )
```

time: 266 us -> 220 us (0.83)
  the two profiles are of different devices: /device:TPU:32 before, /device:TPU:8 now
where the time goes in v2:
time: 220 us; the launch traced here: 218 us
  starting transfers between devices  80.9 us (37%)
  waiting for transfers between devices  64.2 us (29%)
  Pallas kernels  26.8 us (12%)
  local copies, waits for them, and re-layouts  21.2 us (10%)
  between operations  14.6 us (7%)
  other arithmetic  10.7 us (5%)
    unnamed x54, local copies, waits for them, and re-layouts  17.9 us
    ppermute x4, starting transfers between devices, shift_blocks(): lax.ppermute(value, ALL, [(i, i + steps) for i in range(first, last)])  16.4 us
    ppermute x4, waiting for transfers between devices, shift_blocks(): lax.ppermute(value, ALL, [(i, i + steps) for i in range(first, last)])  15.5 us
    pallas_call x1, Pallas kernels, shards(): call(late_kernel, [out((D, TOK)), out((4, TOK), F32), out((3 * TOK, HEADS...  12.6 us
    ppermute x2, starting transfers between devices, reduce_start(): left = lax.ppermute(left, 'z', LEFT)  10.7 us
    ppermute x2, starting transfers between devices, both_xh(): other = lax.ppermute(piece, 'xh', SWAP)  9.27 us
    ppermute x2, waiting for transfers between devices, both_xh(): other = lax.ppermute(piece, 'xh', SWAP)  9.07 us
    all_to_all x1, starting transfers between devices, shards(): lax.all_to_all(send.reshape(EXPERTS, CAPP, SEND), CTX, 0, 0, tiled=True)  8.92 us
  transfers between devices with their start and end apart: 23, of which 15 were waited for; matrix products, arithmetic and copies ran while one was open for 5% of the time, Pallas kernels for 7%

profile of v2, /device:TPU:8, one launch (start us, length us, event | category | flops | bytes accessed | tf_op | source)
XLA Modules:
  0.0 218.5 jit_solution(11259973472985838878)
XLA Ops:
  8.2 4.9 %collective-permute-start = (bf16[48,1536]{1,0:T(8,128)(2,1)S(1)}, bf16[48,1536]{1,0:T(8,128)(2,1)S(1)}, u32[]{:S(2)}, u32[]{:S(2)}) collective-permute-start(bf16[48,1536]{1,0:T(8,128)(2,1)S(1)} %pad.20), channel_id=1, source_target_pairs={{0,2},{2,0},{1,3},{3,1},{4,6},{6,4},{5,7},{7,5},{8,10},{10,8},{9,1... | collective-permute-start | bytes 442376 | tf_op jit(solution)/shard_map/ppermute | solution.py:289
  13.1 4.0 %collective-permute-done = bf16[48,1536]{1,0:T(8,128)(2,1)S(1)} collective-permute-done((bf16[48,1536]{1,0:T(8,128)(2,1)S(1)}, bf16[48,1536]{1,0:T(8,128)(2,1)S(1)}, u32[]{:S(2)}, u32[]{:S(2)}) %collective-permute-start) | collective-permute-done | bytes 147488 | tf_op jit(solution)/shard_map/ppermute | solution.py:289
  23.2 2.1 shard_map.163
  25.9 8.9 %all-to-all-start = ((bf16[16,8,3072]{2,1,0:T(8,128)(2,1)}), bf16[16,8,3072]{2,1,0:T(8,128)(2,1)S(1)}, u32[]{:S(2)}, u32[]{:S(2)}) async-start(bf16[16,8,3072]{2,1,0:T(8,128)(2,1)} %bitcast.6), calls=%async_computation | async-start | bytes 1572864 | tf_op jit(solution)/shard_map/all_to_all | solution.py:326
  35.0 4.3 %collective-permute-start.4 = (bf16[64,1536]{1,0:T(8,128)(2,1)S(1)}, bf16[64,1536]{1,0:T(8,128)(2,1)S(1)}, u32[]{:S(2)}, u32[]{:S(2)}) collective-permute-start(bf16[64,1536]{1,0:T(8,128)(2,1)S(1)} %pad.22), channel_id=1, source_target_pairs={{0,2},{2,0},{1,3},{3,1},{4,6},{6,4},{5,7},{7,5},{8,10},{10,8},{9,1... | collective-permute-start | bytes 589832 | tf_op jit(solution)/shard_map/ppermute | solution.py:289
  39.3 5.0 %collective-permute-done.4 = bf16[64,1536]{1,0:T(8,128)(2,1)S(1)} collective-permute-done((bf16[64,1536]{1,0:T(8,128)(2,1)S(1)}, bf16[64,1536]{1,0:T(8,128)(2,1)S(1)}, u32[]{:S(2)}, u32[]{:S(2)}) %collective-permute-start.4) | collective-permute-done | bytes 196640 | tf_op jit(solution)/shard_map/ppermute | solution.py:289
  45.4 8.4 %all-to-all-done = bf16[16,8,3072]{2,1,0:T(8,128)(2,1)S(1)} async-done(((bf16[16,8,3072]{2,1,0:T(8,128)(2,1)}), bf16[16,8,3072]{2,1,0:T(8,128)(2,1)S(1)}, u32[]{:S(2)}, u32[]{:S(2)}) %all-to-all-start) | async-done | bytes 786464 | tf_op jit(solution)/shard_map/all_to_all | solution.py:326
  53.8 1.9 collective-permute-start.3
  55.8 4.5 %collective-permute-start.1 = (bf16[128,640]{1,0:T(8,128)(2,1)S(1)}, bf16[128,640]{1,0:T(8,128)(2,1)S(1)}, u32[]{:S(2)}, u32[]{:S(2)}) collective-permute-start(bf16[128,640]{1,0:T(8,128)(2,1)S(1)} %fusion.9.own_ref), channel_id=1, source_target_pairs={{0,2},{1,3},{2,4},{3,5},{4,6},{5,7},{6,8},{7,9},{8,10},{9,11},{10,... | collective-permute-start | bytes 491528 | tf_op jit(solution)/shard_map/ppermute | solution.py:298
  60.3 2.1 collective-permute-start.2
  62.4 12.2 %collective-permute-done.1.far_ref = bf16[128,640]{1,0:T(8,128)(2,1)S(1)} collective-permute-done((bf16[128,640]{1,0:T(8,128)(2,1)S(1)}, bf16[128,640]{1,0:T(8,128)(2,1)S(1)}, u32[]{:S(2)}, u32[]{:S(2)}) %collective-permute-start.1) | collective-permute-done | bytes 163872 | tf_op jit(solution)/shard_map/ppermute | solution.py:298
  74.6 1.6 collective-permute-done.2.near_ref
  76.2 7.2 %shard_map.164 = (bf16[384,4096]{1,0:T(8,128)(2,1)S(1)}, bf16[2048,128]{1,0:T(8,128)(2,1)S(1)}, bf16[256,384]{1,0:T(8,128)(2,1)S(1)}, bf16[384,256]{1,0:T(8,128)(2,1)S(1)}) custom-call(bf16[128,2048]{1,0:T(8,128)(2,1)S(1)} %copy-done.4, bf16[128,640]{1,0:T(8,128)(2,1)S(1)} %collective-permute-done.1.far_ref, ...), custom_call_target="tpu_custom_call" | custom-call | bytes 29520000 | tf_op jit(solution)/shard_map/pallas_call | solution.py:333
  83.4 1.7 copy-done.1
  87.1 1.9 collective-permute-start.5
  89.1 4.7 %collective-permute-done.5.wo_ref = bf16[768,1536]{1,0:T(8,128)(2,1)S(1)} collective-permute-done((bf16[768,1536]{1,0:T(8,128)(2,1)}, bf16[768,1536]{1,0:T(8,128)(2,1)S(1)}, u32[]{:S(2)}, u32[]{:S(2)}) %collective-permute-start.5) | collective-permute-done | bytes 2359328 | tf_op jit(solution)/shard_map/ppermute | solution.py:348
  93.8 1.7 copy-done.3
  95.5 2.5 %shard_map.165 = (bf16[128,1664]{1,0:T(8,128)(2,1)S(1)}, bf16[128,1536]{1,0:T(8,128)(2,1)S(1)}) custom-call(bf16[128,3072]{1,0:T(8,128)(2,1)S(1)} %bitcast.56, bf16[768,1536]{1,0:T(8,128)(2,1)S(1)} %copy-done.3, bf16[768,1536]{1,0:T(8,128)(2,1)S(1)} %collective-permute-done.5.wo_ref), custom_call_target="tpu_custom_call" | custom-call | bytes 11070000 | tf_op jit(solution)/shard_map/pallas_call | solution.py:349
  98.7 2.0 collective-permute-start.6
  100.8 1.6 collective-permute-done.6.pg2_ref
  103.1 1.0 copy-done.7
  106.6 1.9 collective-permute-start.7
  108.5 5.1 %collective-permute-start.8 = (bf16[48,1536]{1,0:T(8,128)(2,1)}, bf16[48,1536]{1,0:T(8,128)(2,1)}, u32[]{:S(2)}, u32[]{:S(2)}) collective-permute-start(bf16[48,1536]{1,0:T(8,128)(2,1)} %get-tuple-element.76), channel_id=1, source_target_pairs={{0,28},{4,0},{8,4},{12,8},{16,12},{20,16},{24,20},{28,24},{1,29},{... | collective-permute-start | bytes 442376 | tf_op jit(solution)/shard_map/ppermute | solution.py:264
  113.6 6.4 %all-to-all-start.1 = ((bf16[16,8,1664]{2,1,0:T(8,128)(2,1)}), bf16[16,8,1664]{2,1,0:T(8,128)(2,1)S(1)}, u32[]{:S(2)}, u32[]{:S(2)}) async-start(bf16[16,8,1664]{2,1,0:T(8,128)(2,1)} %bitcast.58), calls=%async_computation.1 | async-start | bytes 851968 | tf_op jit(solution)/shard_map/all_to_all | solution.py:357
  120.5 1.9 fusion.3
  122.3 5.6 %collective-permute-start.10 = (bf16[96,1536]{1,0:T(8,128)(2,1)}, bf16[96,1536]{1,0:T(8,128)(2,1)}, u32[]{:S(2)}, u32[]{:S(2)}) collective-permute-start(bf16[96,1536]{1,0:T(8,128)(2,1)} %get-tuple-element.49), channel_id=1, source_target_pairs={{0,28},{4,0},{8,4},{12,8},{16,12},{20,16},{24,20},{28,24},{1,29},{... | collective-permute-start | bytes 884744 | tf_op jit(solution)/shard_map/ppermute | solution.py:274
  127.9 1.9 collective-permute-start.9
  129.9 4.2 %collective-permute-done.10 = bf16[96,1536]{1,0:T(8,128)(2,1)} collective-permute-done((bf16[96,1536]{1,0:T(8,128)(2,1)}, bf16[96,1536]{1,0:T(8,128)(2,1)}, u32[]{:S(2)}, u32[]{:S(2)}) %collective-permute-start.10) | collective-permute-done | bytes 294944 | tf_op jit(solution)/shard_map/ppermute | solution.py:274
  134.1 5.3 %collective-permute-done.9 = bf16[96,1536]{1,0:T(8,128)(2,1)} collective-permute-done((bf16[96,1536]{1,0:T(8,128)(2,1)}, bf16[96,1536]{1,0:T(8,128)(2,1)}, u32[]{:S(2)}, u32[]{:S(2)}) %collective-permute-start.9) | collective-permute-done | bytes 294944 | tf_op jit(solution)/shard_map/ppermute | solution.py:273
  139.4 2.0 fusion.2
  141.4 1.9 collective-permute-start.11
  143.4 5.1 %collective-permute-start.12 = (bf16[96,1536]{1,0:T(8,128)(2,1)}, bf16[96,1536]{1,0:T(8,128)(2,1)}, u32[]{:S(2)}, u32[]{:S(2)}) collective-permute-start(bf16[96,1536]{1,0:T(8,128)(2,1)} %get-tuple-element.53), channel_id=1, source_target_pairs={{0,28},{4,0},{8,4},{12,8},{16,12},{20,16},{24,20},{28,24},{1,29},{... | collective-permute-start | bytes 884744 | tf_op jit(solution)/shard_map/ppermute | solution.py:274
  148.5 3.5 %collective-permute-done.11 = bf16[96,1536]{1,0:T(8,128)(2,1)} collective-permute-done((bf16[96,1536]{1,0:T(8,128)(2,1)}, bf16[96,1536]{1,0:T(8,128)(2,1)}, u32[]{:S(2)}, u32[]{:S(2)}) %collective-permute-start.11) | collective-permute-done | bytes 294944 | tf_op jit(solution)/shard_map/ppermute | solution.py:273
  152.0 1.2 collective-permute-done.12
  153.2 2.0 fusion.1
  155.2 2.1 collective-permute-start.13
  157.3 5.8 %collective-permute-done.13.oo_any = bf16[1024,1536]{1,0:T(8,128)(2,1)} collective-permute-done((bf16[1024,1536]{1,0:T(8,128)(2,1)}, bf16[1024,1536]{1,0:T(8,128)(2,1)}, u32[]{:S(2)}, u32[]{:S(2)}) %collective-permute-start.13) | collective-permute-done | bytes 3145760 | tf_op jit(solution)/shard_map/ppermute | solution.py:366
  163.1 1.9 copy-done
  165.0 1.9 copy-done.2
  168.8 12.6 %shard_map.167 = (bf16[1440,128]{1,0:T(8,128)(2,1)}, f32[4,128]{1,0:T(4,128)S(1)}, bf16[384,4096]{1,0:T(8,128)(2,1)S(1)}, bf16[128,512]{1,0:T(8,128)(2,1)S(1)}, ...) custom-call(s32[1]{0:T(128)} %bitcast.core_ref, s32[4,128]{1,0:T(4,128)S(1)} %bitcast.63, ...), custom_call_target="tpu_custom_call" | custom-call | bytes 29520000 | tf_op jit(solution)/shard_map/pallas_call | solution.py:367
  181.4 5.3 %collective-permute-start.14 = (bf16[128,512]{1,0:T(8,128)(2,1)S(1)}, bf16[128,512]{1,0:T(8,128)(2,1)S(1)}, u32[]{:S(2)}, u32[]{:S(2)}) collective-permute-start(bf16[128,512]{1,0:T(8,128)(2,1)S(1)} %get-tuple-element.62), channel_id=1, source_target_pairs={{1,0},{2,1},{3,2},{4,3},{5,4},{6,5},{7,6},{8,7},{9,8},{10,9},{11,1... | collective-permute-start | bytes 393224 | tf_op jit(solution)/shard_map/ppermute | solution.py:298
  186.7 1.9 collective-permute-start.16
  188.7 5.1 %collective-permute-start.17 = (bf16[96,1536]{1,0:T(8,128)(2,1)S(1)}, bf16[96,1536]{1,0:T(8,128)(2,1)S(1)}, u32[]{:S(2)}, u32[]{:S(2)}) collective-permute-start(bf16[96,1536]{1,0:T(8,128)(2,1)S(1)} %copy-done.21), channel_id=1, source_target_pairs={{0,28},{4,0},{8,4},{12,8},{16,12},{20,16},{24,20},{28,24},{1,29},{... | collective-permute-start | bytes 884744 | tf_op jit(solution)/shard_map/ppermute | solution.py:284
  193.8 4.5 %collective-permute-start.15 = (bf16[128,512]{1,0:T(8,128)(2,1)S(1)}, bf16[128,512]{1,0:T(8,128)(2,1)S(1)}, u32[]{:S(2)}, u32[]{:S(2)}) collective-permute-start(bf16[128,512]{1,0:T(8,128)(2,1)S(1)} %get-tuple-element.63), channel_id=1, source_target_pairs={{2,0},{3,1},{4,2},{5,3},{6,4},{7,5},{8,6},{9,7},{10,8},{11,9},{12,... | collective-permute-start | bytes 393224 | tf_op jit(solution)/shard_map/ppermute | solution.py:298
  198.9 1.6 shard_map.168
  200.4 1.7 collective-permute-done.15
  202.4 3.2 %collective-permute-start.18 = (bf16[48,1536]{1,0:T(8,128)(2,1)S(1)}, bf16[48,1536]{1,0:T(8,128)(2,1)S(1)}, u32[]{:S(2)}, u32[]{:S(2)}) collective-permute-start(bf16[48,1536]{1,0:T(8,128)(2,1)S(1)} %dynamic-slice_convert_fusion), channel_id=1, source_target_pairs={{0,2},{2,0},{1,3},{3,1},{4,6},{6,4},{5,7},{7,5},{8,10},{10,8},{9,1... | collective-permute-start | bytes 442376 | tf_op jit(solution)/shard_map/ppermute | solution.py:401
  206.2 4.7 %collective-permute-done.18 = bf16[48,1536]{1,0:T(8,128)(2,1)S(1)} collective-permute-done((bf16[48,1536]{1,0:T(8,128)(2,1)S(1)}, bf16[48,1536]{1,0:T(8,128)(2,1)S(1)}, u32[]{:S(2)}, u32[]{:S(2)}) %collective-permute-start.18) | collective-permute-done | bytes 147488 | tf_op jit(solution)/shard_map/ppermute | solution.py:401
  (86 shorter events, 19.1 us)
Async XLA Ops:
  7.2 27.7 %copy-start.23 = (bf16[64,1440]{1,0:T(8,128)(2,1)S(1)}, bf16[64,1440]{1,0:T(8,128)(2,1)}, u32[]{:S(2)}) copy-start(bf16[64,1440]{1,0:T(8,128)(2,1)} %param.23) | copy-start | bytes 552964
  7.2 27.8 %copy-start.26 = (s32[128]{0:T(128)S(1)}, s32[128]{0:T(128)}, u32[]{:S(2)}) copy-start(s32[128]{0:T(128)} %param.15) | copy-start | bytes 1540
  7.2 80.0 %all-gather.3.cloned.1.call-start = ((), (), s32[]{:S(2)}) async-start(), calls=%async_computation.2 | async-start | bytes 2654208 | tf_op jit(solution)/shard_map/all_gather | solution.py:306
  8.2 9.0 %collective-permute-start = (bf16[48,1536]{1,0:T(8,128)(2,1)S(1)}, bf16[48,1536]{1,0:T(8,128)(2,1)S(1)}, u32[]{:S(2)}, u32[]{:S(2)}) collective-permute-start(bf16[48,1536]{1,0:T(8,128)(2,1)S(1)} %pad.20), channel_id=1, source_target_pairs={{0,2},{2,0},{1,3},{3,1},{4,6},{6,4},{5,7},{7,5},{8,10},{10,8},{9,1... | collective-permute-start | bytes 442376 | tf_op jit(solution)/shard_map/ppermute | solution.py:289
  20.5 1.0 copy-start.8
  21.5 1.0 copy-start.9
  22.5 0.7 copy-start.19
  25.9 29.8 %copy-start.24 = (bf16[128,256]{1,0:T(8,128)(2,1)S(1)}, bf16[128,256]{1,0:T(8,128)(2,1)}, u32[]{:S(2)}) copy-start(bf16[128,256]{1,0:T(8,128)(2,1)} %param.14) | copy-start | bytes 196612
  25.9 29.8 %copy-start.25 = (bf16[128,256]{1,0:T(8,128)(2,1)S(1)}, bf16[128,256]{1,0:T(8,128)(2,1)}, u32[]{:S(2)}) copy-start(bf16[128,256]{1,0:T(8,128)(2,1)} %param.13) | copy-start | bytes 196612
  25.9 50.2 %copy-start.4 = (bf16[128,2048]{1,0:T(8,128)(2,1)S(1)}, bf16[128,2048]{1,0:T(8,128)(2,1)}, u32[]{:S(2)}) copy-start(bf16[128,2048]{1,0:T(8,128)(2,1)} %q_ref.1) | copy-start | bytes 1572868
  25.9 27.8 %all-to-all-start = ((bf16[16,8,3072]{2,1,0:T(8,128)(2,1)}), bf16[16,8,3072]{2,1,0:T(8,128)(2,1)S(1)}, u32[]{:S(2)}, u32[]{:S(2)}) async-start(bf16[16,8,3072]{2,1,0:T(8,128)(2,1)} %bitcast.6), calls=%async_computation | async-start | bytes 1572864 | tf_op jit(solution)/shard_map/all_to_all | solution.py:326
  34.8 120.4 %all-gather.5.cloned.1.call-start = ((), (), s32[]{:S(2)}) async-start(), calls=%async_computation.3 | async-start | bytes 3538944 | tf_op jit(solution)/shard_map/all_gather | solution.py:325
  35.0 9.4 %collective-permute-start.4 = (bf16[64,1536]{1,0:T(8,128)(2,1)S(1)}, bf16[64,1536]{1,0:T(8,128)(2,1)S(1)}, u32[]{:S(2)}, u32[]{:S(2)}) collective-permute-start(bf16[64,1536]{1,0:T(8,128)(2,1)S(1)} %pad.22), channel_id=1, source_target_pairs={{0,2},{2,0},{1,3},{3,1},{4,6},{6,4},{5,7},{7,5},{8,10},{10,8},{9,1... | collective-permute-start | bytes 589832 | tf_op jit(solution)/shard_map/ppermute | solution.py:289
  53.8 32.7 %collective-permute-start.3 = (bf16[128,768]{1,0:T(8,128)(2,1)S(1)}, bf16[128,768]{1,0:T(8,128)(2,1)S(1)}, u32[]{:S(2)}, u32[]{:S(2)}) collective-permute-start(bf16[128,768]{1,0:T(8,128)(2,1)S(1)} %get-tuple-element.79), channel_id=1, source_target_pairs={{0,1},{1,0},{2,3},{3,2},{4,5},{5,4},{6,7},{7,6},{8,9},{9,8},{10,11... | collective-permute-start | bytes 589832 | tf_op jit(solution)/shard_map/ppermute | solution.py:328
  55.8 18.8 %collective-permute-start.1 = (bf16[128,640]{1,0:T(8,128)(2,1)S(1)}, bf16[128,640]{1,0:T(8,128)(2,1)S(1)}, u32[]{:S(2)}, u32[]{:S(2)}) collective-permute-start(bf16[128,640]{1,0:T(8,128)(2,1)S(1)} %fusion.9.own_ref), channel_id=1, source_target_pairs={{0,2},{1,3},{2,4},{3,5},{4,6},{5,7},{6,8},{7,9},{8,10},{9,11},{10,... | collective-permute-start | bytes 491528 | tf_op jit(solution)/shard_map/ppermute | solution.py:298
  60.3 15.9 %collective-permute-start.2 = (bf16[128,640]{1,0:T(8,128)(2,1)S(1)}, bf16[128,640]{1,0:T(8,128)(2,1)S(1)}, u32[]{:S(2)}, u32[]{:S(2)}) collective-permute-start(bf16[128,640]{1,0:T(8,128)(2,1)S(1)} %fusion.9.own_ref), channel_id=1, source_target_pairs={{0,1},{1,2},{2,3},{3,4},{4,5},{5,6},{6,7},{7,8},{8,9},{9,10},{10,1... | collective-permute-start | bytes 491528 | tf_op jit(solution)/shard_map/ppermute | solution.py:298
  83.4 1.7 copy-start.1
  85.7 0.7 copy-start.15
  86.4 0.7 copy-start.11
  87.1 6.6 %collective-permute-start.5 = (bf16[768,1536]{1,0:T(8,128)(2,1)}, bf16[768,1536]{1,0:T(8,128)(2,1)S(1)}, u32[]{:S(2)}, u32[]{:S(2)}) collective-permute-start(bf16[768,1536]{1,0:T(8,128)(2,1)} %all-gather.3.cloned.1.call-done.wm_ref), channel_id=1, source_target_pairs={{0,1},{1,0},{2,3},{3,2},{4,5},{5,4},{6,7},{7,6},{8,9},{9,8},{10,11... | collective-permute-start | bytes 7077896 | tf_op jit(solution)/shard_map/ppermute | solution.py:348
  93.8 1.7 copy-start.3
  98.0 0.8 copy-start.5
  98.7 3.6 %collective-permute-start.6 = (bf16[128,1536]{1,0:T(8,128)(2,1)S(1)}, bf16[128,1536]{1,0:T(8,128)(2,1)S(1)}, u32[]{:S(2)}, u32[]{:S(2)}) collective-permute-start(bf16[128,1536]{1,0:T(8,128)(2,1)S(1)} %get-tuple-element.45.pg_ref), channel_id=1, source_target_pairs={{0,1},{1,0},{2,3},{3,2},{4,5},{5,4},{6,7},{7,6},{8,9},{9,8},{10,11... | collective-permute-start | bytes 1179656 | tf_op jit(solution)/shard_map/ppermute | solution.py:360
  102.3 0.7 copy-start.6
  103.1 1.0 copy-start.7
  104.1 0.9 copy-start.12
  106.6 13.6 %collective-permute-start.7 = (bf16[48,1536]{1,0:T(8,128)(2,1)}, bf16[48,1536]{1,0:T(8,128)(2,1)}, u32[]{:S(2)}, u32[]{:S(2)}) collective-permute-start(bf16[48,1536]{1,0:T(8,128)(2,1)} %get-tuple-element.77), channel_id=1, source_target_pairs={{0,4},{4,8},{8,12},{12,16},{16,20},{20,24},{24,28},{28,0},{1,5},{5... | collective-permute-start | bytes 442376 | tf_op jit(solution)/shard_map/ppermute | solution.py:263
  108.5 12.0 %collective-permute-start.8 = (bf16[48,1536]{1,0:T(8,128)(2,1)}, bf16[48,1536]{1,0:T(8,128)(2,1)}, u32[]{:S(2)}, u32[]{:S(2)}) collective-permute-start(bf16[48,1536]{1,0:T(8,128)(2,1)} %get-tuple-element.76), channel_id=1, source_target_pairs={{0,28},{4,0},{8,4},{12,8},{16,12},{20,16},{24,20},{28,24},{1,29},{... | collective-permute-start | bytes 442376 | tf_op jit(solution)/shard_map/ppermute | solution.py:264
  113.6 27.8 %all-to-all-start.1 = ((bf16[16,8,1664]{2,1,0:T(8,128)(2,1)}), bf16[16,8,1664]{2,1,0:T(8,128)(2,1)S(1)}, u32[]{:S(2)}, u32[]{:S(2)}) async-start(bf16[16,8,1664]{2,1,0:T(8,128)(2,1)} %bitcast.58), calls=%async_computation.1 | async-start | bytes 851968 | tf_op jit(solution)/shard_map/all_to_all | solution.py:357
  120.1 43.0 %copy-start.18 = (bf16[128,128]{1,0:T(8,128)(2,1)S(1)}, bf16[128,128]{1,0:T(8,128)(2,1)}, u32[]{:S(2)}) copy-start(bf16[128,128]{1,0:T(8,128)(2,1)} %copy-done.17) | copy-start | bytes 98308
  120.1 43.0 %copy-start.20 = (s32[128,4]{0,1:T(4,128)S(1)}, s32[128,4]{0,1:T(4,128)}, u32[]{:S(2)}) copy-start(s32[128,4]{0,1:T(4,128)} %param.19) | copy-start | bytes 6148
  122.3 11.8 %collective-permute-start.10 = (bf16[96,1536]{1,0:T(8,128)(2,1)}, bf16[96,1536]{1,0:T(8,128)(2,1)}, u32[]{:S(2)}, u32[]{:S(2)}) collective-permute-start(bf16[96,1536]{1,0:T(8,128)(2,1)} %get-tuple-element.49), channel_id=1, source_target_pairs={{0,28},{4,0},{8,4},{12,8},{16,12},{20,16},{24,20},{28,24},{1,29},{... | collective-permute-start | bytes 884744 | tf_op jit(solution)/shard_map/ppermute | solution.py:274
  127.9 11.5 %collective-permute-start.9 = (bf16[96,1536]{1,0:T(8,128)(2,1)}, bf16[96,1536]{1,0:T(8,128)(2,1)}, u32[]{:S(2)}, u32[]{:S(2)}) collective-permute-start(bf16[96,1536]{1,0:T(8,128)(2,1)} %get-tuple-element.48), channel_id=1, source_target_pairs={{0,4},{4,8},{8,12},{12,16},{16,20},{20,24},{24,28},{28,0},{1,5},{5... | collective-permute-start | bytes 884744 | tf_op jit(solution)/shard_map/ppermute | solution.py:273
  141.4 10.6 %collective-permute-start.11 = (bf16[96,1536]{1,0:T(8,128)(2,1)}, bf16[96,1536]{1,0:T(8,128)(2,1)}, u32[]{:S(2)}, u32[]{:S(2)}) collective-permute-start(bf16[96,1536]{1,0:T(8,128)(2,1)} %get-tuple-element.52), channel_id=1, source_target_pairs={{0,4},{4,8},{8,12},{12,16},{16,20},{20,24},{24,28},{28,0},{1,5},{5... | collective-permute-start | bytes 884744 | tf_op jit(solution)/shard_map/ppermute | solution.py:273
  143.4 9.8 %collective-permute-start.12 = (bf16[96,1536]{1,0:T(8,128)(2,1)}, bf16[96,1536]{1,0:T(8,128)(2,1)}, u32[]{:S(2)}, u32[]{:S(2)}) collective-permute-start(bf16[96,1536]{1,0:T(8,128)(2,1)} %get-tuple-element.53), channel_id=1, source_target_pairs={{0,28},{4,0},{8,4},{12,8},{16,12},{20,16},{24,20},{28,24},{1,29},{... | collective-permute-start | bytes 884744 | tf_op jit(solution)/shard_map/ppermute | solution.py:274
  155.2 7.9 %collective-permute-start.13 = (bf16[1024,1536]{1,0:T(8,128)(2,1)}, bf16[1024,1536]{1,0:T(8,128)(2,1)}, u32[]{:S(2)}, u32[]{:S(2)}) collective-permute-start(bf16[1024,1536]{1,0:T(8,128)(2,1)} %all-gather.5.cloned.1.call-done.om_any), channel_id=1, source_target_pairs={{0,1},{1,0},{2,3},{3,2},{4,5},{5,4},{6,7},{7,6},{8,9},{9,8},{10,11... | collective-permute-start | bytes 9437192 | tf_op jit(solution)/shard_map/ppermute | solution.py:366
  163.1 1.9 copy-start
  165.0 1.9 copy-start.2
  166.9 1.0 copy-start.10
  167.9 0.9 copy-start.16
  168.8 17.9 %copy-start.22 = (bf16[96,1536]{1,0:T(8,128)(2,1)S(1)}, bf16[96,1536]{1,0:T(8,128)(2,1)}, u32[]{:S(2)}) copy-start(bf16[96,1536]{1,0:T(8,128)(2,1)} %get-tuple-element.66) | copy-start | bytes 884740
  168.8 19.8 %copy-start.21 = (bf16[96,1536]{1,0:T(8,128)(2,1)S(1)}, bf16[96,1536]{1,0:T(8,128)(2,1)}, u32[]{:S(2)}) copy-start(bf16[96,1536]{1,0:T(8,128)(2,1)} %get-tuple-element.67) | copy-start | bytes 884740
  168.8 30.1 %copy-start.14 = (bf16[256,384]{1,0:T(8,128)(2,1)S(1)}, bf16[256,384]{1,0:T(8,128)(2,1)}, u32[]{:S(2)}) copy-start(bf16[256,384]{1,0:T(8,128)(2,1)} %copy-done.13) | copy-start | bytes 589828
  181.4 19.0 %collective-permute-start.14 = (bf16[128,512]{1,0:T(8,128)(2,1)S(1)}, bf16[128,512]{1,0:T(8,128)(2,1)S(1)}, u32[]{:S(2)}, u32[]{:S(2)}) collective-permute-start(bf16[128,512]{1,0:T(8,128)(2,1)S(1)} %get-tuple-element.62), channel_id=1, source_target_pairs={{1,0},{2,1},{3,2},{4,3},{5,4},{6,5},{7,6},{8,7},{9,8},{10,9},{11,1... | collective-permute-start | bytes 393224 | tf_op jit(solution)/shard_map/ppermute | solution.py:298
  186.7 15.5 %collective-permute-start.16 = (bf16[96,1536]{1,0:T(8,128)(2,1)S(1)}, bf16[96,1536]{1,0:T(8,128)(2,1)S(1)}, u32[]{:S(2)}, u32[]{:S(2)}) collective-permute-start(bf16[96,1536]{1,0:T(8,128)(2,1)S(1)} %copy-done.22), channel_id=1, source_target_pairs={{0,4},{4,8},{8,12},{12,16},{16,20},{20,24},{24,28},{28,0},{1,5},{5... | collective-permute-start | bytes 884744 | tf_op jit(solution)/shard_map/ppermute | solution.py:283
  188.7 13.6 %collective-permute-start.17 = (bf16[96,1536]{1,0:T(8,128)(2,1)S(1)}, bf16[96,1536]{1,0:T(8,128)(2,1)S(1)}, u32[]{:S(2)}, u32[]{:S(2)}) collective-permute-start(bf16[96,1536]{1,0:T(8,128)(2,1)S(1)} %copy-done.21), channel_id=1, source_target_pairs={{0,28},{4,0},{8,4},{12,8},{16,12},{20,16},{24,20},{28,24},{1,29},{... | collective-permute-start | bytes 884744 | tf_op jit(solution)/shard_map/ppermute | solution.py:284
  193.8 8.4 %collective-permute-start.15 = (bf16[128,512]{1,0:T(8,128)(2,1)S(1)}, bf16[128,512]{1,0:T(8,128)(2,1)S(1)}, u32[]{:S(2)}, u32[]{:S(2)}) collective-permute-start(bf16[128,512]{1,0:T(8,128)(2,1)S(1)} %get-tuple-element.63), channel_id=1, source_target_pairs={{2,0},{3,1},{4,2},{5,3},{6,4},{7,5},{8,6},{9,7},{10,8},{11,9},{12,... | collective-permute-start | bytes 393224 | tf_op jit(solution)/shard_map/ppermute | solution.py:298
  202.4 8.5 %collective-permute-start.18 = (bf16[48,1536]{1,0:T(8,128)(2,1)S(1)}, bf16[48,1536]{1,0:T(8,128)(2,1)S(1)}, u32[]{:S(2)}, u32[]{:S(2)}) collective-permute-start(bf16[48,1536]{1,0:T(8,128)(2,1)S(1)} %dynamic-slice_convert_fusion), channel_id=1, source_target_pairs={{0,2},{2,0},{1,3},{3,1},{4,6},{6,4},{5,7},{7,5},{8,10},{10,8},{9,1... | collective-permute-start | bytes 442376 | tf_op jit(solution)/shard_map/ppermute | solution.py:401
  (2 other events, 1.3 us)
Sparse Core Ops, SparseCore 0:
  19.0 49.5 all-gather.2
  70.8 52.3 all-gather.4

commit v3 on v2

--- a/solution.py
+++ b/solution.py
@@ -34,39 +34,38 @@
     return lax.dot_general(a, b, (dims, ((), ())), preferred_element_type=F32)
 
 
-def spec_vmem():
-    return pl.BlockSpec(memory_space=pltpu.VMEM)
-
-
-def spec_smem():
-    return pl.BlockSpec(memory_space=pltpu.SMEM)
+SPACES = {"s": pltpu.SMEM, "v": pltpu.VMEM, "h": pltpu.HBM}
 
 
 def out(shape, dtype=BF):
     return jax.ShapeDtypeStruct(shape, dtype)
 
 
-def call(kernel, outs, scratch, weight_us, n_smem, n_vmem, n_any=0):
+def call(kernel, ins, outs, out_spaces, scratch, weight_us):
     return pl.pallas_call(
         kernel,
         out_shape=outs,
-        in_specs=[spec_smem()] * n_smem
-        + [spec_vmem()] * n_vmem
-        + [pl.BlockSpec(memory_space=pl.ANY)] * n_any,
-        out_specs=[spec_vmem()] * len(outs),
+        in_specs=[pl.BlockSpec(memory_space=SPACES[k]) for k in ins],
+        out_specs=[pl.BlockSpec(memory_space=SPACES[k]) for k in out_spaces],
         scratch_shapes=scratch,
-        compiler_params=pltpu.CompilerParams(vmem_limit_bytes=26 * 1024 * 1024),
+        compiler_params=pltpu.CompilerParams(vmem_limit_bytes=60 * 1024 * 1024),
         cost_estimate=pl.CostEstimate(
             flops=0, bytes_accessed=int(weight_us * 3690000), transcendentals=0
         ),
     )
 
 
+def copies_of(pairs, sems):
+    return [pltpu.make_async_copy(a, b, sems.at[i]) for i, (a, b) in enumerate(pairs)]
+
+
 def order(value, *ties):
     return lax.optimization_barrier((value, *ties))[0]
 
 
-def dispatch_kernel(picked_ref, held_ref, gate_ref, place_ref, x_ref, g_ref, out_ref, sent_ref):
+def dispatch_kernel(
+    picked_ref, held_ref, gate_ref, place_ref, x_ref, g_ref, out_ref, sent_any, sent_ref, sems
+):
     held = held_ref[...]
     chosen = [picked_ref[s : s + 1, :] == held for s in range(4)]
     routed = chosen[0] | chosen[1] | chosen[2] | chosen[3]
@@ -80,6 +79,8 @@
     sent = routed & (rank == slot.astype(F32))
     sent_bf = jnp.where(sent, 1.0, 0.0).astype(BF)
     sent_ref[...] = sent_bf
+    copy = pltpu.make_async_copy(sent_ref, sent_any, sems.at[0])
+    copy.start()
     gate = jnp.zeros((ROWS, TOK), F32)
     for s in range(4):
         gate = gate + jnp.where(chosen[s] & sent, gate_ref[s : s + 1, :], 0.0)
@@ -93,9 +94,13 @@
     out_ref[:, DP:] = jnp.concatenate(
         [grads, jnp.broadcast_to(gate, (ROWS, SEND - DP - F)).astype(BF)], axis=1
     )
-
-
-def shares_kernel(q_ref, far_ref, near_ref, own_ref, label_ref, shares_ref, qt_ref, kt_ref, v_ref, kv_s, bias_s):
+    copy.wait()
+
+
+def shares_kernel(
+    q_ref, far_ref, near_ref, own_ref, label_ref, shares_any, qt_any, kt_any, v_any,
+    kv_s, bias_s, shares_ref, qt_ref, kt_ref, v_ref, sems,
+):
     for part, ref in enumerate((far_ref, near_ref, own_ref)):
         kv_s[part * TOK : (part + 1) * TOK, :] = ref[...]
     marks = kv_s[:, 2 * KV :].astype(F32)
@@ -110,6 +115,7 @@
         kt_ref[t * 128 : (t + 1) * 128, :] = jnp.transpose(
             kv_s[:, t * 128 : (t + 1) * 128].astype(F32)
         ).astype(BF)
+    copies = []
     for g in range(KV_HEADS):
         k_one = kv_s[:, g * HD : (g + 1) * HD]
 
@@ -125,9 +131,29 @@
             return carry
 
         lax.fori_loop(0, 4, pair, 0)
-
-
-def expert_kernel(got_ref, wm_ref, wo_ref, back_ref, pg_ref, pre_ref):
+        columns = slice(g * 8 * TOK, (g + 1) * 8 * TOK)
+        copies.append(
+            pltpu.make_async_copy(
+                shares_ref.at[:, columns], shares_any.at[:, columns], sems.at[g]
+            )
+        )
+        copies[-1].start()
+    pairs = ((qt_ref, qt_any), (kt_ref, kt_any), (v_ref, v_any))
+    for i, (source, target) in enumerate(pairs):
+        copies.append(pltpu.make_async_copy(source, target, sems.at[4 + i]))
+        copies[-1].start()
+    for copy in copies:
+        copy.wait()
+
+
+def expert_kernel(
+    got_ref, wm_any, wo_any, back_any, pg_any, wm_ref, wo_ref, back_ref, pg_ref, pre_ref, sems
+):
+    loads = copies_of(((wm_any, wm_ref), (wo_any, wo_ref)), sems)
+    for copy in loads:
+        copy.start()
+    for copy in loads:
+        copy.wait()
     step = 512
     for lo in range(0, DP, step):
         at = slice(lo, lo + step)
@@ -143,6 +169,8 @@
         total = total + jnp.sum(grad * (pre * sig), axis=1, keepdims=True)
         slope = sig * (1.0 + pre * (1.0 - sig))
         pg_ref[:, lo : lo + step] = (gate * grad * slope).astype(BF)
+    store = pltpu.make_async_copy(pg_ref, pg_any, sems.at[2])
+    store.start()
     pg = pg_ref[...]
     for c in range(HALF // 256):
         r = slice(c * 256, (c + 1) * 256)
@@ -151,9 +179,21 @@
             pg, wo_ref[r, :], ((1,), (1,))
         ).astype(BF)
     back_ref[:, DP:] = jnp.broadcast_to(total, (ROWS, BACK - DP)).astype(BF)
-
-
-def map_kernel(x_ref, x2_ref, pg_ref, pg2_ref, out_ref):
+    returned = pltpu.make_async_copy(back_ref, back_any, sems.at[3])
+    returned.start()
+    store.wait()
+    returned.wait()
+
+
+def map_kernel(
+    x_any, x2_any, pg_any, pg2_any, out_ref, x_ref, x2_ref, pg_ref, pg2_ref, sems
+):
+    pairs = ((x_any, x_ref), (x2_any, x2_ref), (pg_any, pg_ref), (pg2_any, pg2_ref))
+    loads = copies_of(pairs, sems)
+    for copy in loads:
+        copy.start()
+    for copy in loads:
+        copy.wait()
     pg = jnp.concatenate([pg_ref[...], pg2_ref[...]], axis=0)
     for c in range(HALF // 256):
         at = slice(c * 256, (c + 1) * 256)
@@ -162,21 +202,20 @@
 
 
 def late_kernel(
-    core_ref, picked_ref, held_ref, sent_ref, place_ref, back_ref, v_ref,
-    skip_any, om_any, oo_any, qt_any, shares_any,
+    at_ref, picked_ref, held_ref, place_ref, back_ref,
+    sent_any, v_any, skip_any, om_any, oo_any, qt_any, shares_any,
     src_ref, gate_ref, sg_ref, farg_ref, nearg_ref, owng_ref,
-    hidden_s, cot_s, acck_s, accv_s, skip_ref, om_ref, oo_ref, qt_ref, shares_ref, sems,
+    hidden_s, cot_s, acck_s, accv_s,
+    sent_ref, v_ref, skip_ref, om_ref, oo_ref, qt_ref, shares_ref, sems,
 ):
     pairs = (
-        (skip_any, skip_ref), (om_any, om_ref), (oo_any, oo_ref),
-        (qt_any, qt_ref), (shares_any, shares_ref),
-    )
-    copies = [
-        pltpu.make_async_copy(source, target, sems.at[i])
-        for i, (source, target) in enumerate(pairs)
-    ]
+        (sent_any, sent_ref), (skip_any, skip_ref), (om_any, om_ref), (oo_any, oo_ref),
+        (v_any, v_ref), (qt_any, qt_ref), (shares_any, shares_ref),
+    )
+    copies = copies_of(pairs, sems)
     for copy in copies:
         copy.start()
+    copies[0].wait()
     sent_bf = sent_ref[...]
     sent = sent_bf.astype(F32) > 0.5
     held = held_ref[...]
@@ -191,24 +230,25 @@
         pick = jnp.where(feature == place_ref[:, c * 256 : (c + 1) * 256], 1.0, 0.0).astype(BF)
         total = total + dot(pick, src[:, c * 256 : (c + 1) * 256], ((1,), (1,)))
     src_ref[...] = total.astype(BF)
-    copies[0].wait()
+    copies[1].wait()
     hidden_s[:D, :] = (skip_ref[...].astype(F32) + total).astype(BF)
     hidden_s[D:, :] = jnp.zeros((DP - D, TOK), BF)
 
-    core = core_ref[0]
+    core, xh = at_ref[0], at_ref[1]
     for ref, place, copy in (
-        (om_ref, core * HD, copies[1]),
-        (oo_ref, HD - core * HD, copies[2]),
+        (om_ref, core * HD, copies[2]),
+        (oo_ref, HD - core * HD, copies[3]),
     ):
         copy.wait()
         for c in range(4):
             block = dot(ref[c * 256 : (c + 1) * 256, :], hidden_s[...], ((1,), (0,))).astype(BF)
             for j in range(4):
-                at = pl.multiple_of((c * 4 + j) * 128 + place, HD)
+                across = xh if j % 2 == 0 else 1 - xh
+                at = pl.multiple_of((c * 2 + j // 2) * 256 + across * 128 + place, HD)
                 cot_s[pl.ds(at, HD), :] = block[j * HD : (j + 1) * HD]
 
-    copies[3].wait()
-    copies[4].wait()
+    for copy in copies[4:]:
+        copy.wait()
     for t in range(2):
         sums = []
         for g in (2 * t, 2 * t + 1):
@@ -265,17 +305,19 @@
     right, left = lax.optimization_barrier((right, left))
     right = jnp.pad(right, ((0, half), (0, 0)))
     left = jnp.pad(left, ((half, 0), (0, 0)))
+    marks = []
     for k in (3, 2):
         right = (chunk(k).astype(F32) + right.astype(F32)).astype(BF)
         left = (chunk(8 - k).astype(F32) + left.astype(F32)).astype(BF)
-        ties = (returned,) if k == 2 else ()
+        ties = (returned,) if k == 3 else ()
         right, left = lax.optimization_barrier((right, left, *ties))[:2]
+        marks = (right, left)
         right = lax.ppermute(right, "z", RIGHT)
         left = lax.ppermute(left, "z", LEFT)
         right, left = lax.optimization_barrier((right, left))
     right = (chunk(1).astype(F32) + right.astype(F32)).astype(BF)
     left = (chunk(7).astype(F32) + left.astype(F32)).astype(BF)
-    return right, left, chunk(0)
+    return right, left, chunk(0), marks
 
 
 def reduce_end(right, left, mine, late):
@@ -286,11 +328,7 @@
 
 
 def both_xh(piece):
-    other = lax.ppermute(piece, "xh", SWAP)
-    lower = lax.axis_index("xh") == 0
-    return jnp.concatenate(
-        [jnp.where(lower, piece, other), jnp.where(lower, other, piece)], axis=0
-    )
+    return jnp.concatenate([piece, lax.ppermute(piece, "xh", SWAP)], axis=0)
 
 
 def shift_blocks(value, steps):
@@ -300,6 +338,7 @@
 
 def shards(q, keys, values, label, skip, x, g, picked, mix, retained, weights, out_map):
     core = lax.axis_index("core")
+    xh = lax.axis_index("xh")
     w_pad = jnp.pad(weights[0], ((0, SEG - SHARD), (0, DP - F)))
     o_pad = jnp.pad(out_map, ((0, 0), (0, DP - D)))
     w_pair = both_xh(w_pad)
@@ -316,94 +355,122 @@
     half = spot // HALF
     rest = spot % HALF
     within = rest % SEG
-    owner = (rest // SEG) * 2 + (half ^ core)
+    pair = rest // SEG
+    owner = (pair // 2) * 4 + ((pair % 2) ^ xh) * 2 + (half ^ core)
     place = jnp.where(within < SHARD, owner * SHARD + within, -1)[None, :]
-    send, sent = call(dispatch_kernel, [out((ROWS, SEND)), out((ROWS, TOK))], [], 2, 0, 6)(
-        picked_t, held, mix.astype(F32).T, place, x.T, g.T
-    )
-    o_pair = both_xh(order(o_pad, send))
-    o_mine = lax.all_gather(o_pair, "z", axis=0, tiled=True)
+    dma = pltpu.SemaphoreType.DMA
+    send, sent = call(
+        dispatch_kernel,
+        "vvvvvv",
+        [out((ROWS, SEND)), out((ROWS, TOK))],
+        "vh",
+        [pltpu.VMEM((ROWS, TOK), BF), dma((1,))],
+        2,
+    )(picked_t, held, mix.astype(F32).T, place, x.T, g.T)
     got = lax.all_to_all(send.reshape(EXPERTS, CAPP, SEND), CTX, 0, 0, tiled=True)
-    got = got.reshape(ROWS, SEND)
-    x_swapped = lax.ppermute(got[:, HALF:DP], "core", SWAP)
     own = order(own, send)
     near = shift_blocks(own, 1)
     far = shift_blocks(own, 2)
-
+    shares_shape, qt_shape = (3 * TOK, HEADS * TOK), (HEADS * HD, TOK)
+    kt_shape, v_shape = (KV, 3 * TOK), (3 * TOK, KV)
     shares, q_t, k_t, v_win = call(
         shares_kernel,
+        "vvvvv",
+        [out(shares_shape), out(qt_shape), out(kt_shape), out(v_shape)],
+        "hhhh",
         [
-            out((3 * TOK, HEADS * TOK)),
-            out((HEADS * HD, TOK)),
-            out((KV, 3 * TOK)),
-            out((3 * TOK, KV)),
+            pltpu.VMEM((3 * TOK, WIDE), BF),
+            pltpu.VMEM((3 * TOK, 2 * TOK), F32),
+            pltpu.VMEM(shares_shape, BF),
+            pltpu.VMEM(qt_shape, BF),
+            pltpu.VMEM(kt_shape, BF),
+            pltpu.VMEM(v_shape, BF),
+            dma((7,)),
         ],
-        [pltpu.VMEM((3 * TOK, WIDE), BF), pltpu.VMEM((3 * TOK, 2 * TOK), F32)],
         8,
-        0,
-        5,
     )(q, far, near, own, plus.astype(F32)[None, :])
 
-    w_mine = order(w_mine, v_win, x_swapped, o_pair)
+    got = order(got, v_win).reshape(ROWS, SEND)
+    x_swapped = lax.ppermute(got[:, HALF:DP], "core", SWAP)
+    o_pair = both_xh(order(o_pad, v_win))
+    o_mine = lax.all_gather(o_pair, "z", axis=0, tiled=True)
+    w_mine = order(w_mine, x_swapped, o_pair)
     w_other = lax.ppermute(w_mine, "core", SWAP)
     back, pg = call(
         expert_kernel,
+        "vhh",
         [out((ROWS, BACK)), out((ROWS, DP))],
-        [pltpu.VMEM((ROWS, DP), F32)],
-        3,
-        0,
+        "hh",
+        [
+            pltpu.VMEM((HALF, DP), BF),
+            pltpu.VMEM((HALF, DP), BF),
+            pltpu.VMEM((ROWS, BACK), BF),
+            pltpu.VMEM((ROWS, DP), BF),
+            pltpu.VMEM((ROWS, DP), F32),
+            dma((4,)),
+        ],
         3,
     )(got, w_mine, w_other)
     returned = lax.all_to_all(back.reshape(EXPERTS, CAPP, BACK), CTX, 0, 0, tiled=True)
     returned = returned.reshape(ROWS, BACK)
 
     pg_swapped = lax.ppermute(pg, "core", SWAP)
-    partial = call(map_kernel, [out((HALF, DP))], [], 2, 0, 4)(
-        got[:, :HALF], x_swapped, pg, pg_swapped
-    )[0]
-    right, left, mine = reduce_start(partial.reshape(8, 2 * SEG, DP), returned)
-    o_mine = order(o_mine, right, left)
+    partial = call(
+        map_kernel,
+        "hhhh",
+        [out((HALF, DP))],
+        "v",
+        [
+            pltpu.VMEM((ROWS, HALF), BF),
+            pltpu.VMEM((ROWS, HALF), BF),
+            pltpu.VMEM((ROWS, DP), BF),
+            pltpu.VMEM((ROWS, DP), BF),
+            dma((4,)),
+        ],
+        2,
+    )(got[:, :HALF], x_swapped, pg, pg_swapped)[0]
+    right, left, mine, marks = reduce_start(partial.reshape(8, 2 * SEG, DP), returned)
+    o_mine = order(o_mine, *marks)
     o_other = lax.ppermute(o_mine, "core", SWAP)
     src_t, gate_t, sg, far_g, near_g, own_g = call(
         late_kernel,
+        "svvvvhhhhhhh",
         [
             out((D, TOK)),
             out((4, TOK), F32),
-            out((3 * TOK, HEADS * TOK)),
+            out(shares_shape),
             out((TOK, 2 * KV)),
             out((TOK, 2 * KV)),
             out((TOK, 2 * KV), F32),
         ],
+        "vvvvvv",
         [
             pltpu.VMEM((DP, TOK), BF),
             pltpu.VMEM((HEADS * HD, TOK), BF),
             pltpu.VMEM((3 * TOK, HD), F32),
             pltpu.VMEM((3 * TOK, HD), F32),
+            pltpu.VMEM((ROWS, TOK), BF),
+            pltpu.VMEM(v_shape, BF),
             pltpu.VMEM((D, TOK), BF),
             pltpu.VMEM((16 * HD, DP), BF),
             pltpu.VMEM((16 * HD, DP), BF),
-            pltpu.VMEM((HEADS * HD, TOK), BF),
-            pltpu.VMEM((3 * TOK, HEADS * TOK), BF),
-            pltpu.SemaphoreType.DMA((5,)),
+            pltpu.VMEM(qt_shape, BF),
+            pltpu.VMEM(shares_shape, BF),
+            dma((7,)),
         ],
         8,
-        1,
-        6,
-        5,
     )(
-        core[None].astype(jnp.int32), picked_t, held, sent, place, returned, v_win,
-        skip.T, o_mine, o_other, q_t, shares,
+        jnp.stack([core, xh]).astype(jnp.int32), picked_t, held, place, returned,
+        sent, v_win, skip.T, o_mine, o_other, q_t, shares,
     )
     merged = reduce_end(right, left, mine, near_g)
-    xh = lax.axis_index("xh")
-    away = lax.dynamic_slice_in_dim(merged, (1 - xh) * SEG, SEG, 0).astype(BF)
-    kept = lax.dynamic_slice_in_dim(merged, xh * SEG, SEG, 0)
-    map_grad = (kept + lax.ppermute(away, "xh", SWAP).astype(F32)).astype(BF)
+    away = merged[SEG:].astype(BF)
+    map_grad = (merged[:SEG] + lax.ppermute(away, "xh", SWAP).astype(F32)).astype(BF)
     map_grad = map_grad[None, :SHARD, :F]
 
     got_near = shift_blocks(near_g, -1)
     got_far = shift_blocks(far_g, -2)
-    q_grad = call(query_kernel, [out((TOK, HEADS * HD))], [], 3, 0, 2)(sg, k_t)[0]
+    q_grad = call(query_kernel, "vv", [out((TOK, HEADS * HD))], "v", [], 3)(sg, k_t)[0]
     kv_grad = (own_g + got_near.astype(F32) + got_far.astype(F32)).astype(BF)
     return (
         q_grad,

time: 220 us -> 214 us (0.973)
  the two profiles are of different devices: /device:TPU:8 before, /device:TPU:40 now
where the time goes in v3:
time: 214 us; the launch traced here: 213 us
  starting transfers between devices  83.7 us (39%)
  waiting for transfers between devices  49.3 us (23%)
  Pallas kernels  42.6 us (20%)
  between operations  14.5 us (7%)
  other arithmetic  12.9 us (6%)
  local copies, waits for them, and re-layouts  10.3 us (5%)
    ppermute x4, starting transfers between devices, shift_blocks(): lax.ppermute(value, ALL, [(i, i + steps) for i in range(first, last)])  18.4 us
    pallas_call x1, Pallas kernels, shards(): call(late_kernel, 'svvvvhhhhhhh', [out((D, TOK)), out((4, TOK), F32), out...  15.6 us
    ppermute x2, waiting for transfers between devices, both_xh(): return jnp.concatenate([piece, lax.ppermute(piece, 'xh', SWAP)], axis=0)  13.1 us
    ppermute x2, starting transfers between devices, reduce_start(): left = lax.ppermute(left, 'z', LEFT)  10.6 us
    pallas_call x1, Pallas kernels, shards(): call(shares_kernel, 'vvvvv', [out(shares_shape), out(qt_shape), out(kt_sh...  9.65 us
    ppermute x2, waiting for transfers between devices, reduce_start(): right = lax.ppermute(right, 'z', RIGHT)  9.59 us
    ppermute x1, starting transfers between devices, reduce_start(): left = lax.ppermute(chunk(4)[half:], 'z', LEFT)  8.87 us
    all_to_all x1, starting transfers between devices, shards(): lax.all_to_all(back.reshape(EXPERTS, CAPP, BACK), CTX, 0, 0, tiled=True)  7.54 us
  transfers between devices with their start and end apart: 23, of which 14 were waited for; matrix products, arithmetic and copies ran while one was open for 7% of the time, Pallas kernels for 13%

profile of v3, /device:TPU:40, one launch (start us, length us, event | category | flops | bytes accessed | tf_op | source)
XLA Modules:
  0.0 213.3 jit_solution(11760917610598703073)
XLA Ops:
  8.2 4.9 %collective-permute-start = (bf16[48,1536]{1,0:T(8,128)(2,1)S(1)}, bf16[48,1536]{1,0:T(8,128)(2,1)S(1)}, u32[]{:S(2)}, u32[]{:S(2)}) collective-permute-start(bf16[48,1536]{1,0:T(8,128)(2,1)S(1)} %pad.20), channel_id=1, source_target_pairs={{0,2},{2,0},{1,3},{3,1},{4,6},{6,4},{5,7},{7,5},{8,10},{10,8},{9,1... | collective-permute-start | bytes 442376 | tf_op jit(solution)/shard_map/ppermute | solution.py:331
  13.1 4.0 %collective-permute-done = bf16[48,1536]{1,0:T(8,128)(2,1)S(1)} collective-permute-done((bf16[48,1536]{1,0:T(8,128)(2,1)S(1)}, bf16[48,1536]{1,0:T(8,128)(2,1)S(1)}, u32[]{:S(2)}, u32[]{:S(2)}) %collective-permute-start) | collective-permute-done | bytes 147488 | tf_op jit(solution)/shard_map/ppermute | solution.py:331
  17.9 1.1 convert_bitcast_fusion.3
  21.6 1.3 convert_bitcast_fusion.gate_ref
  23.6 3.3 %shard_map.163 = (bf16[128,3072]{1,0:T(8,128)(2,1)}, bf16[128,128]{1,0:T(8,128)(2,1)}) custom-call(s32[4,128]{1,0:T(4,128)} %bitcast.65, s32[128,1]{1,0:T(8,128)} %broadcast_in_dim_reshape.4.held_ref, f32[4,128]{1,0:T(4,128)} %convert_bitcast_fusion.gate_ref, s32[1,1536]{1,0:T(1,128)} %compare_select_fusion.place_ref, bf16[1440,128]{1,0:T(8,128)(2,1)} %bitcast.61, ...), custom_call_target="tpu_custom_call" | custom-call | bytes 7380000 | tf_op jit(solution)/shard_map/pallas_call | solution.py:362
  26.9 1.9 collective-permute-start.2
  28.9 4.9 %collective-permute-start.1 = (bf16[128,640]{1,0:T(8,128)(2,1)S(1)}, bf16[128,640]{1,0:T(8,128)(2,1)S(1)}, u32[]{:S(2)}, u32[]{:S(2)}) collective-permute-start(bf16[128,640]{1,0:T(8,128)(2,1)S(1)} %fusion.9.own_ref), channel_id=1, source_target_pairs={{0,2},{1,3},{2,4},{3,5},{4,6},{5,7},{6,8},{7,9},{8,10},{9,11},{10,... | collective-permute-start | bytes 491528 | tf_op jit(solution)/shard_map/ppermute | solution.py:336
  33.8 7.2 %all-to-all-start = ((bf16[16,8,3072]{2,1,0:T(8,128)(2,1)}), bf16[16,8,3072]{2,1,0:T(8,128)(2,1)S(1)}, u32[]{:S(2)}, u32[]{:S(2)}) async-start(bf16[16,8,3072]{2,1,0:T(8,128)(2,1)} %bitcast.59), calls=%async_computation | async-start | bytes 1572864 | tf_op jit(solution)/shard_map/all_to_all | solution.py:370
  41.0 1.4 collective-permute-done.2.near_ref
  42.4 3.8 %collective-permute-done.1.far_ref = bf16[128,640]{1,0:T(8,128)(2,1)S(1)} collective-permute-done((bf16[128,640]{1,0:T(8,128)(2,1)S(1)}, bf16[128,640]{1,0:T(8,128)(2,1)S(1)}, u32[]{:S(2)}, u32[]{:S(2)}) %collective-permute-start.1) | collective-permute-done | bytes 163872 | tf_op jit(solution)/shard_map/ppermute | solution.py:336
  46.9 9.7 %shard_map.164 = (bf16[384,4096]{1,0:T(8,128)(2,1)}, bf16[2048,128]{1,0:T(8,128)(2,1)}, bf16[256,384]{1,0:T(8,128)(2,1)}, bf16[384,256]{1,0:T(8,128)(2,1)}) custom-call(bf16[128,2048]{1,0:T(8,128)(2,1)} %q_ref.1, bf16[128,640]{1,0:T(8,128)(2,1)} %copy-done.11, bf16[128,640]{1,0:T(8,128)(2,1)} %copy-done.10, bf16[128,640]{1,0:T(8,128)(2,1)} %copy-done.5, ...), custom_call_target="tpu_custom_call" | custom-call | bytes 29520000 | tf_op jit(solution)/shard_map/pallas_call | solution.py:376
  56.6 1.9 collective-permute-start.4
  58.5 9.1 %collective-permute-done.4 = bf16[64,1536]{1,0:T(8,128)(2,1)S(1)} collective-permute-done((bf16[64,1536]{1,0:T(8,128)(2,1)S(1)}, bf16[64,1536]{1,0:T(8,128)(2,1)S(1)}, u32[]{:S(2)}, u32[]{:S(2)}) %collective-permute-start.4) | collective-permute-done | bytes 196640 | tf_op jit(solution)/shard_map/ppermute | solution.py:331
  69.2 1.9 collective-permute-start.3
  71.1 1.4 collective-permute-done.3.x2_any
  72.5 2.0 collective-permute-start.5
  74.5 4.6 %collective-permute-done.5.wo_any = bf16[768,1536]{1,0:T(8,128)(2,1)S(1)} collective-permute-done((bf16[768,1536]{1,0:T(8,128)(2,1)}, bf16[768,1536]{1,0:T(8,128)(2,1)S(1)}, u32[]{:S(2)}, u32[]{:S(2)}) %collective-permute-start.5) | collective-permute-done | bytes 2359328 | tf_op jit(solution)/shard_map/ppermute | solution.py:398
  79.1 1.5 copy-done.2
  80.6 6.8 %shard_map.165 = (bf16[128,1664]{1,0:T(8,128)(2,1)}, bf16[128,1536]{1,0:T(8,128)(2,1)}) custom-call(bf16[128,3072]{1,0:T(8,128)(2,1)} %bitcast.57, bf16[768,1536]{1,0:T(8,128)(2,1)} %all-gather.3.cloned.1.call-done.wm_any, bf16[768,1536]{1,0:T(8,128)(2,1)} %copy-done.2), custom_call_target="tpu_custom_call" | custom-call | bytes 11070000 | tf_op jit(solution)/shard_map/pallas_call | solution.py:399
  87.4 2.0 collective-permute-start.6
  89.5 7.5 %all-to-all-start.1 = ((bf16[16,8,1664]{2,1,0:T(8,128)(2,1)}), bf16[16,8,1664]{2,1,0:T(8,128)(2,1)S(1)}, u32[]{:S(2)}, u32[]{:S(2)}) async-start(bf16[16,8,1664]{2,1,0:T(8,128)(2,1)} %bitcast.60), calls=%async_computation.1 | async-start | bytes 851968 | tf_op jit(solution)/shard_map/all_to_all | solution.py:414
  97.8 3.6 %shard_map.166 = bf16[768,1536]{1,0:T(8,128)(2,1)} custom-call(bf16[128,768]{1,0:T(8,128)(2,1)} %get-tuple-element.80.x_any, bf16[128,768]{1,0:T(8,128)(2,1)} %copy-done.8, bf16[128,1536]{1,0:T(8,128)(2,1)} %get-tuple-element.47.pg_any, bf16[128,1536]{1,0:T(8,128)(2,1)} %copy-done.6), custom_call_target="tpu_custom_call" | custom-call | bytes 7380000 | tf_op jit(solution)/shard_map/pallas_call | solution.py:418
  102.5 8.9 %collective-permute-start.8 = (bf16[48,1536]{1,0:T(8,128)(2,1)S(1)}, bf16[48,1536]{1,0:T(8,128)(2,1)S(1)}, u32[]{:S(2)}, u32[]{:S(2)}) collective-permute-start(bf16[48,1536]{1,0:T(8,128)(2,1)S(1)} %get-tuple-element.78), channel_id=1, source_target_pairs={{0,28},{4,0},{8,4},{12,8},{16,12},{20,16},{24,20},{28,24},{1,29},{... | collective-permute-start | bytes 442376 | tf_op jit(solution)/shard_map/ppermute | solution.py:304
  111.4 1.9 collective-permute-start.7
  113.3 4.8 %collective-permute-done.8 = bf16[48,1536]{1,0:T(8,128)(2,1)S(1)} collective-permute-done((bf16[48,1536]{1,0:T(8,128)(2,1)S(1)}, bf16[48,1536]{1,0:T(8,128)(2,1)S(1)}, u32[]{:S(2)}, u32[]{:S(2)}) %collective-permute-start.8) | collective-permute-done | bytes 147488 | tf_op jit(solution)/shard_map/ppermute | solution.py:304
  118.1 3.5 %collective-permute-done.7 = bf16[48,1536]{1,0:T(8,128)(2,1)S(1)} collective-permute-done((bf16[48,1536]{1,0:T(8,128)(2,1)S(1)}, bf16[48,1536]{1,0:T(8,128)(2,1)S(1)}, u32[]{:S(2)}, u32[]{:S(2)}) %collective-permute-start.7) | collective-permute-done | bytes 147488 | tf_op jit(solution)/shard_map/ppermute | solution.py:303
  121.6 1.1 fusion.4
  122.7 2.3 %collective-permute-start.9 = (bf16[96,1536]{1,0:T(8,128)(2,1)S(1)}, bf16[96,1536]{1,0:T(8,128)(2,1)S(1)}, u32[]{:S(2)}, u32[]{:S(2)}) collective-permute-start(bf16[96,1536]{1,0:T(8,128)(2,1)S(1)} %get-tuple-element.50), channel_id=1, source_target_pairs={{0,4},{4,8},{8,12},{12,16},{16,20},{20,24},{24,28},{28,0},{1,5},{5... | collective-permute-start | bytes 884744 | tf_op jit(solution)/shard_map/ppermute | solution.py:315
  125.0 4.8 %collective-permute-start.10 = (bf16[96,1536]{1,0:T(8,128)(2,1)S(1)}, bf16[96,1536]{1,0:T(8,128)(2,1)S(1)}, u32[]{:S(2)}, u32[]{:S(2)}) collective-permute-start(bf16[96,1536]{1,0:T(8,128)(2,1)S(1)} %get-tuple-element.51), channel_id=1, source_target_pairs={{0,28},{4,0},{8,4},{12,8},{16,12},{20,16},{24,20},{28,24},{1,29},{... | collective-permute-start | bytes 884744 | tf_op jit(solution)/shard_map/ppermute | solution.py:316
  129.8 4.4 %collective-permute-done.9 = bf16[96,1536]{1,0:T(8,128)(2,1)S(1)} collective-permute-done((bf16[96,1536]{1,0:T(8,128)(2,1)S(1)}, bf16[96,1536]{1,0:T(8,128)(2,1)S(1)}, u32[]{:S(2)}, u32[]{:S(2)}) %collective-permute-start.9) | collective-permute-done | bytes 294944 | tf_op jit(solution)/shard_map/ppermute | solution.py:315
  134.2 1.2 collective-permute-done.10
  135.4 1.9 fusion.3
  137.3 1.9 collective-permute-start.11
  139.2 1.9 collective-permute-start.14
  141.2 5.8 %collective-permute-start.15 = (bf16[96,1536]{1,0:T(8,128)(2,1)S(1)}, bf16[96,1536]{1,0:T(8,128)(2,1)}, u32[]{:S(2)}, u32[]{:S(2)}) collective-permute-start(bf16[96,1536]{1,0:T(8,128)(2,1)S(1)} %get-tuple-element.55), channel_id=1, source_target_pairs={{0,28},{4,0},{8,4},{12,8},{16,12},{20,16},{24,20},{28,24},{1,29},{... | collective-permute-start | bytes 884744 | tf_op jit(solution)/shard_map/ppermute | solution.py:316
  147.7 5.2 %collective-permute-done.14 = bf16[96,1536]{1,0:T(8,128)(2,1)} collective-permute-done((bf16[96,1536]{1,0:T(8,128)(2,1)}, bf16[96,1536]{1,0:T(8,128)(2,1)}, u32[]{:S(2)}, u32[]{:S(2)}) %collective-permute-start.14) | collective-permute-done | bytes 294944 | tf_op jit(solution)/shard_map/ppermute | solution.py:315
  153.7 1.4 fusion
  155.1 1.6 copy-done.1
  156.7 15.6 %shard_map.167 = (bf16[1440,128]{1,0:T(8,128)(2,1)}, f32[4,128]{1,0:T(4,128)}, bf16[384,4096]{1,0:T(8,128)(2,1)}, bf16[128,512]{1,0:T(8,128)(2,1)}, bf16[128,512]{1,0:T(8,128)(2,1)}, /*index=5*/f32[128,512]{1,0:T(8,128)}) custom-call(s32[2]{0:T(128)} %pad_add_fusion.at_ref, s32[4,128]{1,0:T(4,128)} %bitcast.66, s32[128,1]{1,0:T(8,128)} %broadcast_in_dim_reshape.4.held_ref, ...), custom_call_target="tpu_custom_call" | custom-call | bytes 29520000 | tf_op jit(solution)/shard_map/pallas_call | solution.py:435
  172.3 7.8 %collective-permute-start.12 = (bf16[128,512]{1,0:T(8,128)(2,1)}, bf16[128,512]{1,0:T(8,128)(2,1)S(1)}, u32[]{:S(2)}, u32[]{:S(2)}) collective-permute-start(bf16[128,512]{1,0:T(8,128)(2,1)} %get-tuple-element.62), channel_id=1, source_target_pairs={{1,0},{2,1},{3,2},{4,3},{5,4},{6,5},{7,6},{8,7},{9,8},{10,9},{11,1... | collective-permute-start | bytes 393224 | tf_op jit(solution)/shard_map/ppermute | solution.py:336
  180.1 3.7 %collective-permute-start.13 = (bf16[128,512]{1,0:T(8,128)(2,1)}, bf16[128,512]{1,0:T(8,128)(2,1)S(1)}, u32[]{:S(2)}, u32[]{:S(2)}) collective-permute-start(bf16[128,512]{1,0:T(8,128)(2,1)} %get-tuple-element.63), channel_id=1, source_target_pairs={{2,0},{3,1},{4,2},{5,3},{6,4},{7,5},{8,6},{9,7},{10,8},{11,9},{12,... | collective-permute-start | bytes 393224 | tf_op jit(solution)/shard_map/ppermute | solution.py:336
  183.9 1.9 collective-permute-start.16
  185.8 5.1 %collective-permute-start.17 = (bf16[96,1536]{1,0:T(8,128)(2,1)S(1)}, bf16[96,1536]{1,0:T(8,128)(2,1)S(1)}, u32[]{:S(2)}, u32[]{:S(2)}) collective-permute-start(bf16[96,1536]{1,0:T(8,128)(2,1)S(1)} %get-tuple-element.69), channel_id=1, source_target_pairs={{0,28},{4,0},{8,4},{12,8},{16,12},{20,16},{24,20},{28,24},{1,29},{... | collective-permute-start | bytes 884744 | tf_op jit(solution)/shard_map/ppermute | solution.py:326
  190.9 1.2 convert_bitcast_fusion.1
  192.2 3.5 %shard_map.168 = bf16[128,2048]{1,0:T(8,128)(2,1)} custom-call(bf16[384,4096]{1,0:T(8,128)(2,1)} %get-tuple-element.59.sg_ref, bf16[256,384]{1,0:T(8,128)(2,1)} %get-tuple-element.60.kt_ref), custom_call_target="tpu_custom_call" | custom-call | bytes 11070000 | tf_op jit(solution)/shard_map/pallas_call | solution.py:473
  196.1 1.1 fusion.2
  197.2 3.2 %collective-permute-start.18 = (bf16[48,1536]{1,0:T(8,128)(2,1)S(1)}, bf16[48,1536]{1,0:T(8,128)(2,1)S(1)}, u32[]{:S(2)}, u32[]{:S(2)}) collective-permute-start(bf16[48,1536]{1,0:T(8,128)(2,1)S(1)} %slice.64), channel_id=1, source_target_pairs={{0,2},{2,0},{1,3},{3,1},{4,6},{6,4},{5,7},{7,5},{8,10},{10,8},{9,1... | collective-permute-start | bytes 442376 | tf_op jit(solution)/shard_map/ppermute | solution.py:468
  201.1 4.6 %collective-permute-done.18 = bf16[48,1536]{1,0:T(8,128)(2,1)S(1)} collective-permute-done((bf16[48,1536]{1,0:T(8,128)(2,1)S(1)}, bf16[48,1536]{1,0:T(8,128)(2,1)S(1)}, u32[]{:S(2)}, u32[]{:S(2)}) %collective-permute-start.18) | collective-permute-done | bytes 147488 | tf_op jit(solution)/shard_map/ppermute | solution.py:468
  (57 shorter events, 12.4 us)
Async XLA Ops:
  7.2 33.8 %copy-start.9 = (bf16[64,1440]{1,0:T(8,128)(2,1)S(1)}, bf16[64,1440]{1,0:T(8,128)(2,1)}, u32[]{:S(2)}) copy-start(bf16[64,1440]{1,0:T(8,128)(2,1)} %param.23) | copy-start | bytes 552964
  7.2 65.3 %all-gather.3.cloned.1.call-start = ((), (), s32[]{:S(2)}) async-start(), calls=%async_computation.2 | async-start | bytes 2654208 | tf_op jit(solution)/shard_map/all_gather | solution.py:345
  8.2 9.0 %collective-permute-start = (bf16[48,1536]{1,0:T(8,128)(2,1)S(1)}, bf16[48,1536]{1,0:T(8,128)(2,1)S(1)}, u32[]{:S(2)}, u32[]{:S(2)}) collective-permute-start(bf16[48,1536]{1,0:T(8,128)(2,1)S(1)} %pad.20), channel_id=1, source_target_pairs={{0,2},{2,0},{1,3},{3,1},{4,6},{6,4},{5,7},{7,5},{8,10},{10,8},{9,1... | collective-permute-start | bytes 442376 | tf_op jit(solution)/shard_map/ppermute | solution.py:331
  21.6 24.7 %copy-start.5 = (bf16[128,640]{1,0:T(8,128)(2,1)}, bf16[128,640]{1,0:T(8,128)(2,1)S(1)}, u32[]{:S(2)}) copy-start(bf16[128,640]{1,0:T(8,128)(2,1)S(1)} %fusion.9.own_ref) | copy-start | bytes 491524
  26.9 15.5 %collective-permute-start.2 = (bf16[128,640]{1,0:T(8,128)(2,1)S(1)}, bf16[128,640]{1,0:T(8,128)(2,1)S(1)}, u32[]{:S(2)}, u32[]{:S(2)}) collective-permute-start(bf16[128,640]{1,0:T(8,128)(2,1)S(1)} %fusion.9.own_ref), channel_id=1, source_target_pairs={{0,1},{1,2},{2,3},{3,4},{4,5},{5,6},{6,7},{7,8},{8,9},{9,10},{10,1... | collective-permute-start | bytes 491528 | tf_op jit(solution)/shard_map/ppermute | solution.py:336
  28.9 17.4 %collective-permute-start.1 = (bf16[128,640]{1,0:T(8,128)(2,1)S(1)}, bf16[128,640]{1,0:T(8,128)(2,1)S(1)}, u32[]{:S(2)}, u32[]{:S(2)}) collective-permute-start(bf16[128,640]{1,0:T(8,128)(2,1)S(1)} %fusion.9.own_ref), channel_id=1, source_target_pairs={{0,2},{1,3},{2,4},{3,5},{4,6},{5,7},{6,8},{7,9},{8,10},{9,11},{10,... | collective-permute-start | bytes 491528 | tf_op jit(solution)/shard_map/ppermute | solution.py:336
  33.8 34.6 %all-to-all-start = ((bf16[16,8,3072]{2,1,0:T(8,128)(2,1)}), bf16[16,8,3072]{2,1,0:T(8,128)(2,1)S(1)}, u32[]{:S(2)}, u32[]{:S(2)}) async-start(bf16[16,8,3072]{2,1,0:T(8,128)(2,1)} %bitcast.59), calls=%async_computation | async-start | bytes 1572864 | tf_op jit(solution)/shard_map/all_to_all | solution.py:370
  41.0 96.4 %all-gather.5.cloned.1.call-start = ((), (), s32[]{:S(2)}) async-start(), calls=%async_computation.3 | async-start | bytes 3538944 | tf_op jit(solution)/shard_map/all_gather | solution.py:396
  42.4 3.8 %copy-start.10 = (bf16[128,640]{1,0:T(8,128)(2,1)}, bf16[128,640]{1,0:T(8,128)(2,1)S(1)}, u32[]{:S(2)}) copy-start(bf16[128,640]{1,0:T(8,128)(2,1)S(1)} %collective-permute-done.2.near_ref) | copy-start | bytes 491524
  46.2 0.7 copy-start.11
  56.6 11.0 %collective-permute-start.4 = (bf16[64,1536]{1,0:T(8,128)(2,1)S(1)}, bf16[64,1536]{1,0:T(8,128)(2,1)S(1)}, u32[]{:S(2)}, u32[]{:S(2)}) collective-permute-start(bf16[64,1536]{1,0:T(8,128)(2,1)S(1)} %pad.22), channel_id=1, source_target_pairs={{0,2},{2,0},{1,3},{3,1},{4,6},{6,4},{5,7},{7,5},{8,10},{10,8},{9,1... | collective-permute-start | bytes 589832 | tf_op jit(solution)/shard_map/ppermute | solution.py:331
  67.6 0.7 copy-start.4
  68.4 10.7 %copy-start = (bf16[16,8,3072]{2,1,0:T(8,128)(2,1)}, bf16[16,8,3072]{2,1,0:T(8,128)(2,1)S(1)}, u32[]{:S(2)}) copy-start(bf16[16,8,3072]{2,1,0:T(8,128)(2,1)S(1)} %all-to-all-done) | copy-start | bytes 2359300
  69.2 3.3 %collective-permute-start.3 = (bf16[128,768]{1,0:T(8,128)(2,1)S(1)}, bf16[128,768]{1,0:T(8,128)(2,1)S(1)}, u32[]{:S(2)}, u32[]{:S(2)}) collective-permute-start(bf16[128,768]{1,0:T(8,128)(2,1)S(1)} %get-tuple-element.81), channel_id=1, source_target_pairs={{0,1},{1,0},{2,3},{3,2},{4,5},{5,4},{6,7},{7,6},{8,9},{9,8},{10,11... | collective-permute-start | bytes 589832 | tf_op jit(solution)/shard_map/ppermute | solution.py:394
  72.5 24.6 %copy-start.8 = (bf16[128,768]{1,0:T(8,128)(2,1)}, bf16[128,768]{1,0:T(8,128)(2,1)S(1)}, u32[]{:S(2)}) copy-start(bf16[128,768]{1,0:T(8,128)(2,1)S(1)} %collective-permute-done.3.x2_any) | copy-start | bytes 589828
  72.5 6.6 %collective-permute-start.5 = (bf16[768,1536]{1,0:T(8,128)(2,1)}, bf16[768,1536]{1,0:T(8,128)(2,1)S(1)}, u32[]{:S(2)}, u32[]{:S(2)}) collective-permute-start(bf16[768,1536]{1,0:T(8,128)(2,1)} %all-gather.3.cloned.1.call-done.wm_any), channel_id=1, source_target_pairs={{0,1},{1,0},{2,3},{3,2},{4,5},{5,4},{6,7},{7,6},{8,9},{9,8},{10,11... | collective-permute-start | bytes 7077896 | tf_op jit(solution)/shard_map/ppermute | solution.py:398
  79.1 1.5 copy-start.2
  87.4 9.6 %collective-permute-start.6 = (bf16[128,1536]{1,0:T(8,128)(2,1)}, bf16[128,1536]{1,0:T(8,128)(2,1)S(1)}, u32[]{:S(2)}, u32[]{:S(2)}) collective-permute-start(bf16[128,1536]{1,0:T(8,128)(2,1)} %get-tuple-element.47.pg_any), channel_id=1, source_target_pairs={{0,1},{1,0},{2,3},{3,2},{4,5},{5,4},{6,7},{7,6},{8,9},{9,8},{10,11... | collective-permute-start | bytes 1179656 | tf_op jit(solution)/shard_map/ppermute | solution.py:417
  89.5 33.2 %all-to-all-start.1 = ((bf16[16,8,1664]{2,1,0:T(8,128)(2,1)}), bf16[16,8,1664]{2,1,0:T(8,128)(2,1)S(1)}, u32[]{:S(2)}, u32[]{:S(2)}) async-start(bf16[16,8,1664]{2,1,0:T(8,128)(2,1)} %bitcast.60), calls=%async_computation.1 | async-start | bytes 851968 | tf_op jit(solution)/shard_map/all_to_all | solution.py:414
  97.0 0.8 copy-start.6
  102.5 15.6 %collective-permute-start.8 = (bf16[48,1536]{1,0:T(8,128)(2,1)S(1)}, bf16[48,1536]{1,0:T(8,128)(2,1)S(1)}, u32[]{:S(2)}, u32[]{:S(2)}) collective-permute-start(bf16[48,1536]{1,0:T(8,128)(2,1)S(1)} %get-tuple-element.78), channel_id=1, source_target_pairs={{0,28},{4,0},{8,4},{12,8},{16,12},{20,16},{24,20},{28,24},{1,29},{... | collective-permute-start | bytes 442376 | tf_op jit(solution)/shard_map/ppermute | solution.py:304
  111.4 10.2 %collective-permute-start.7 = (bf16[48,1536]{1,0:T(8,128)(2,1)S(1)}, bf16[48,1536]{1,0:T(8,128)(2,1)S(1)}, u32[]{:S(2)}, u32[]{:S(2)}) collective-permute-start(bf16[48,1536]{1,0:T(8,128)(2,1)S(1)} %get-tuple-element.79), channel_id=1, source_target_pairs={{0,4},{4,8},{8,12},{12,16},{16,20},{20,24},{24,28},{28,0},{1,5},{5... | collective-permute-start | bytes 442376 | tf_op jit(solution)/shard_map/ppermute | solution.py:303
  122.7 14.6 %copy-start.3 = (bf16[16,8,1664]{2,1,0:T(8,128)(2,1)}, bf16[16,8,1664]{2,1,0:T(8,128)(2,1)S(1)}, u32[]{:S(2)}) copy-start(bf16[16,8,1664]{2,1,0:T(8,128)(2,1)S(1)} %all-to-all-done.1) | copy-start | bytes 1277956
  122.7 11.5 %collective-permute-start.9 = (bf16[96,1536]{1,0:T(8,128)(2,1)S(1)}, bf16[96,1536]{1,0:T(8,128)(2,1)S(1)}, u32[]{:S(2)}, u32[]{:S(2)}) collective-permute-start(bf16[96,1536]{1,0:T(8,128)(2,1)S(1)} %get-tuple-element.50), channel_id=1, source_target_pairs={{0,4},{4,8},{8,12},{12,16},{16,20},{20,24},{24,28},{28,0},{1,5},{5... | collective-permute-start | bytes 884744 | tf_op jit(solution)/shard_map/ppermute | solution.py:315
  125.0 10.4 %collective-permute-start.10 = (bf16[96,1536]{1,0:T(8,128)(2,1)S(1)}, bf16[96,1536]{1,0:T(8,128)(2,1)S(1)}, u32[]{:S(2)}, u32[]{:S(2)}) collective-permute-start(bf16[96,1536]{1,0:T(8,128)(2,1)S(1)} %get-tuple-element.51), channel_id=1, source_target_pairs={{0,28},{4,0},{8,4},{12,8},{16,12},{20,16},{24,20},{28,24},{1,29},{... | collective-permute-start | bytes 884744 | tf_op jit(solution)/shard_map/ppermute | solution.py:316
  137.3 17.7 %collective-permute-start.11 = (bf16[1024,1536]{1,0:T(8,128)(2,1)}, bf16[1024,1536]{1,0:T(8,128)(2,1)S(1)}, u32[]{:S(2)}, u32[]{:S(2)}) collective-permute-start(bf16[1024,1536]{1,0:T(8,128)(2,1)} %all-gather.5.cloned.1.call-done.om_any), channel_id=1, source_target_pairs={{0,1},{1,0},{2,3},{3,2},{4,5},{5,4},{6,7},{7,6},{8,9},{9,8},{10,11... | collective-permute-start | bytes 9437192 | tf_op jit(solution)/shard_map/ppermute | solution.py:434
  139.2 13.6 %collective-permute-start.14 = (bf16[96,1536]{1,0:T(8,128)(2,1)}, bf16[96,1536]{1,0:T(8,128)(2,1)}, u32[]{:S(2)}, u32[]{:S(2)}) collective-permute-start(bf16[96,1536]{1,0:T(8,128)(2,1)} %get-tuple-element.54), channel_id=1, source_target_pairs={{0,4},{4,8},{8,12},{12,16},{16,20},{20,24},{24,28},{28,0},{1,5},{5... | collective-permute-start | bytes 884744 | tf_op jit(solution)/shard_map/ppermute | solution.py:315
  141.2 12.5 %collective-permute-start.15 = (bf16[96,1536]{1,0:T(8,128)(2,1)S(1)}, bf16[96,1536]{1,0:T(8,128)(2,1)}, u32[]{:S(2)}, u32[]{:S(2)}) collective-permute-start(bf16[96,1536]{1,0:T(8,128)(2,1)S(1)} %get-tuple-element.55), channel_id=1, source_target_pairs={{0,28},{4,0},{8,4},{12,8},{16,12},{20,16},{24,20},{28,24},{1,29},{... | collective-permute-start | bytes 884744 | tf_op jit(solution)/shard_map/ppermute | solution.py:316
  155.1 1.6 copy-start.1
  172.3 23.3 %copy-start.7 = (f32[128,512]{1,0:T(8,128)S(1)}, f32[128,512]{1,0:T(8,128)}, u32[]{:S(2)}) copy-start(f32[128,512]{1,0:T(8,128)} %get-tuple-element.61) | copy-start | bytes 786436
  172.3 23.3 %collective-permute-start.12 = (bf16[128,512]{1,0:T(8,128)(2,1)}, bf16[128,512]{1,0:T(8,128)(2,1)S(1)}, u32[]{:S(2)}, u32[]{:S(2)}) collective-permute-start(bf16[128,512]{1,0:T(8,128)(2,1)} %get-tuple-element.62), channel_id=1, source_target_pairs={{1,0},{2,1},{3,2},{4,3},{5,4},{6,5},{7,6},{8,7},{9,8},{10,9},{11,1... | collective-permute-start | bytes 393224 | tf_op jit(solution)/shard_map/ppermute | solution.py:336
  180.1 15.5 %collective-permute-start.13 = (bf16[128,512]{1,0:T(8,128)(2,1)}, bf16[128,512]{1,0:T(8,128)(2,1)S(1)}, u32[]{:S(2)}, u32[]{:S(2)}) collective-permute-start(bf16[128,512]{1,0:T(8,128)(2,1)} %get-tuple-element.63), channel_id=1, source_target_pairs={{2,0},{3,1},{4,2},{5,3},{6,4},{7,5},{8,6},{9,7},{10,8},{11,9},{12,... | collective-permute-start | bytes 393224 | tf_op jit(solution)/shard_map/ppermute | solution.py:336
  183.9 11.9 %collective-permute-start.16 = (bf16[96,1536]{1,0:T(8,128)(2,1)S(1)}, bf16[96,1536]{1,0:T(8,128)(2,1)S(1)}, u32[]{:S(2)}, u32[]{:S(2)}) collective-permute-start(bf16[96,1536]{1,0:T(8,128)(2,1)S(1)} %get-tuple-element.68), channel_id=1, source_target_pairs={{0,4},{4,8},{8,12},{12,16},{16,20},{20,24},{24,28},{28,0},{1,5},{5... | collective-permute-start | bytes 884744 | tf_op jit(solution)/shard_map/ppermute | solution.py:325
  185.8 10.3 %collective-permute-start.17 = (bf16[96,1536]{1,0:T(8,128)(2,1)S(1)}, bf16[96,1536]{1,0:T(8,128)(2,1)S(1)}, u32[]{:S(2)}, u32[]{:S(2)}) collective-permute-start(bf16[96,1536]{1,0:T(8,128)(2,1)S(1)} %get-tuple-element.69), channel_id=1, source_target_pairs={{0,28},{4,0},{8,4},{12,8},{16,12},{20,16},{24,20},{28,24},{1,29},{... | collective-permute-start | bytes 884744 | tf_op jit(solution)/shard_map/ppermute | solution.py:326
  197.2 8.5 %collective-permute-start.18 = (bf16[48,1536]{1,0:T(8,128)(2,1)S(1)}, bf16[48,1536]{1,0:T(8,128)(2,1)S(1)}, u32[]{:S(2)}, u32[]{:S(2)}) collective-permute-start(bf16[48,1536]{1,0:T(8,128)(2,1)S(1)} %slice.64), channel_id=1, source_target_pairs={{0,2},{2,0},{1,3},{3,1},{4,6},{6,4},{5,7},{7,5},{8,10},{10,8},{9,1... | collective-permute-start | bytes 442376 | tf_op jit(solution)/shard_map/ppermute | solution.py:468
Sparse Core Ops, SparseCore 0:
  18.1 49.2 all-gather.2
  69.4 52.3 all-gather.4

commit v4 on v3

--- a/solution.py
+++ b/solution.py
@@ -147,65 +147,61 @@
 
 
 def expert_kernel(
-    got_ref, wm_any, wo_any, back_any, pg_any, wm_ref, wo_ref, back_ref, pg_ref, pre_ref, sems
+    got_ref, got2_ref, wm_any, wo_any, back_any, part_any,
+    wm_ref, wo_ref, back_ref, pg_ref, pre_ref, part_ref, sems,
 ):
     loads = copies_of(((wm_any, wm_ref), (wo_any, wo_ref)), sems)
     for copy in loads:
         copy.start()
+    x_mine = jnp.concatenate([got_ref[:, :HALF], got2_ref[:, HALF:DP]], axis=0)
+    x_other = jnp.concatenate([got_ref[:, HALF:DP], got2_ref[:, :HALF]], axis=0)
     for copy in loads:
         copy.wait()
     step = 512
     for lo in range(0, DP, step):
         at = slice(lo, lo + step)
-        pre_ref[:, at] = dot(got_ref[:, :HALF], wm_ref[:, at], ((1,), (0,))) + dot(
-            got_ref[:, HALF:DP], wo_ref[:, at], ((1,), (0,))
+        pre_ref[:, at] = dot(x_mine, wm_ref[:, at], ((1,), (0,))) + dot(
+            x_other, wo_ref[:, at], ((1,), (0,))
         )
-    gate = got_ref[:, DP + F : DP + F + 1].astype(F32)
-    total = jnp.zeros((ROWS, 1), F32)
+    gate_at = slice(DP + F, DP + F + 1)
+    gate = jnp.concatenate([got_ref[:, gate_at], got2_ref[:, gate_at]], axis=0).astype(F32)
+    total = jnp.zeros((2 * ROWS, 1), F32)
     for lo in range(0, DP, step):
         pre = pre_ref[:, lo : lo + step]
-        grad = got_ref[:, DP + lo : DP + lo + step].astype(F32)
+        at = slice(DP + lo, DP + lo + step)
+        grad = jnp.concatenate([got_ref[:, at], got2_ref[:, at]], axis=0).astype(F32)
         sig = 1.0 / (1.0 + jnp.exp(-pre))
         total = total + jnp.sum(grad * (pre * sig), axis=1, keepdims=True)
         slope = sig * (1.0 + pre * (1.0 - sig))
         pg_ref[:, lo : lo + step] = (gate * grad * slope).astype(BF)
-    store = pltpu.make_async_copy(pg_ref, pg_any, sems.at[2])
-    store.start()
     pg = pg_ref[...]
+    stores = []
+    for c in range(HALF // 256):
+        r = slice(c * 256, (c + 1) * 256)
+        part_ref[r, :] = dot(x_mine[:, r], pg, ((0,), (0,))).astype(BF)
+        stores.append(
+            pltpu.make_async_copy(part_ref.at[r, :], part_any.at[r, :], sems.at[2 + c])
+        )
+        stores[-1].start()
+    pg = pg_ref[:ROWS, :]
     for c in range(HALF // 256):
         r = slice(c * 256, (c + 1) * 256)
         back_ref[:, c * 256 : (c + 1) * 256] = dot(pg, wm_ref[r, :], ((1,), (1,))).astype(BF)
         back_ref[:, HALF + c * 256 : HALF + (c + 1) * 256] = dot(
             pg, wo_ref[r, :], ((1,), (1,))
         ).astype(BF)
-    back_ref[:, DP:] = jnp.broadcast_to(total, (ROWS, BACK - DP)).astype(BF)
-    returned = pltpu.make_async_copy(back_ref, back_any, sems.at[3])
-    returned.start()
-    store.wait()
-    returned.wait()
-
-
-def map_kernel(
-    x_any, x2_any, pg_any, pg2_any, out_ref, x_ref, x2_ref, pg_ref, pg2_ref, sems
-):
-    pairs = ((x_any, x_ref), (x2_any, x2_ref), (pg_any, pg_ref), (pg2_any, pg2_ref))
-    loads = copies_of(pairs, sems)
-    for copy in loads:
-        copy.start()
-    for copy in loads:
-        copy.wait()
-    pg = jnp.concatenate([pg_ref[...], pg2_ref[...]], axis=0)
-    for c in range(HALF // 256):
-        at = slice(c * 256, (c + 1) * 256)
-        rows = jnp.concatenate([x_ref[:, at], x2_ref[:, at]], axis=0)
-        out_ref[at, :] = dot(rows, pg, ((0,), (0,))).astype(BF)
+    back_ref[:, DP:] = jnp.broadcast_to(total[:ROWS], (ROWS, BACK - DP)).astype(BF)
+    stores.append(pltpu.make_async_copy(back_ref, back_any, sems.at[5]))
+    stores[-1].start()
+    for copy in stores:
+        copy.wait()
 
 
 def late_kernel(
-    at_ref, picked_ref, held_ref, place_ref, back_ref,
-    sent_any, v_any, skip_any, om_any, oo_any, qt_any, shares_any,
+    at_ref, picked_ref, held_ref, place_ref,
+    p0, p1, p2, p3, p4, p5, p6, p7, sent_any, v_any, skip_any, om_any, oo_any, qt_any, shares_any,
     src_ref, gate_ref, sg_ref, farg_ref, nearg_ref, owng_ref,
-    hidden_s, cot_s, acck_s, accv_s,
+    hidden_s, cot_s, acck_s, accv_s, back_ref,
     sent_ref, v_ref, skip_ref, om_ref, oo_ref, qt_ref, shares_ref, sems,
 ):
     pairs = (
@@ -213,8 +209,14 @@
         (v_any, v_ref), (qt_any, qt_ref), (shares_any, shares_ref),
     )
     copies = copies_of(pairs, sems)
-    for copy in copies:
+    arrived = []
+    for i, piece in enumerate((p0, p1, p2, p3, p4, p5, p6, p7)):
+        rows = pl.ds(pl.multiple_of(((at_ref[2] + i) % 8) * 16, 16), 16)
+        arrived.append(pltpu.make_async_copy(piece, back_ref.at[rows, :], sems.at[7 + i]))
+    for copy in arrived + copies:
         copy.start()
+    for copy in arrived:
+        copy.wait()
     copies[0].wait()
     sent_bf = sent_ref[...]
     sent = sent_bf.astype(F32) > 0.5
@@ -289,46 +291,30 @@
         qg_ref[:, n * 128 : (n + 1) * 128] = jnp.transpose(both).astype(BF)
 
 
-RIGHT = [(i, (i + 1) % 8) for i in range(8)]
-LEFT = [(i, (i + 7) % 8) for i in range(8)]
-
-
-def reduce_start(parts, returned):
-    half = parts.shape[1] // 2
-    z = lax.axis_index("z")
-
-    def chunk(k):
-        return lax.dynamic_index_in_dim(parts, (z + k) % 8, 0, keepdims=False)
-
-    right = lax.ppermute(chunk(4)[:half], "z", RIGHT)
-    left = lax.ppermute(chunk(4)[half:], "z", LEFT)
-    right, left = lax.optimization_barrier((right, left))
-    right = jnp.pad(right, ((0, half), (0, 0)))
-    left = jnp.pad(left, ((half, 0), (0, 0)))
-    marks = []
-    for k in (3, 2):
-        right = (chunk(k).astype(F32) + right.astype(F32)).astype(BF)
-        left = (chunk(8 - k).astype(F32) + left.astype(F32)).astype(BF)
-        ties = (returned,) if k == 3 else ()
-        right, left = lax.optimization_barrier((right, left, *ties))[:2]
-        marks = (right, left)
-        right = lax.ppermute(right, "z", RIGHT)
-        left = lax.ppermute(left, "z", LEFT)
-        right, left = lax.optimization_barrier((right, left))
-    right = (chunk(1).astype(F32) + right.astype(F32)).astype(BF)
-    left = (chunk(7).astype(F32) + left.astype(F32)).astype(BF)
-    return right, left, chunk(0), marks
-
-
-def reduce_end(right, left, mine, late):
-    right, left = lax.optimization_barrier((right, left, late))[:2]
-    right = lax.ppermute(right, "z", RIGHT)
-    left = lax.ppermute(left, "z", LEFT)
-    return mine.astype(F32) + right.astype(F32) + left.astype(F32)
-
-
-def both_xh(piece):
-    return jnp.concatenate([piece, lax.ppermute(piece, "xh", SWAP)], axis=0)
+def give_back(back):
+    y, xl = lax.axis_index("y"), lax.axis_index("xl")
+    grid = back.reshape(8, 2, CAPP, BACK)
+    turned = jnp.concatenate([grid, grid], axis=0)
+    keep = lax.dynamic_slice(turned, (y, xl, 0, 0), (8, 1, CAPP, BACK))
+    give = lax.dynamic_slice(turned, (y, 1 - xl, 0, 0), (8, 1, CAPP, BACK))
+    got = lax.ppermute(give, "xl", SWAP)
+    both = jnp.concatenate(
+        [jnp.where(xl == 0, keep, got), jnp.where(xl == 0, got, keep)], axis=1
+    ).reshape(8, 2 * CAPP, BACK)
+    pieces = [both[0]]
+    for k in range(7, 0, -1):
+        pieces.append(lax.ppermute(both[k], "y", [(i, (i + k) % 8) for i in range(8)]))
+    return pieces
+
+
+def both_xh(piece, natural):
+    other = lax.ppermute(piece, "xh", SWAP)
+    if not natural:
+        return jnp.concatenate([piece, other], axis=0)
+    lower = lax.axis_index("xh") == 0
+    return jnp.concatenate(
+        [jnp.where(lower, piece, other), jnp.where(lower, other, piece)], axis=0
+    )
 
 
 def shift_blocks(value, steps):
@@ -341,7 +327,7 @@
     xh = lax.axis_index("xh")
     w_pad = jnp.pad(weights[0], ((0, SEG - SHARD), (0, DP - F)))
     o_pad = jnp.pad(out_map, ((0, 0), (0, DP - D)))
-    w_pair = both_xh(w_pad)
+    w_pair = both_xh(w_pad, True)
     w_mine = lax.all_gather(w_pair, "z", axis=0, tiled=True)
 
     plus = (label + 1).astype(jnp.int32)
@@ -356,7 +342,7 @@
     rest = spot % HALF
     within = rest % SEG
     pair = rest // SEG
-    owner = (pair // 2) * 4 + ((pair % 2) ^ xh) * 2 + (half ^ core)
+    owner = (pair // 2) * 4 + (pair % 2) * 2 + (half ^ core)
     place = jnp.where(within < SHARD, owner * SHARD + within, -1)[None, :]
     dma = pltpu.SemaphoreType.DMA
     send, sent = call(
@@ -391,50 +377,36 @@
     )(q, far, near, own, plus.astype(F32)[None, :])
 
     got = order(got, v_win).reshape(ROWS, SEND)
-    x_swapped = lax.ppermute(got[:, HALF:DP], "core", SWAP)
-    o_pair = both_xh(order(o_pad, v_win))
+    got_other = lax.ppermute(got, "core", SWAP)
+    o_pair = both_xh(order(o_pad, send), False)
     o_mine = lax.all_gather(o_pair, "z", axis=0, tiled=True)
-    w_mine = order(w_mine, x_swapped, o_pair)
+    w_mine = order(w_mine, got_other, o_pair)
     w_other = lax.ppermute(w_mine, "core", SWAP)
-    back, pg = call(
+    back, partial = call(
         expert_kernel,
-        "vhh",
-        [out((ROWS, BACK)), out((ROWS, DP))],
+        "vvhh",
+        [out((ROWS, BACK)), out((HALF, DP))],
         "hh",
         [
             pltpu.VMEM((HALF, DP), BF),
             pltpu.VMEM((HALF, DP), BF),
             pltpu.VMEM((ROWS, BACK), BF),
-            pltpu.VMEM((ROWS, DP), BF),
-            pltpu.VMEM((ROWS, DP), F32),
-            dma((4,)),
+            pltpu.VMEM((2 * ROWS, DP), BF),
+            pltpu.VMEM((2 * ROWS, DP), F32),
+            pltpu.VMEM((HALF, DP), BF),
+            dma((6,)),
         ],
         3,
-    )(got, w_mine, w_other)
-    returned = lax.all_to_all(back.reshape(EXPERTS, CAPP, BACK), CTX, 0, 0, tiled=True)
-    returned = returned.reshape(ROWS, BACK)
-
-    pg_swapped = lax.ppermute(pg, "core", SWAP)
-    partial = call(
-        map_kernel,
-        "hhhh",
-        [out((HALF, DP))],
-        "v",
-        [
-            pltpu.VMEM((ROWS, HALF), BF),
-            pltpu.VMEM((ROWS, HALF), BF),
-            pltpu.VMEM((ROWS, DP), BF),
-            pltpu.VMEM((ROWS, DP), BF),
-            dma((4,)),
-        ],
-        2,
-    )(got[:, :HALF], x_swapped, pg, pg_swapped)[0]
-    right, left, mine, marks = reduce_start(partial.reshape(8, 2 * SEG, DP), returned)
-    o_mine = order(o_mine, *marks)
+    )(got, got_other, w_mine, w_other)
+    terms = lax.all_to_all(partial.reshape(16, SEG, DP), ("z", "xh"), 0, 0, tiled=True)
+    map_grad = jnp.sum(terms.astype(F32), axis=0)[None, :SHARD, :F].astype(BF)
+
+    returned = give_back(back)
+    o_mine = order(o_mine, *returned)
     o_other = lax.ppermute(o_mine, "core", SWAP)
     src_t, gate_t, sg, far_g, near_g, own_g = call(
         late_kernel,
-        "svvvvhhhhhhh",
+        "svvvhhhhhhhhhhhhhhh",
         [
             out((D, TOK)),
             out((4, TOK), F32),
@@ -449,6 +421,7 @@
             pltpu.VMEM((HEADS * HD, TOK), BF),
             pltpu.VMEM((3 * TOK, HD), F32),
             pltpu.VMEM((3 * TOK, HD), F32),
+            pltpu.VMEM((ROWS, BACK), BF),
             pltpu.VMEM((ROWS, TOK), BF),
             pltpu.VMEM(v_shape, BF),
             pltpu.VMEM((D, TOK), BF),
@@ -456,21 +429,16 @@
             pltpu.VMEM((16 * HD, DP), BF),
             pltpu.VMEM(qt_shape, BF),
             pltpu.VMEM(shares_shape, BF),
-            dma((7,)),
+            dma((15,)),
         ],
-        8,
+        0.1,
     )(
-        jnp.stack([core, xh]).astype(jnp.int32), picked_t, held, place, returned,
-        sent, v_win, skip.T, o_mine, o_other, q_t, shares,
-    )
-    merged = reduce_end(right, left, mine, near_g)
-    away = merged[SEG:].astype(BF)
-    map_grad = (merged[:SEG] + lax.ppermute(away, "xh", SWAP).astype(F32)).astype(BF)
-    map_grad = map_grad[None, :SHARD, :F]
-
+        jnp.stack([core, xh, lax.axis_index("y")]).astype(jnp.int32), picked_t, held, place,
+        *returned, sent, v_win, skip.T, o_mine, o_other, q_t, shares,
+    )
     got_near = shift_blocks(near_g, -1)
     got_far = shift_blocks(far_g, -2)
-    q_grad = call(query_kernel, "vv", [out((TOK, HEADS * HD))], "v", [], 3)(sg, k_t)[0]
+    q_grad = call(query_kernel, "vv", [out((TOK, HEADS * HD))], "v", [], 0.1)(sg, k_t)[0]
     kv_grad = (own_g + got_near.astype(F32) + got_far.astype(F32)).astype(BF)
     return (
         q_grad,

time: 214 us -> 195 us (0.911)
  the two profiles are of different devices: /device:TPU:40 before, /device:TPU:16 now
where the time goes in v4:
time: 195 us; the launch traced here: 194 us
  starting transfers between devices  81.2 us (42%)
  waiting for transfers between devices  42.2 us (22%)
  Pallas kernels  40.4 us (21%)
  between operations  14.5 us (7%)
  other arithmetic  7.73 us (4%)
  local copies, waits for them, and re-layouts  7.69 us (4%)
    ppermute x7, starting transfers between devices, give_back(): lax.ppermute(both[k], 'y', [(i, (i + k) % 8) for i in range(8)])  27.6 us
    ppermute x4, starting transfers between devices, shift_blocks(): lax.ppermute(value, ALL, [(i, i + steps) for i in range(first, last)])  17.1 us
    ppermute x4, waiting for transfers between devices, shift_blocks(): lax.ppermute(value, ALL, [(i, i + steps) for i in range(first, last)])  16.3 us
    pallas_call x1, Pallas kernels, shards(): call(late_kernel, 'svvvhhhhhhhhhhhhhhh', [out((D, TOK)), out((4, TOK), F3...  15.5 us
    pallas_call x1, Pallas kernels, shards(): call(shares_kernel, 'vvvvv', [out(shares_shape), out(qt_shape), out(kt_sh...  9.67 us
    ppermute x2, waiting for transfers between devices, both_xh(): other = lax.ppermute(piece, 'xh', SWAP)  9.38 us
    ppermute x2, starting transfers between devices, both_xh(): other = lax.ppermute(piece, 'xh', SWAP)  9.26 us
    all_to_all x1, starting transfers between devices, shards(): lax.all_to_all(send.reshape(EXPERTS, CAPP, SEND), CTX, 0, 0, tiled=True)  8.7 us
  transfers between devices with their start and end apart: 21, of which 10 were waited for; matrix products, arithmetic and copies ran while one was open for 5% of the time, Pallas kernels for 21%

profile of v4, /device:TPU:16, one launch (start us, length us, event | category | flops | bytes accessed | tf_op | source)
XLA Modules:
  0.0 193.8 jit_solution(8969923297238802219)
XLA Ops:
  7.2 0.9 pad.12
  8.2 4.9 %collective-permute-start = (bf16[48,1536]{1,0:T(8,128)(2,1)S(1)}, bf16[48,1536]{1,0:T(8,128)(2,1)S(1)}, u32[]{:S(2)}, u32[]{:S(2)}) collective-permute-start(bf16[48,1536]{1,0:T(8,128)(2,1)S(1)} %pad.12), channel_id=1, source_target_pairs={{0,2},{2,0},{1,3},{3,1},{4,6},{6,4},{5,7},{7,5},{8,10},{10,8},{9,1... | collective-permute-start | bytes 442376 | tf_op jit(solution)/shard_map/ppermute | solution.py:311
  13.1 4.0 %collective-permute-done = bf16[48,1536]{1,0:T(8,128)(2,1)S(1)} collective-permute-done((bf16[48,1536]{1,0:T(8,128)(2,1)S(1)}, bf16[48,1536]{1,0:T(8,128)(2,1)S(1)}, u32[]{:S(2)}, u32[]{:S(2)}) %collective-permute-start) | collective-permute-done | bytes 147488 | tf_op jit(solution)/shard_map/ppermute | solution.py:311
  17.2 1.0 broadcast_select_fusion.3
  18.1 0.7 pad_maximum_fusion
  18.9 0.7 broadcast_in_dim.10
  19.6 0.7 broadcast_in_dim_reshape.4.held_ref
  20.3 0.9 pad.14
  21.3 1.3 convert_bitcast_fusion.gate_ref
  22.5 0.7 compare_select_fusion.place_ref
  23.3 3.4 %shard_map.163 = (bf16[128,3072]{1,0:T(8,128)(2,1)}, bf16[128,128]{1,0:T(8,128)(2,1)}) custom-call(s32[4,128]{1,0:T(4,128)} %bitcast.53, s32[128,1]{1,0:T(8,128)} %broadcast_in_dim_reshape.4.held_ref, f32[4,128]{1,0:T(4,128)} %convert_bitcast_fusion.gate_ref, s32[1,1536]{1,0:T(1,128)} %compare_select_fusion.place_ref, bf16[1440,128]{1,0:T(8,128)(2,1)} %bitcast.50, ...), custom_call_target="tpu_custom_call" | custom-call | bytes 7380000 | tf_op jit(solution)/shard_map/pallas_call | solution.py:348
  26.6 8.7 %all-to-all-start = ((bf16[16,8,3072]{2,1,0:T(8,128)(2,1)}), bf16[16,8,3072]{2,1,0:T(8,128)(2,1)S(1)}, u32[]{:S(2)}, u32[]{:S(2)}) async-start(bf16[16,8,3072]{2,1,0:T(8,128)(2,1)} %bitcast.47), calls=%async_computation | async-start | bytes 1572864 | tf_op jit(solution)/shard_map/all_to_all | solution.py:356
  35.4 4.3 %collective-permute-start.4 = (bf16[64,1536]{1,0:T(8,128)(2,1)S(1)}, bf16[64,1536]{1,0:T(8,128)(2,1)S(1)}, u32[]{:S(2)}, u32[]{:S(2)}) collective-permute-start(bf16[64,1536]{1,0:T(8,128)(2,1)S(1)} %pad.14), channel_id=1, source_target_pairs={{0,2},{2,0},{1,3},{3,1},{4,6},{6,4},{5,7},{7,5},{8,10},{10,8},{9,1... | collective-permute-start | bytes 589832 | tf_op jit(solution)/shard_map/ppermute | solution.py:311
  39.7 5.3 %collective-permute-done.4 = bf16[64,1536]{1,0:T(8,128)(2,1)S(1)} collective-permute-done((bf16[64,1536]{1,0:T(8,128)(2,1)S(1)}, bf16[64,1536]{1,0:T(8,128)(2,1)S(1)}, u32[]{:S(2)}, u32[]{:S(2)}) %collective-permute-start.4) | collective-permute-done | bytes 196640 | tf_op jit(solution)/shard_map/ppermute | solution.py:311
  45.1 0.7 copy-done.3
  46.6 1.9 collective-permute-start.2
  48.5 4.1 %collective-permute-start.1 = (bf16[128,640]{1,0:T(8,128)(2,1)S(1)}, bf16[128,640]{1,0:T(8,128)(2,1)S(1)}, u32[]{:S(2)}, u32[]{:S(2)}) collective-permute-start(bf16[128,640]{1,0:T(8,128)(2,1)S(1)} %fusion.3.own_ref), channel_id=1, source_target_pairs={{0,2},{1,3},{2,4},{3,5},{4,6},{5,7},{6,8},{7,9},{8,10},{9,11},{10,... | collective-permute-start | bytes 491528 | tf_op jit(solution)/shard_map/ppermute | solution.py:322
  52.6 12.7 %collective-permute-done.2.near_ref = bf16[128,640]{1,0:T(8,128)(2,1)S(1)} collective-permute-done((bf16[128,640]{1,0:T(8,128)(2,1)S(1)}, bf16[128,640]{1,0:T(8,128)(2,1)S(1)}, u32[]{:S(2)}, u32[]{:S(2)}) %collective-permute-start.2) | collective-permute-done | bytes 163872 | tf_op jit(solution)/shard_map/ppermute | solution.py:322
  65.3 1.6 collective-permute-done.1.far_ref
  67.6 9.7 %shard_map.164 = (bf16[384,4096]{1,0:T(8,128)(2,1)}, bf16[2048,128]{1,0:T(8,128)(2,1)}, bf16[256,384]{1,0:T(8,128)(2,1)}, bf16[384,256]{1,0:T(8,128)(2,1)}) custom-call(bf16[128,2048]{1,0:T(8,128)(2,1)} %q_ref.1, bf16[128,640]{1,0:T(8,128)(2,1)} %copy-done.7, bf16[128,640]{1,0:T(8,128)(2,1)} %copy-done.6, bf16[128,640]{1,0:T(8,128)(2,1)} %copy-done.4, ...), custom_call_target="tpu_custom_call" | custom-call | bytes 29520000 | tf_op jit(solution)/shard_map/pallas_call | solution.py:362
  77.3 2.7 %collective-permute-start.3 = (bf16[128,3072]{1,0:T(8,128)(2,1)S(1)}, bf16[128,3072]{1,0:T(8,128)(2,1)}, u32[]{:S(2)}, u32[]{:S(2)}) collective-permute-start(bf16[128,3072]{1,0:T(8,128)(2,1)S(1)} %bitcast.42), channel_id=1, source_target_pairs={{0,1},{1,0},{2,3},{3,2},{4,5},{5,4},{6,7},{7,6},{8,9},{9,8},{10,11... | collective-permute-start | bytes 2359304 | tf_op jit(solution)/shard_map/ppermute | solution.py:380
  80.0 2.0 %collective-permute-done.3.got2_ref = bf16[128,3072]{1,0:T(8,128)(2,1)} collective-permute-done((bf16[128,3072]{1,0:T(8,128)(2,1)S(1)}, bf16[128,3072]{1,0:T(8,128)(2,1)}, u32[]{:S(2)}, u32[]{:S(2)}) %collective-permute-start.3) | collective-permute-done | bytes 786464 | tf_op jit(solution)/shard_map/ppermute | solution.py:380
  82.0 2.3 %collective-permute-start.5 = (bf16[768,1536]{1,0:T(8,128)(2,1)}, bf16[768,1536]{1,0:T(8,128)(2,1)S(1)}, u32[]{:S(2)}, u32[]{:S(2)}) collective-permute-start(bf16[768,1536]{1,0:T(8,128)(2,1)} %all-gather.3.cloned.1.call-done.wm_any), channel_id=1, source_target_pairs={{0,1},{1,0},{2,3},{3,2},{4,5},{5,4},{6,7},{7,6},{8,9},{9,8},{10,11... | collective-permute-start | bytes 7077896 | tf_op jit(solution)/shard_map/ppermute | solution.py:384
  84.3 4.3 %collective-permute-done.5.wo_any = bf16[768,1536]{1,0:T(8,128)(2,1)S(1)} collective-permute-done((bf16[768,1536]{1,0:T(8,128)(2,1)}, bf16[768,1536]{1,0:T(8,128)(2,1)S(1)}, u32[]{:S(2)}, u32[]{:S(2)}) %collective-permute-start.5) | collective-permute-done | bytes 2359328 | tf_op jit(solution)/shard_map/ppermute | solution.py:384
  88.7 1.4 copy-done.1
  90.1 8.4 %shard_map.165 = (bf16[128,1664]{1,0:T(8,128)(2,1)}, bf16[768,1536]{1,0:T(8,128)(2,1)}) custom-call(bf16[128,3072]{1,0:T(8,128)(2,1)} %bitcast.43, bf16[128,3072]{1,0:T(8,128)(2,1)} %collective-permute-done.3.got2_ref, bf16[768,1536]{1,0:T(8,128)(2,1)} %all-gather.3.cloned.1.call-done.wm_any, bf16[768,1536]{1,0:T(8,128)(2,1)} %copy-done.1), custom_call_target="tpu_custom_call" | custom-call | bytes 11070000 | tf_op jit(solution)/shard_map/pallas_call | solution.py:385
  98.5 1.1 fusion.1
  99.6 4.6 %collective-permute-start.6 = (bf16[8,1,8,1664]{3,2,1,0:T(8,128)(2,1)S(1)}, bf16[8,1,8,1664]{3,2,1,0:T(8,128)(2,1)S(1)}, u32[]{:S(2)}, u32[]{:S(2)}) collective-permute-start(bf16[8,1,8,1664]{3,2,1,0:T(8,128)(2,1)S(1)} %fusion.1), channel_id=1, source_target_pairs={{0,32},{32,0},{1,33},{33,1},{2,34},{34,2},{3,35},{35,3},{4,36},{36... | collective-permute-start | bytes 638984 | tf_op jit(solution)/shard_map/ppermute | solution.py:300
  104.2 6.8 %all-to-all-start.1 = ((bf16[16,48,1536]{2,1,0:T(8,128)(2,1)}), bf16[16,48,1536]{2,1,0:T(8,128)(2,1)S(1)}, u32[]{:S(2)}, u32[]{:S(2)}) async-start(bf16[16,48,1536]{2,1,0:T(8,128)(2,1)} %bitcast.44), calls=%async_computation.1 | async-start | bytes 4718592 | tf_op jit(solution)/shard_map/all_to_all | solution.py:401
  111.2 0.7 fusion.11
  111.9 3.4 %collective-permute-start.13 = (bf16[16,1664]{1,0:T(8,128)(2,1)S(1)}, bf16[16,1664]{1,0:T(8,128)(2,1)S(1)}, u32[]{:S(2)}, u32[]{:S(2)}) collective-permute-start(bf16[16,1664]{1,0:T(8,128)(2,1)S(1)} %get-tuple-element.50), channel_id=1, source_target_pairs={{0,64},{64,128},{128,192},{192,256},{256,320},{320,384},{384,448},... | collective-permute-start | bytes 159752 | tf_op jit(solution)/shard_map/ppermute | solution.py:306
  115.3 2.4 %collective-permute-start.7 = (bf16[16,1664]{1,0:T(8,128)(2,1)S(1)}, bf16[16,1664]{1,0:T(8,128)(2,1)S(1)}, u32[]{:S(2)}, u32[]{:S(2)}) collective-permute-start(bf16[16,1664]{1,0:T(8,128)(2,1)S(1)} %get-tuple-element.52), channel_id=1, source_target_pairs={{0,448},{64,0},{128,64},{192,128},{256,192},{320,256},{384,320},{4... | collective-permute-start | bytes 159752 | tf_op jit(solution)/shard_map/ppermute | solution.py:306
  117.7 3.7 %collective-permute-start.8 = (bf16[16,1664]{1,0:T(8,128)(2,1)S(1)}, bf16[16,1664]{1,0:T(8,128)(2,1)S(1)}, u32[]{:S(2)}, u32[]{:S(2)}) collective-permute-start(bf16[16,1664]{1,0:T(8,128)(2,1)S(1)} %get-tuple-element.53), channel_id=1, source_target_pairs={{0,384},{64,448},{128,0},{192,64},{256,128},{320,192},{384,256},{4... | collective-permute-start | bytes 159752 | tf_op jit(solution)/shard_map/ppermute | solution.py:306
  121.4 5.2 %collective-permute-start.9 = (bf16[16,1664]{1,0:T(8,128)(2,1)S(1)}, bf16[16,1664]{1,0:T(8,128)(2,1)S(1)}, u32[]{:S(2)}, u32[]{:S(2)}) collective-permute-start(bf16[16,1664]{1,0:T(8,128)(2,1)S(1)} %get-tuple-element.54), channel_id=1, source_target_pairs={{0,320},{64,384},{128,448},{192,0},{256,64},{320,128},{384,192},{4... | collective-permute-start | bytes 159752 | tf_op jit(solution)/shard_map/ppermute | solution.py:306
  126.6 4.1 %collective-permute-start.10 = (bf16[16,1664]{1,0:T(8,128)(2,1)S(1)}, bf16[16,1664]{1,0:T(8,128)(2,1)S(1)}, u32[]{:S(2)}, u32[]{:S(2)}) collective-permute-start(bf16[16,1664]{1,0:T(8,128)(2,1)S(1)} %get-tuple-element.55), channel_id=1, source_target_pairs={{0,256},{64,320},{128,384},{192,448},{256,0},{320,64},{384,128},{4... | collective-permute-start | bytes 159752 | tf_op jit(solution)/shard_map/ppermute | solution.py:306
  130.7 6.9 %collective-permute-start.11 = (bf16[16,1664]{1,0:T(8,128)(2,1)S(1)}, bf16[16,1664]{1,0:T(8,128)(2,1)S(1)}, u32[]{:S(2)}, u32[]{:S(2)}) collective-permute-start(bf16[16,1664]{1,0:T(8,128)(2,1)S(1)} %get-tuple-element.56), channel_id=1, source_target_pairs={{0,192},{64,256},{128,320},{192,384},{256,448},{320,0},{384,64},{4... | collective-permute-start | bytes 159752 | tf_op jit(solution)/shard_map/ppermute | solution.py:306
  137.7 1.9 collective-permute-start.12
  139.6 1.8 all-gather.5.cloned.1.call-done.om_any
  141.5 3.2 %collective-permute-done.12.p6 = bf16[16,1664]{1,0:T(8,128)(2,1)S(1)} collective-permute-done((bf16[16,1664]{1,0:T(8,128)(2,1)S(1)}, bf16[16,1664]{1,0:T(8,128)(2,1)S(1)}, u32[]{:S(2)}, u32[]{:S(2)}) %collective-permute-start.12) | collective-permute-done | bytes 53280 | tf_op jit(solution)/shard_map/ppermute | solution.py:306
  144.6 2.1 %collective-permute-start.14 = (bf16[1024,1536]{1,0:T(8,128)(2,1)}, bf16[1024,1536]{1,0:T(8,128)(2,1)}, u32[]{:S(2)}, u32[]{:S(2)}) collective-permute-start(bf16[1024,1536]{1,0:T(8,128)(2,1)} %all-gather.5.cloned.1.call-done.om_any), channel_id=1, source_target_pairs={{0,1},{1,0},{2,3},{3,2},{4,5},{5,4},{6,7},{7,6},{8,9},{9,8},{10,11... | collective-permute-start | bytes 9437192 | tf_op jit(solution)/shard_map/ppermute | solution.py:406
  146.7 0.7 pad_add_fusion.at_ref
  147.4 5.1 %collective-permute-done.14.oo_any = bf16[1024,1536]{1,0:T(8,128)(2,1)} collective-permute-done((bf16[1024,1536]{1,0:T(8,128)(2,1)}, bf16[1024,1536]{1,0:T(8,128)(2,1)}, u32[]{:S(2)}, u32[]{:S(2)}) %collective-permute-start.14) | collective-permute-done | bytes 3145760 | tf_op jit(solution)/shard_map/ppermute | solution.py:406
  152.6 15.5 %shard_map.166 = (bf16[1440,128]{1,0:T(8,128)(2,1)}, f32[4,128]{1,0:T(4,128)}, bf16[384,4096]{1,0:T(8,128)(2,1)}, bf16[128,512]{1,0:T(8,128)(2,1)}, bf16[128,512]{1,0:T(8,128)(2,1)}, /*index=5*/f32[128,512]{1,0:T(8,128)}) custom-call(s32[3]{0:T(128)} %pad_add_fusion.at_ref, s32[4,128]{1,0:T(4,128)} %bitcast.54, s32[128,1]{1,0:T(8,128)} %broadcast_in_dim_reshape.4.held_ref, ...), custom_call_target="tpu_custom_call" | custom-call | bytes 369000 | tf_op jit(solution)/shard_map/pallas_call | solution.py:407
  168.1 8.6 %collective-permute-start.15 = (bf16[128,512]{1,0:T(8,128)(2,1)}, bf16[128,512]{1,0:T(8,128)(2,1)S(1)}, u32[]{:S(2)}, u32[]{:S(2)}) collective-permute-start(bf16[128,512]{1,0:T(8,128)(2,1)} %get-tuple-element.41), channel_id=1, source_target_pairs={{1,0},{2,1},{3,2},{4,3},{5,4},{6,5},{7,6},{8,7},{9,8},{10,9},{11,1... | collective-permute-start | bytes 393224 | tf_op jit(solution)/shard_map/ppermute | solution.py:322
  176.6 2.5 %collective-permute-start.16 = (bf16[128,512]{1,0:T(8,128)(2,1)}, bf16[128,512]{1,0:T(8,128)(2,1)S(1)}, u32[]{:S(2)}, u32[]{:S(2)}) collective-permute-start(bf16[128,512]{1,0:T(8,128)(2,1)} %get-tuple-element.42), channel_id=1, source_target_pairs={{2,0},{3,1},{4,2},{5,3},{6,4},{7,5},{8,6},{9,7},{10,8},{11,9},{12,... | collective-permute-start | bytes 393224 | tf_op jit(solution)/shard_map/ppermute | solution.py:322
  179.1 3.5 %shard_map.167 = bf16[128,2048]{1,0:T(8,128)(2,1)} custom-call(bf16[384,4096]{1,0:T(8,128)(2,1)} %get-tuple-element.38.sg_ref, bf16[256,384]{1,0:T(8,128)(2,1)} %get-tuple-element.39.kt_ref), custom_call_target="tpu_custom_call" | custom-call | bytes 369000 | tf_op jit(solution)/shard_map/pallas_call | solution.py:441
  183.1 2.0 %collective-permute-done.16 = bf16[128,512]{1,0:T(8,128)(2,1)S(1)} collective-permute-done((bf16[128,512]{1,0:T(8,128)(2,1)}, bf16[128,512]{1,0:T(8,128)(2,1)S(1)}, u32[]{:S(2)}, u32[]{:S(2)}) %collective-permute-start.16) | collective-permute-done | bytes 131104 | tf_op jit(solution)/shard_map/ppermute | solution.py:322
  186.2 0.7 slice_bitcast_fusion
  (63 shorter events, 3.3 us)
Async XLA Ops:
  7.2 38.7 %copy-start.18 = (s32[128]{0:T(128)S(1)}, s32[128]{0:T(128)}, u32[]{:S(2)}) copy-start(s32[128]{0:T(128)} %param.15) | copy-start | bytes 1540
  7.2 39.4 %copy-start.8 = (bf16[128,256]{1,0:T(8,128)(2,1)S(1)}, bf16[128,256]{1,0:T(8,128)(2,1)}, u32[]{:S(2)}) copy-start(bf16[128,256]{1,0:T(8,128)(2,1)} %param.14) | copy-start | bytes 196612
  7.2 39.4 %copy-start.9 = (bf16[128,256]{1,0:T(8,128)(2,1)S(1)}, bf16[128,256]{1,0:T(8,128)(2,1)}, u32[]{:S(2)}) copy-start(bf16[128,256]{1,0:T(8,128)(2,1)} %param.13) | copy-start | bytes 196612
  7.2 74.8 %all-gather.3.cloned.1.call-start = ((), (), s32[]{:S(2)}) async-start(), calls=%async_computation.2 | async-start | bytes 2654208 | tf_op jit(solution)/shard_map/all_gather | solution.py:331
  8.2 9.0 %collective-permute-start = (bf16[48,1536]{1,0:T(8,128)(2,1)S(1)}, bf16[48,1536]{1,0:T(8,128)(2,1)S(1)}, u32[]{:S(2)}, u32[]{:S(2)}) collective-permute-start(bf16[48,1536]{1,0:T(8,128)(2,1)S(1)} %pad.12), channel_id=1, source_target_pairs={{0,2},{2,0},{1,3},{3,1},{4,6},{6,4},{5,7},{7,5},{8,10},{10,8},{9,1... | collective-permute-start | bytes 442376 | tf_op jit(solution)/shard_map/ppermute | solution.py:311
  26.6 50.6 %all-to-all-start = ((bf16[16,8,3072]{2,1,0:T(8,128)(2,1)}), bf16[16,8,3072]{2,1,0:T(8,128)(2,1)S(1)}, u32[]{:S(2)}, u32[]{:S(2)}) async-start(bf16[16,8,3072]{2,1,0:T(8,128)(2,1)} %bitcast.47), calls=%async_computation | async-start | bytes 1572864 | tf_op jit(solution)/shard_map/all_to_all | solution.py:356
  35.3 106.1 %all-gather.5.cloned.1.call-start = ((), (), s32[]{:S(2)}) async-start(), calls=%async_computation.3 | async-start | bytes 3538944 | tf_op jit(solution)/shard_map/all_gather | solution.py:382
  35.4 9.7 %collective-permute-start.4 = (bf16[64,1536]{1,0:T(8,128)(2,1)S(1)}, bf16[64,1536]{1,0:T(8,128)(2,1)S(1)}, u32[]{:S(2)}, u32[]{:S(2)}) collective-permute-start(bf16[64,1536]{1,0:T(8,128)(2,1)S(1)} %pad.14), channel_id=1, source_target_pairs={{0,2},{2,0},{1,3},{3,1},{4,6},{6,4},{5,7},{7,5},{8,10},{10,8},{9,1... | collective-permute-start | bytes 589832 | tf_op jit(solution)/shard_map/ppermute | solution.py:311
  45.1 0.7 copy-start.3
  46.6 20.3 %copy-start.4 = (bf16[128,640]{1,0:T(8,128)(2,1)}, bf16[128,640]{1,0:T(8,128)(2,1)S(1)}, u32[]{:S(2)}) copy-start(bf16[128,640]{1,0:T(8,128)(2,1)S(1)} %fusion.3.own_ref) | copy-start | bytes 491524
  46.6 18.7 %collective-permute-start.2 = (bf16[128,640]{1,0:T(8,128)(2,1)S(1)}, bf16[128,640]{1,0:T(8,128)(2,1)S(1)}, u32[]{:S(2)}, u32[]{:S(2)}) collective-permute-start(bf16[128,640]{1,0:T(8,128)(2,1)S(1)} %fusion.3.own_ref), channel_id=1, source_target_pairs={{0,1},{1,2},{2,3},{3,4},{4,5},{5,6},{6,7},{7,8},{8,9},{9,10},{10,1... | collective-permute-start | bytes 491528 | tf_op jit(solution)/shard_map/ppermute | solution.py:322
  48.5 18.4 %collective-permute-start.1 = (bf16[128,640]{1,0:T(8,128)(2,1)S(1)}, bf16[128,640]{1,0:T(8,128)(2,1)S(1)}, u32[]{:S(2)}, u32[]{:S(2)}) collective-permute-start(bf16[128,640]{1,0:T(8,128)(2,1)S(1)} %fusion.3.own_ref), channel_id=1, source_target_pairs={{0,2},{1,3},{2,4},{3,5},{4,6},{5,7},{6,8},{7,9},{8,10},{9,11},{10,... | collective-permute-start | bytes 491528 | tf_op jit(solution)/shard_map/ppermute | solution.py:322
  65.3 1.6 copy-start.6
  66.9 0.7 copy-start.7
  77.3 11.4 %copy-start = (bf16[16,8,3072]{2,1,0:T(8,128)(2,1)}, bf16[16,8,3072]{2,1,0:T(8,128)(2,1)S(1)}, u32[]{:S(2)}) copy-start(bf16[16,8,3072]{2,1,0:T(8,128)(2,1)S(1)} %all-to-all-done) | copy-start | bytes 2359300
  77.3 4.8 %collective-permute-start.3 = (bf16[128,3072]{1,0:T(8,128)(2,1)S(1)}, bf16[128,3072]{1,0:T(8,128)(2,1)}, u32[]{:S(2)}, u32[]{:S(2)}) collective-permute-start(bf16[128,3072]{1,0:T(8,128)(2,1)S(1)} %bitcast.42), channel_id=1, source_target_pairs={{0,1},{1,0},{2,3},{3,2},{4,5},{5,4},{6,7},{7,6},{8,9},{9,8},{10,11... | collective-permute-start | bytes 2359304 | tf_op jit(solution)/shard_map/ppermute | solution.py:380
  82.0 6.6 %collective-permute-start.5 = (bf16[768,1536]{1,0:T(8,128)(2,1)}, bf16[768,1536]{1,0:T(8,128)(2,1)S(1)}, u32[]{:S(2)}, u32[]{:S(2)}) collective-permute-start(bf16[768,1536]{1,0:T(8,128)(2,1)} %all-gather.3.cloned.1.call-done.wm_any), channel_id=1, source_target_pairs={{0,1},{1,0},{2,3},{3,2},{4,5},{5,4},{6,7},{7,6},{8,9},{9,8},{10,11... | collective-permute-start | bytes 7077896 | tf_op jit(solution)/shard_map/ppermute | solution.py:384
  88.7 1.4 copy-start.1
  98.5 12.6 %copy-start.2 = (bf16[128,1664]{1,0:T(8,128)(2,1)S(1)}, bf16[128,1664]{1,0:T(8,128)(2,1)}, u32[]{:S(2)}) copy-start(bf16[128,1664]{1,0:T(8,128)(2,1)} %get-tuple-element.33) | copy-start | bytes 1277956
  99.6 11.5 %collective-permute-start.6 = (bf16[8,1,8,1664]{3,2,1,0:T(8,128)(2,1)S(1)}, bf16[8,1,8,1664]{3,2,1,0:T(8,128)(2,1)S(1)}, u32[]{:S(2)}, u32[]{:S(2)}) collective-permute-start(bf16[8,1,8,1664]{3,2,1,0:T(8,128)(2,1)S(1)} %fusion.1), channel_id=1, source_target_pairs={{0,32},{32,0},{1,33},{33,1},{2,34},{34,2},{3,35},{35,3},{4,36},{36... | collective-permute-start | bytes 638984 | tf_op jit(solution)/shard_map/ppermute | solution.py:300
  104.2 81.7 %all-to-all-start.1 = ((bf16[16,48,1536]{2,1,0:T(8,128)(2,1)}), bf16[16,48,1536]{2,1,0:T(8,128)(2,1)S(1)}, u32[]{:S(2)}, u32[]{:S(2)}) async-start(bf16[16,48,1536]{2,1,0:T(8,128)(2,1)} %bitcast.44), calls=%async_computation.1 | async-start | bytes 4718592 | tf_op jit(solution)/shard_map/all_to_all | solution.py:401
  111.9 18.8 %collective-permute-start.13 = (bf16[16,1664]{1,0:T(8,128)(2,1)S(1)}, bf16[16,1664]{1,0:T(8,128)(2,1)S(1)}, u32[]{:S(2)}, u32[]{:S(2)}) collective-permute-start(bf16[16,1664]{1,0:T(8,128)(2,1)S(1)} %get-tuple-element.50), channel_id=1, source_target_pairs={{0,64},{64,128},{128,192},{192,256},{256,320},{320,384},{384,448},... | collective-permute-start | bytes 159752 | tf_op jit(solution)/shard_map/ppermute | solution.py:306
  115.3 22.4 %collective-permute-start.7 = (bf16[16,1664]{1,0:T(8,128)(2,1)S(1)}, bf16[16,1664]{1,0:T(8,128)(2,1)S(1)}, u32[]{:S(2)}, u32[]{:S(2)}) collective-permute-start(bf16[16,1664]{1,0:T(8,128)(2,1)S(1)} %get-tuple-element.52), channel_id=1, source_target_pairs={{0,448},{64,0},{128,64},{192,128},{256,192},{320,256},{384,320},{4... | collective-permute-start | bytes 159752 | tf_op jit(solution)/shard_map/ppermute | solution.py:306
  117.7 23.7 %collective-permute-start.8 = (bf16[16,1664]{1,0:T(8,128)(2,1)S(1)}, bf16[16,1664]{1,0:T(8,128)(2,1)S(1)}, u32[]{:S(2)}, u32[]{:S(2)}) collective-permute-start(bf16[16,1664]{1,0:T(8,128)(2,1)S(1)} %get-tuple-element.53), channel_id=1, source_target_pairs={{0,384},{64,448},{128,0},{192,64},{256,128},{320,192},{384,256},{4... | collective-permute-start | bytes 159752 | tf_op jit(solution)/shard_map/ppermute | solution.py:306
  121.4 20.0 %collective-permute-start.9 = (bf16[16,1664]{1,0:T(8,128)(2,1)S(1)}, bf16[16,1664]{1,0:T(8,128)(2,1)S(1)}, u32[]{:S(2)}, u32[]{:S(2)}) collective-permute-start(bf16[16,1664]{1,0:T(8,128)(2,1)S(1)} %get-tuple-element.54), channel_id=1, source_target_pairs={{0,320},{64,384},{128,448},{192,0},{256,64},{320,128},{384,192},{4... | collective-permute-start | bytes 159752 | tf_op jit(solution)/shard_map/ppermute | solution.py:306
  126.6 14.8 %collective-permute-start.10 = (bf16[16,1664]{1,0:T(8,128)(2,1)S(1)}, bf16[16,1664]{1,0:T(8,128)(2,1)S(1)}, u32[]{:S(2)}, u32[]{:S(2)}) collective-permute-start(bf16[16,1664]{1,0:T(8,128)(2,1)S(1)} %get-tuple-element.55), channel_id=1, source_target_pairs={{0,256},{64,320},{128,384},{192,448},{256,0},{320,64},{384,128},{4... | collective-permute-start | bytes 159752 | tf_op jit(solution)/shard_map/ppermute | solution.py:306
  130.7 21.8 %copy-start.10 = (bf16[16,1664]{1,0:T(8,128)(2,1)}, bf16[16,1664]{1,0:T(8,128)(2,1)S(1)}, u32[]{:S(2)}) copy-start(bf16[16,1664]{1,0:T(8,128)(2,1)S(1)} %collective-permute-done.13.p7) | copy-start | bytes 159748
  130.7 10.7 %collective-permute-start.11 = (bf16[16,1664]{1,0:T(8,128)(2,1)S(1)}, bf16[16,1664]{1,0:T(8,128)(2,1)S(1)}, u32[]{:S(2)}, u32[]{:S(2)}) collective-permute-start(bf16[16,1664]{1,0:T(8,128)(2,1)S(1)} %get-tuple-element.56), channel_id=1, source_target_pairs={{0,192},{64,256},{128,320},{192,384},{256,448},{320,0},{384,64},{4... | collective-permute-start | bytes 159752 | tf_op jit(solution)/shard_map/ppermute | solution.py:306
  137.7 14.8 %copy-start.11 = (bf16[16,1664]{1,0:T(8,128)(2,1)}, bf16[16,1664]{1,0:T(8,128)(2,1)S(1)}, u32[]{:S(2)}) copy-start(bf16[16,1664]{1,0:T(8,128)(2,1)S(1)} %collective-permute-done.7.p1) | copy-start | bytes 159748
  137.7 6.9 %collective-permute-start.12 = (bf16[16,1664]{1,0:T(8,128)(2,1)S(1)}, bf16[16,1664]{1,0:T(8,128)(2,1)S(1)}, u32[]{:S(2)}, u32[]{:S(2)}) collective-permute-start(bf16[16,1664]{1,0:T(8,128)(2,1)S(1)} %get-tuple-element.57), channel_id=1, source_target_pairs={{0,128},{64,192},{128,256},{192,320},{256,384},{320,448},{384,0},{... | collective-permute-start | bytes 159752 | tf_op jit(solution)/shard_map/ppermute | solution.py:306
  141.4 11.1 %copy-start.12 = (bf16[16,1664]{1,0:T(8,128)(2,1)}, bf16[16,1664]{1,0:T(8,128)(2,1)S(1)}, u32[]{:S(2)}) copy-start(bf16[16,1664]{1,0:T(8,128)(2,1)S(1)} %collective-permute-done.8.p2) | copy-start | bytes 159748
  141.4 11.1 %copy-start.13 = (bf16[16,1664]{1,0:T(8,128)(2,1)}, bf16[16,1664]{1,0:T(8,128)(2,1)S(1)}, u32[]{:S(2)}) copy-start(bf16[16,1664]{1,0:T(8,128)(2,1)S(1)} %collective-permute-done.9.p3) | copy-start | bytes 159748
  141.4 11.1 %copy-start.14 = (bf16[16,1664]{1,0:T(8,128)(2,1)}, bf16[16,1664]{1,0:T(8,128)(2,1)S(1)}, u32[]{:S(2)}) copy-start(bf16[16,1664]{1,0:T(8,128)(2,1)S(1)} %collective-permute-done.10.p4) | copy-start | bytes 159748
  141.4 11.1 %copy-start.15 = (bf16[16,1664]{1,0:T(8,128)(2,1)}, bf16[16,1664]{1,0:T(8,128)(2,1)S(1)}, u32[]{:S(2)}) copy-start(bf16[16,1664]{1,0:T(8,128)(2,1)S(1)} %collective-permute-done.11.p5) | copy-start | bytes 159748
  144.6 7.9 %copy-start.16 = (bf16[16,1664]{1,0:T(8,128)(2,1)}, bf16[16,1664]{1,0:T(8,128)(2,1)S(1)}, u32[]{:S(2)}) copy-start(bf16[16,1664]{1,0:T(8,128)(2,1)S(1)} %collective-permute-done.12.p6) | copy-start | bytes 159748
  144.6 7.9 %collective-permute-start.14 = (bf16[1024,1536]{1,0:T(8,128)(2,1)}, bf16[1024,1536]{1,0:T(8,128)(2,1)}, u32[]{:S(2)}, u32[]{:S(2)}) collective-permute-start(bf16[1024,1536]{1,0:T(8,128)(2,1)} %all-gather.5.cloned.1.call-done.om_any), channel_id=1, source_target_pairs={{0,1},{1,0},{2,3},{3,2},{4,5},{5,4},{6,7},{7,6},{8,9},{9,8},{10,11... | collective-permute-start | bytes 9437192 | tf_op jit(solution)/shard_map/ppermute | solution.py:406
  168.0 14.5 %copy-start.17 = (f32[4,128]{1,0:T(4,128)S(1)}, f32[4,128]{1,0:T(4,128)}, u32[]{:S(2)}) copy-start(f32[4,128]{1,0:T(4,128)} %get-tuple-element.44) | copy-start | bytes 6148
  168.0 17.1 %copy-start.5 = (f32[128,512]{1,0:T(8,128)S(1)}, f32[128,512]{1,0:T(8,128)}, u32[]{:S(2)}) copy-start(f32[128,512]{1,0:T(8,128)} %get-tuple-element.40) | copy-start | bytes 786436
  168.1 15.1 %collective-permute-start.15 = (bf16[128,512]{1,0:T(8,128)(2,1)}, bf16[128,512]{1,0:T(8,128)(2,1)S(1)}, u32[]{:S(2)}, u32[]{:S(2)}) collective-permute-start(bf16[128,512]{1,0:T(8,128)(2,1)} %get-tuple-element.41), channel_id=1, source_target_pairs={{1,0},{2,1},{3,2},{4,3},{5,4},{6,5},{7,6},{8,7},{9,8},{10,9},{11,1... | collective-permute-start | bytes 393224 | tf_op jit(solution)/shard_map/ppermute | solution.py:322
  176.6 8.6 %collective-permute-start.16 = (bf16[128,512]{1,0:T(8,128)(2,1)}, bf16[128,512]{1,0:T(8,128)(2,1)S(1)}, u32[]{:S(2)}, u32[]{:S(2)}) collective-permute-start(bf16[128,512]{1,0:T(8,128)(2,1)} %get-tuple-element.42), channel_id=1, source_target_pairs={{2,0},{3,1},{4,2},{5,3},{6,4},{7,5},{8,6},{9,7},{10,8},{11,9},{12,... | collective-permute-start | bytes 393224 | tf_op jit(solution)/shard_map/ppermute | solution.py:322
Sparse Core Ops, SparseCore 0:
  19.0 49.4 all-gather.2
  70.6 70.7 all-gather.4

commit v5 on v4

--- a/solution.py
+++ b/solution.py
@@ -64,7 +64,8 @@
 
 
 def dispatch_kernel(
-    picked_ref, held_ref, gate_ref, place_ref, x_ref, g_ref, out_ref, sent_any, sent_ref, sems
+    picked_ref, held_ref, gate_ref, place_ref, x_ref, g_ref, skip_ref, map_ref,
+    out_ref, map_out, sent_any, skip_any, sent_ref, skip_s, sems,
 ):
     held = held_ref[...]
     chosen = [picked_ref[s : s + 1, :] == held for s in range(4)]
@@ -89,12 +90,18 @@
     feature = lax.broadcasted_iota(jnp.int32, (D, 256), 0)
     for c in range(DP // 256):
         pick = jnp.where(feature == place_ref[:, c * 256 : (c + 1) * 256], 1.0, 0.0).astype(BF)
-        out_ref[:, c * 256 : (c + 1) * 256] = dot(rows, pick, ((1,), (0,))).astype(BF)
+        at = slice(c * 256, (c + 1) * 256)
+        out_ref[:, at] = dot(rows, pick, ((1,), (0,))).astype(BF)
+        map_out[:, at] = dot(map_ref[...], pick, ((1,), (0,))).astype(BF)
+        skip_s[:, at] = dot(skip_ref[...], pick, ((0,), (0,))).astype(BF)
+    skip_copy = pltpu.make_async_copy(skip_s, skip_any, sems.at[1])
+    skip_copy.start()
     grads = dot(sent_bf, g_ref[...], ((1,), (1,))).astype(BF)
     out_ref[:, DP:] = jnp.concatenate(
         [grads, jnp.broadcast_to(gate, (ROWS, SEND - DP - F)).astype(BF)], axis=1
     )
     copy.wait()
+    skip_copy.wait()
 
 
 def shares_kernel(
@@ -147,16 +154,14 @@
 
 
 def expert_kernel(
-    got_ref, got2_ref, wm_any, wo_any, back_any, part_any,
-    wm_ref, wo_ref, back_ref, pg_ref, pre_ref, part_ref, sems,
+    got_ref, got2_ref, wo_ref, wm_any, back_any, part_any,
+    wm_ref, back_ref, pg_ref, pre_ref, part_ref, sems,
 ):
-    loads = copies_of(((wm_any, wm_ref), (wo_any, wo_ref)), sems)
-    for copy in loads:
-        copy.start()
+    load = pltpu.make_async_copy(wm_any, wm_ref, sems.at[0])
+    load.start()
     x_mine = jnp.concatenate([got_ref[:, :HALF], got2_ref[:, HALF:DP]], axis=0)
     x_other = jnp.concatenate([got_ref[:, HALF:DP], got2_ref[:, :HALF]], axis=0)
-    for copy in loads:
-        copy.wait()
+    load.wait()
     step = 512
     for lo in range(0, DP, step):
         at = slice(lo, lo + step)
@@ -197,22 +202,20 @@
         copy.wait()
 
 
-def late_kernel(
-    at_ref, picked_ref, held_ref, place_ref,
-    p0, p1, p2, p3, p4, p5, p6, p7, sent_any, v_any, skip_any, om_any, oo_any, qt_any, shares_any,
-    src_ref, gate_ref, sg_ref, farg_ref, nearg_ref, owng_ref,
-    hidden_s, cot_s, acck_s, accv_s, back_ref,
-    sent_ref, v_ref, skip_ref, om_ref, oo_ref, qt_ref, shares_ref, sems,
+def combine_kernel(
+    at_ref, picked_ref, held_ref, back_any, sent_any, skip_any, om_any,
+    gate_ref, src_ref, hidden_ref, cot_ref, back_ref, sent_ref, skip_ref, om_ref, sems,
 ):
-    pairs = (
-        (sent_any, sent_ref), (skip_any, skip_ref), (om_any, om_ref), (oo_any, oo_ref),
-        (v_any, v_ref), (qt_any, qt_ref), (shares_any, shares_ref),
-    )
+    pairs = ((sent_any, sent_ref), (skip_any, skip_ref), (om_any, om_ref))
     copies = copies_of(pairs, sems)
     arrived = []
-    for i, piece in enumerate((p0, p1, p2, p3, p4, p5, p6, p7)):
-        rows = pl.ds(pl.multiple_of(((at_ref[2] + i) % 8) * 16, 16), 16)
-        arrived.append(pltpu.make_async_copy(piece, back_ref.at[rows, :], sems.at[7 + i]))
+    for k in range(8):
+        rows = pl.ds(pl.multiple_of(((at_ref[2] + 8 - k) % 8) * 16, 16), 16)
+        arrived.append(
+            pltpu.make_async_copy(
+                back_any.at[k * 16 : (k + 1) * 16, :], back_ref.at[rows, :], sems.at[3 + k]
+            )
+        )
     for copy in arrived + copies:
         copy.start()
     for copy in arrived:
@@ -226,30 +229,42 @@
         mine = (picked_ref[s : s + 1, :] == held) & sent
         gate_ref[s : s + 1, :] = jnp.sum(jnp.where(mine, gate_part, 0.0), axis=0, keepdims=True)
     src = dot(sent_bf, back_ref[:, :DP], ((0,), (0,))).astype(BF)
-    feature = lax.broadcasted_iota(jnp.int32, (D, 256), 0)
-    total = jnp.zeros((D, TOK), F32)
-    for c in range(DP // 256):
-        pick = jnp.where(feature == place_ref[:, c * 256 : (c + 1) * 256], 1.0, 0.0).astype(BF)
-        total = total + dot(pick, src[:, c * 256 : (c + 1) * 256], ((1,), (1,)))
-    src_ref[...] = total.astype(BF)
+    src_ref[...] = src
     copies[1].wait()
-    hidden_s[:D, :] = (skip_ref[...].astype(F32) + total).astype(BF)
-    hidden_s[D:, :] = jnp.zeros((DP - D, TOK), BF)
-
+    hidden = (skip_ref[...].astype(F32) + src.astype(F32)).astype(BF)
+    hidden_ref[...] = hidden
+    copies[2].wait()
+    for c in range(4):
+        rows = slice(c * 256, (c + 1) * 256)
+        cot_ref[rows, :] = dot(om_ref[rows, :], hidden, ((1,), (1,))).astype(BF)
+
+
+def late_kernel(
+    at_ref, cotm_ref, hidden_ref, v_any, oo_any, qt_any, shares_any,
+    sg_ref, farg_ref, nearg_ref, owng_ref,
+    cot_s, acck_s, accv_s, v_ref, oo_ref, qt_ref, shares_ref, sems,
+):
+    pairs = ((oo_any, oo_ref), (v_any, v_ref), (qt_any, qt_ref), (shares_any, shares_ref))
+    copies = copies_of(pairs, sems)
+    for copy in copies:
+        copy.start()
     core, xh = at_ref[0], at_ref[1]
-    for ref, place, copy in (
-        (om_ref, core * HD, copies[2]),
-        (oo_ref, HD - core * HD, copies[3]),
-    ):
-        copy.wait()
-        for c in range(4):
-            block = dot(ref[c * 256 : (c + 1) * 256, :], hidden_s[...], ((1,), (0,))).astype(BF)
-            for j in range(4):
-                across = xh if j % 2 == 0 else 1 - xh
-                at = pl.multiple_of((c * 2 + j // 2) * 256 + across * 128 + place, HD)
-                cot_s[pl.ds(at, HD), :] = block[j * HD : (j + 1) * HD]
-
-    for copy in copies[4:]:
+
+    def spread(block, c, place):
+        for j in range(4):
+            across = xh if j % 2 == 0 else 1 - xh
+            at = pl.multiple_of((c * 2 + j // 2) * 256 + across * 128 + place, HD)
+            cot_s[pl.ds(at, HD), :] = block[j * HD : (j + 1) * HD]
+
+    for c in range(4):
+        spread(cotm_ref[c * 256 : (c + 1) * 256, :], c, core * HD)
+    hidden = jnp.concatenate([hidden_ref[:, HALF:], hidden_ref[:, :HALF]], axis=1)
+    copies[0].wait()
+    for c in range(4):
+        rows = slice(c * 256, (c + 1) * 256)
+        spread(dot(oo_ref[rows, :], hidden, ((1,), (1,))).astype(BF), c, HD - core * HD)
+
+    for copy in copies[1:]:
         copy.wait()
     for t in range(2):
         sums = []
@@ -283,12 +298,19 @@
             owng_ref[:, at] = tile[2 * TOK :]
 
 
-def query_kernel(sg_ref, kt_ref, qg_ref):
+def query_kernel(sg_ref, kt_ref, src_ref, place_ref, qg_ref, out_ref):
     for n in range(16):
         g = n // 4
         qg = dot(kt_ref[g * HD : (g + 1) * HD, :], sg_ref[:, n * 256 : (n + 1) * 256], ((1,), (0,)))
         both = jnp.concatenate([qg[:, :TOK], qg[:, TOK:]], axis=0) * 0.125
         qg_ref[:, n * 128 : (n + 1) * 128] = jnp.transpose(both).astype(BF)
+    feature = lax.broadcasted_iota(jnp.int32, (D, 256), 0)
+    total = jnp.zeros((D, TOK), F32)
+    for c in range(DP // 256):
+        at = slice(c * 256, (c + 1) * 256)
+        pick = jnp.where(feature == place_ref[:, at], 1.0, 0.0).astype(BF)
+        total = total + dot(pick, src_ref[:, at], ((1,), (1,)))
+    out_ref[...] = total.astype(BF)
 
 
 def give_back(back):
@@ -300,17 +322,18 @@
     got = lax.ppermute(give, "xl", SWAP)
     both = jnp.concatenate(
         [jnp.where(xl == 0, keep, got), jnp.where(xl == 0, got, keep)], axis=1
-    ).reshape(8, 2 * CAPP, BACK)
-    pieces = [both[0]]
-    for k in range(7, 0, -1):
-        pieces.append(lax.ppermute(both[k], "y", [(i, (i + k) % 8) for i in range(8)]))
-    return pieces
-
-
-def both_xh(piece, natural):
+    )
+    both = both.reshape(2, 2, 2, 2 * CAPP, BACK)
+    for bit, axis in ((1, 2), (2, 1), (4, 0)):
+        stay = lax.slice_in_dim(both, 0, 1, axis=axis)
+        move = lax.slice_in_dim(both, 1, 2, axis=axis)
+        move = lax.ppermute(move, "y", [(i, (i + bit) % 8) for i in range(8)])
+        both = jnp.concatenate([stay, move], axis=axis)
+    return both.reshape(ROWS, BACK)
+
+
+def both_xh(piece):
     other = lax.ppermute(piece, "xh", SWAP)
-    if not natural:
-        return jnp.concatenate([piece, other], axis=0)
     lower = lax.axis_index("xh") == 0
     return jnp.concatenate(
         [jnp.where(lower, piece, other), jnp.where(lower, other, piece)], axis=0
@@ -326,8 +349,7 @@
     core = lax.axis_index("core")
     xh = lax.axis_index("xh")
     w_pad = jnp.pad(weights[0], ((0, SEG - SHARD), (0, DP - F)))
-    o_pad = jnp.pad(out_map, ((0, 0), (0, DP - D)))
-    w_pair = both_xh(w_pad, True)
+    w_pair = both_xh(w_pad)
     w_mine = lax.all_gather(w_pair, "z", axis=0, tiled=True)
 
     plus = (label + 1).astype(jnp.int32)
@@ -337,26 +359,28 @@
     )
     picked_t = order(picked.T, w_pair)
     held = jnp.repeat(retained[:EXPERTS], CAPP)[:, None]
-    spot = jnp.arange(DP, dtype=jnp.int32)
-    half = spot // HALF
-    rest = spot % HALF
+    column = jnp.arange(DP, dtype=jnp.int32)
+    half = column // HALF
+    rest = column % HALF
     within = rest % SEG
     pair = rest // SEG
     owner = (pair // 2) * 4 + (pair % 2) * 2 + (half ^ core)
     place = jnp.where(within < SHARD, owner * SHARD + within, -1)[None, :]
     dma = pltpu.SemaphoreType.DMA
-    send, sent = call(
+    send, o_placed, sent, skip_placed = call(
         dispatch_kernel,
-        "vvvvvv",
-        [out((ROWS, SEND)), out((ROWS, TOK))],
-        "vh",
-        [pltpu.VMEM((ROWS, TOK), BF), dma((1,))],
+        "vvvvvvvv",
+        [out((ROWS, SEND)), out((HD, DP)), out((ROWS, TOK)), out((TOK, DP))],
+        "vvhh",
+        [pltpu.VMEM((ROWS, TOK), BF), pltpu.VMEM((TOK, DP), BF), dma((2,))],
         2,
-    )(picked_t, held, mix.astype(F32).T, place, x.T, g.T)
+    )(picked_t, held, mix.astype(F32).T, place, x.T, g.T, skip.T, out_map)
     got = lax.all_to_all(send.reshape(EXPERTS, CAPP, SEND), CTX, 0, 0, tiled=True)
     own = order(own, send)
     near = shift_blocks(own, 1)
     far = shift_blocks(own, 2)
+    o_across = lax.ppermute(o_placed, "xh", SWAP)
+    near, far, o_across = lax.optimization_barrier((near, far, o_across))
     shares_shape, qt_shape = (3 * TOK, HEADS * TOK), (HEADS * HD, TOK)
     kt_shape, v_shape = (KV, 3 * TOK), (3 * TOK, KV)
     shares, q_t, k_t, v_win = call(
@@ -378,17 +402,16 @@
 
     got = order(got, v_win).reshape(ROWS, SEND)
     got_other = lax.ppermute(got, "core", SWAP)
-    o_pair = both_xh(order(o_pad, send), False)
+    o_pair = jnp.concatenate([o_placed, o_across], axis=0)
     o_mine = lax.all_gather(o_pair, "z", axis=0, tiled=True)
     w_mine = order(w_mine, got_other, o_pair)
     w_other = lax.ppermute(w_mine, "core", SWAP)
     back, partial = call(
         expert_kernel,
-        "vvhh",
+        "vvvh",
         [out((ROWS, BACK)), out((HALF, DP))],
         "hh",
         [
-            pltpu.VMEM((HALF, DP), BF),
             pltpu.VMEM((HALF, DP), BF),
             pltpu.VMEM((ROWS, BACK), BF),
             pltpu.VMEM((2 * ROWS, DP), BF),
@@ -397,48 +420,56 @@
             dma((6,)),
         ],
         3,
-    )(got, got_other, w_mine, w_other)
+    )(got, got_other, w_other, w_mine)
     terms = lax.all_to_all(partial.reshape(16, SEG, DP), ("z", "xh"), 0, 0, tiled=True)
     map_grad = jnp.sum(terms.astype(F32), axis=0)[None, :SHARD, :F].astype(BF)
 
     returned = give_back(back)
-    o_mine = order(o_mine, *returned)
+    o_mine = order(o_mine, returned)
     o_other = lax.ppermute(o_mine, "core", SWAP)
-    src_t, gate_t, sg, far_g, near_g, own_g = call(
+    spot = jnp.stack([core, xh, lax.axis_index("y")]).astype(jnp.int32)
+    half_shape = (16 * HD, DP)
+    gate_t, src, hidden, cot_mine = call(
+        combine_kernel,
+        "svvhhhh",
+        [out((4, TOK), F32), out((TOK, DP)), out((TOK, DP)), out((16 * HD, TOK))],
+        "vvvv",
+        [
+            pltpu.VMEM((ROWS, BACK), BF),
+            pltpu.VMEM((ROWS, TOK), BF),
+            pltpu.VMEM((TOK, DP), BF),
+            pltpu.VMEM(half_shape, BF),
+            dma((11,)),
+        ],
+        3,
+    )(spot, picked_t, held, returned, sent, skip_placed, o_mine)
+    sg, far_g, near_g, own_g = call(
         late_kernel,
-        "svvvhhhhhhhhhhhhhhh",
+        "svvhhhh",
         [
-            out((D, TOK)),
-            out((4, TOK), F32),
             out(shares_shape),
             out((TOK, 2 * KV)),
             out((TOK, 2 * KV)),
             out((TOK, 2 * KV), F32),
         ],
-        "vvvvvv",
+        "vvvv",
         [
-            pltpu.VMEM((DP, TOK), BF),
             pltpu.VMEM((HEADS * HD, TOK), BF),
             pltpu.VMEM((3 * TOK, HD), F32),
             pltpu.VMEM((3 * TOK, HD), F32),
-            pltpu.VMEM((ROWS, BACK), BF),
-            pltpu.VMEM((ROWS, TOK), BF),
             pltpu.VMEM(v_shape, BF),
-            pltpu.VMEM((D, TOK), BF),
-            pltpu.VMEM((16 * HD, DP), BF),
-            pltpu.VMEM((16 * HD, DP), BF),
+            pltpu.VMEM(half_shape, BF),
             pltpu.VMEM(qt_shape, BF),
             pltpu.VMEM(shares_shape, BF),
-            dma((15,)),
+            dma((4,)),
         ],
         0.1,
-    )(
-        jnp.stack([core, xh, lax.axis_index("y")]).astype(jnp.int32), picked_t, held, place,
-        *returned, sent, v_win, skip.T, o_mine, o_other, q_t, shares,
-    )
+    )(spot, cot_mine, hidden, v_win, o_other, q_t, shares)
     got_near = shift_blocks(near_g, -1)
     got_far = shift_blocks(far_g, -2)
-    q_grad = call(query_kernel, "vv", [out((TOK, HEADS * HD))], "v", [], 0.1)(sg, k_t)[0]
+    q_grad, src_t = call(
+        query_kernel, "vvvv", [out((TOK, HEADS * HD)), out((D, TOK))], "vv", [], 0.1
+    )(sg, k_t, src, place)
     kv_grad = (own_g + got_near.astype(F32) + got_far.astype(F32)).astype(BF)
     return (
         q_grad,

time: 195 us -> 201 us (1.031)
  the two profiles are of different devices: /device:TPU:16 before, /device:TPU:17 now
where the time goes in v5:
time: 201 us; the launch traced here: 200 us
  waiting for transfers between devices  64.5 us (32%)
  starting transfers between devices  57.8 us (29%)
  Pallas kernels  45.3 us (23%)
  between operations  14.4 us (7%)
  other arithmetic  9 us (4%)
  local copies, waits for them, and re-layouts  8.57 us (4%)
    ppermute x4, waiting for transfers between devices, shift_blocks(): lax.ppermute(value, ALL, [(i, i + steps) for i in range(first, last)])  29 us
    ppermute x3, waiting for transfers between devices, give_back(): move = lax.ppermute(move, 'y', [(i, (i + bit) % 8) for i in range(8)])  20.2 us
    ppermute x4, starting transfers between devices, shift_blocks(): lax.ppermute(value, ALL, [(i, i + steps) for i in range(first, last)])  15.1 us
    ppermute x3, starting transfers between devices, give_back(): move = lax.ppermute(move, 'y', [(i, (i + bit) % 8) for i in range(8)])  12.5 us
    pallas_call x1, Pallas kernels, shards(): call(late_kernel, 'svvhhhh', [out(shares_shape), out((TOK, 2 * KV)), out(...  11.9 us
    pallas_call x1, Pallas kernels, shards(): call(shares_kernel, 'vvvvv', [out(shares_shape), out(qt_shape), out(kt_sh...  9.65 us
    pallas_call x1, Pallas kernels, shards(): call(expert_kernel, 'vvvh', [out((ROWS, BACK)), out((HALF, DP))], 'hh', [...  8.5 us
    all_to_all x1, starting transfers between devices, shards(): lax.all_to_all(send.reshape(EXPERTS, CAPP, SEND), CTX, 0, 0, tiled=True)  7.81 us
  transfers between devices with their start and end apart: 17, of which 11 were waited for; matrix products, arithmetic and copies ran while one was open for 5% of the time, Pallas kernels for 23%

profile of v5, /device:TPU:17, one launch (start us, length us, event | category | flops | bytes accessed | tf_op | source)
XLA Modules:
  0.0 199.6 jit_solution(12324362950317907974)
XLA Ops:
  7.2 0.9 pad.8
  8.2 4.7 %collective-permute-start = (bf16[48,1536]{1,0:T(8,128)(2,1)S(1)}, bf16[48,1536]{1,0:T(8,128)(2,1)S(1)}, u32[]{:S(2)}, u32[]{:S(2)}) collective-permute-start(bf16[48,1536]{1,0:T(8,128)(2,1)S(1)} %pad.8), channel_id=1, source_target_pairs={{0,2},{2,0},{1,3},{3,1},{4,6},{6,4},{5,7},{7,5},{8,10},{10,8},{9,1... | collective-permute-start | bytes 442376 | tf_op jit(solution)/shard_map/ppermute | solution.py:336
  12.8 3.4 %collective-permute-done = bf16[48,1536]{1,0:T(8,128)(2,1)S(1)} collective-permute-done((bf16[48,1536]{1,0:T(8,128)(2,1)S(1)}, bf16[48,1536]{1,0:T(8,128)(2,1)S(1)}, u32[]{:S(2)}, u32[]{:S(2)}) %collective-permute-start) | collective-permute-done | bytes 147488 | tf_op jit(solution)/shard_map/ppermute | solution.py:336
  16.3 1.0 broadcast_select_fusion.3
  17.3 0.7 pad_maximum_fusion.2
  18.0 0.7 broadcast_in_dim.10
  18.7 0.7 broadcast_in_dim_reshape.4.held_ref
  19.5 1.3 convert_bitcast_fusion.gate_ref
  20.7 0.7 compare_select_fusion.place_ref
  21.4 5.5 %shard_map.163 = (bf16[128,3072]{1,0:T(8,128)(2,1)}, bf16[64,1536]{1,0:T(8,128)(2,1)}, bf16[128,128]{1,0:T(8,128)(2,1)}, bf16[128,1536]{1,0:T(8,128)(2,1)}) custom-call(s32[4,128]{1,0:T(4,128)} %bitcast.41, s32[128,1]{1,0:T(8,128)} %broadcast_in_dim_reshape.4.held_ref, f32[4,128]{1,0:T(4,128)} %convert_bitcast_fusion.gate_ref, ...), custom_call_target="tpu_custom_call" | custom-call | bytes 7380000 | tf_op jit(solution)/shard_map/pallas_call | solution.py:370
  27.0 7.8 %all-to-all-start = ((bf16[16,8,3072]{2,1,0:T(8,128)(2,1)}), bf16[16,8,3072]{2,1,0:T(8,128)(2,1)S(1)}, u32[]{:S(2)}, u32[]{:S(2)}) async-start(bf16[16,8,3072]{2,1,0:T(8,128)(2,1)} %bitcast.35), calls=%async_computation | async-start | bytes 1572864 | tf_op jit(solution)/shard_map/all_to_all | solution.py:378
  35.5 4.4 %collective-permute-start.3 = (bf16[64,1536]{1,0:T(8,128)(2,1)}, bf16[64,1536]{1,0:T(8,128)(2,1)S(1)}, u32[]{:S(2)}, u32[]{:S(2)}) collective-permute-start(bf16[64,1536]{1,0:T(8,128)(2,1)} %get-tuple-element.37), channel_id=1, source_target_pairs={{0,2},{2,0},{1,3},{3,1},{4,6},{6,4},{5,7},{7,5},{8,10},{10,8},{9,1... | collective-permute-start | bytes 589832 | tf_op jit(solution)/shard_map/ppermute | solution.py:382
  39.9 5.0 %collective-permute-start.1 = (bf16[128,640]{1,0:T(8,128)(2,1)S(1)}, bf16[128,640]{1,0:T(8,128)(2,1)S(1)}, u32[]{:S(2)}, u32[]{:S(2)}) collective-permute-start(bf16[128,640]{1,0:T(8,128)(2,1)S(1)} %fusion.5.own_ref), channel_id=1, source_target_pairs={{0,1},{1,2},{2,3},{3,4},{4,5},{5,6},{6,7},{7,8},{8,9},{9,10},{10,1... | collective-permute-start | bytes 491528 | tf_op jit(solution)/shard_map/ppermute | solution.py:345
  45.0 5.8 %collective-permute-start.2 = (bf16[128,640]{1,0:T(8,128)(2,1)S(1)}, bf16[128,640]{1,0:T(8,128)(2,1)S(1)}, u32[]{:S(2)}, u32[]{:S(2)}) collective-permute-start(bf16[128,640]{1,0:T(8,128)(2,1)S(1)} %fusion.5.own_ref), channel_id=1, source_target_pairs={{0,2},{1,3},{2,4},{3,5},{4,6},{5,7},{6,8},{7,9},{8,10},{9,11},{10,... | collective-permute-start | bytes 491528 | tf_op jit(solution)/shard_map/ppermute | solution.py:345
  50.8 2.3 %collective-permute-done.1.near_ref = bf16[128,640]{1,0:T(8,128)(2,1)S(1)} collective-permute-done((bf16[128,640]{1,0:T(8,128)(2,1)S(1)}, bf16[128,640]{1,0:T(8,128)(2,1)S(1)}, u32[]{:S(2)}, u32[]{:S(2)}) %collective-permute-start.1) | collective-permute-done | bytes 163872 | tf_op jit(solution)/shard_map/ppermute | solution.py:345
  53.1 16.0 %collective-permute-done.2.far_ref = bf16[128,640]{1,0:T(8,128)(2,1)S(1)} collective-permute-done((bf16[128,640]{1,0:T(8,128)(2,1)S(1)}, bf16[128,640]{1,0:T(8,128)(2,1)S(1)}, u32[]{:S(2)}, u32[]{:S(2)}) %collective-permute-start.2) | collective-permute-done | bytes 163872 | tf_op jit(solution)/shard_map/ppermute | solution.py:345
  69.1 0.6 copy-done.7
  69.7 9.6 %shard_map.164 = (bf16[384,4096]{1,0:T(8,128)(2,1)}, bf16[2048,128]{1,0:T(8,128)(2,1)}, bf16[256,384]{1,0:T(8,128)(2,1)}, bf16[384,256]{1,0:T(8,128)(2,1)}) custom-call(bf16[128,2048]{1,0:T(8,128)(2,1)} %q_ref.1, bf16[128,640]{1,0:T(8,128)(2,1)} %copy-done.7, bf16[128,640]{1,0:T(8,128)(2,1)} %copy-done.6, bf16[128,640]{1,0:T(8,128)(2,1)} %copy-done.4, ...), custom_call_target="tpu_custom_call" | custom-call | bytes 29520000 | tf_op jit(solution)/shard_map/pallas_call | solution.py:386
  79.4 1.9 collective-permute-start.4
  81.3 0.9 constant_dynamic-update-slice_fusion.1
  82.3 0.8 copy-done.2
  83.6 0.9 copy-done.3
  84.5 2.0 %collective-permute-start.5 = (bf16[768,1536]{1,0:T(8,128)(2,1)}, bf16[768,1536]{1,0:T(8,128)(2,1)S(1)}, u32[]{:S(2)}, u32[]{:S(2)}) collective-permute-start(bf16[768,1536]{1,0:T(8,128)(2,1)} %all-gather.3.cloned.1.call-done.wm_any), channel_id=1, source_target_pairs={{0,1},{1,0},{2,3},{3,2},{4,5},{5,4},{6,7},{7,6},{8,9},{9,8},{10,11... | collective-permute-start | bytes 7077896 | tf_op jit(solution)/shard_map/ppermute | solution.py:408
  86.5 4.6 %collective-permute-done.5.wo_ref = bf16[768,1536]{1,0:T(8,128)(2,1)S(1)} collective-permute-done((bf16[768,1536]{1,0:T(8,128)(2,1)}, bf16[768,1536]{1,0:T(8,128)(2,1)S(1)}, u32[]{:S(2)}, u32[]{:S(2)}) %collective-permute-start.5) | collective-permute-done | bytes 2359328 | tf_op jit(solution)/shard_map/ppermute | solution.py:408
  91.1 1.4 copy-done.1
  92.6 8.5 %shard_map.165 = (bf16[128,1664]{1,0:T(8,128)(2,1)}, bf16[768,1536]{1,0:T(8,128)(2,1)}) custom-call(bf16[128,3072]{1,0:T(8,128)(2,1)} %bitcast.29, bf16[128,3072]{1,0:T(8,128)(2,1)} %copy-done.3, bf16[768,1536]{1,0:T(8,128)(2,1)} %copy-done.1, bf16[768,1536]{1,0:T(8,128)(2,1)} %all-gather.3.cloned.1.call-done.wm_any), custom_call_target="tpu_custom_call" | custom-call | bytes 11070000 | tf_op jit(solution)/shard_map/pallas_call | solution.py:409
  101.1 1.0 fusion.3
  102.1 1.9 collective-permute-start.6
  104.0 6.8 %collective-permute-done.6 = bf16[8,1,8,1664]{3,2,1,0:T(8,128)(2,1)S(1)} collective-permute-done((bf16[8,1,8,1664]{3,2,1,0:T(8,128)(2,1)S(1)}, bf16[8,1,8,1664]{3,2,1,0:T(8,128)(2,1)S(1)}, u32[]{:S(2)}, u32[]{:S(2)}) %collective-permute-start.6) | collective-permute-done | bytes 213024 | tf_op jit(solution)/shard_map/ppermute | solution.py:322
  110.8 1.2 broadcast_select_fusion.1
  112.1 3.2 %collective-permute-start.7 = (bf16[2,2,1,16,1664]{4,3,2,1,0:T(8,128)(2,1)S(1)}, bf16[2,2,1,16,1664]{4,3,2,1,0:T(8,128)(2,1)S(1)}, u32[]{:S(2)}, u32[]{:S(2)}) collective-permute-start(bf16[2,2,1,16,1664]{4,3,2,1,0:T(8,128)(2,1)S(1)} %get-tuple-element.71), channel_id=1, source_target_pairs={{0,64},{64,128},{128,192},{192,256},{256,320},{320,384},{384,448},... | collective-permute-start | bytes 638984 | tf_op jit(solution)/shard_map/ppermute | solution.py:330
  115.3 4.8 %collective-permute-done.7 = bf16[2,2,1,16,1664]{4,3,2,1,0:T(8,128)(2,1)S(1)} collective-permute-done((bf16[2,2,1,16,1664]{4,3,2,1,0:T(8,128)(2,1)S(1)}, bf16[2,2,1,16,1664]{4,3,2,1,0:T(8,128)(2,1)S(1)}, u32[]{:S(2)}, u32[]{:S(2)}) %collective-permute-start.7) | collective-permute-done | bytes 213024 | tf_op jit(solution)/shard_map/ppermute | solution.py:330
  120.1 6.5 %collective-permute-start.8 = (bf16[2,1,2,16,1664]{4,3,2,1,0:T(8,128)(2,1)S(1)}, bf16[2,1,2,16,1664]{4,3,2,1,0:T(8,128)(2,1)S(1)}, u32[]{:S(2)}, u32[]{:S(2)}) collective-permute-start(bf16[2,1,2,16,1664]{4,3,2,1,0:T(8,128)(2,1)S(1)} %get-tuple-element.69), channel_id=1, source_target_pairs={{0,128},{64,192},{128,256},{192,320},{256,384},{320,448},{384,0},{... | collective-permute-start | bytes 638984 | tf_op jit(solution)/shard_map/ppermute | solution.py:330
  126.6 3.7 %all-to-all-start.1 = ((bf16[16,48,1536]{2,1,0:T(8,128)(2,1)}), bf16[16,48,1536]{2,1,0:T(8,128)(2,1)S(1)}, u32[]{:S(2)}, u32[]{:S(2)}) async-start(bf16[16,48,1536]{2,1,0:T(8,128)(2,1)} %bitcast.30), calls=%async_computation.1 | async-start | bytes 4718592 | tf_op jit(solution)/shard_map/all_to_all | solution.py:424
  130.3 4.3 %collective-permute-done.8 = bf16[2,1,2,16,1664]{4,3,2,1,0:T(8,128)(2,1)S(1)} collective-permute-done((bf16[2,1,2,16,1664]{4,3,2,1,0:T(8,128)(2,1)S(1)}, bf16[2,1,2,16,1664]{4,3,2,1,0:T(8,128)(2,1)S(1)}, u32[]{:S(2)}, u32[]{:S(2)}) %collective-permute-start.8) | collective-permute-done | bytes 213024 | tf_op jit(solution)/shard_map/ppermute | solution.py:330
  134.7 2.9 %collective-permute-start.9 = (bf16[1,2,2,16,1664]{4,3,2,1,0:T(8,128)(2,1)S(1)}, bf16[1,2,2,16,1664]{4,3,2,1,0:T(8,128)(2,1)S(1)}, u32[]{:S(2)}, u32[]{:S(2)}) collective-permute-start(bf16[1,2,2,16,1664]{4,3,2,1,0:T(8,128)(2,1)S(1)} %get-tuple-element.67), channel_id=1, source_target_pairs={{0,256},{64,320},{128,384},{192,448},{256,0},{320,64},{384,128},{4... | collective-permute-start | bytes 638984 | tf_op jit(solution)/shard_map/ppermute | solution.py:330
  137.5 11.2 %collective-permute-done.9 = bf16[1,2,2,16,1664]{4,3,2,1,0:T(8,128)(2,1)S(1)} collective-permute-done((bf16[1,2,2,16,1664]{4,3,2,1,0:T(8,128)(2,1)S(1)}, bf16[1,2,2,16,1664]{4,3,2,1,0:T(8,128)(2,1)S(1)}, u32[]{:S(2)}, u32[]{:S(2)}) %collective-permute-start.9) | collective-permute-done | bytes 213024 | tf_op jit(solution)/shard_map/ppermute | solution.py:330
  148.7 0.8 pad_maximum_fusion.1
  149.5 3.8 %collective-permute-start.10 = (bf16[1024,1536]{1,0:T(8,128)(2,1)}, bf16[1024,1536]{1,0:T(8,128)(2,1)}, u32[]{:S(2)}, u32[]{:S(2)}) collective-permute-start(bf16[1024,1536]{1,0:T(8,128)(2,1)} %all-gather.5.cloned.1.call-done.om_any), channel_id=1, source_target_pairs={{0,1},{1,0},{2,3},{3,2},{4,5},{5,4},{6,7},{7,6},{8,9},{9,8},{10,11... | collective-permute-start | bytes 9437192 | tf_op jit(solution)/shard_map/ppermute | solution.py:429
  153.9 4.9 %shard_map.166 = (f32[4,128]{1,0:T(4,128)}, bf16[128,1536]{1,0:T(8,128)(2,1)}, bf16[128,1536]{1,0:T(8,128)(2,1)}, bf16[1024,128]{1,0:T(8,128)(2,1)}) custom-call(s32[3]{0:T(128)} %pad_add_fusion.at_ref, s32[4,128]{1,0:T(4,128)} %bitcast.42, s32[128,1]{1,0:T(8,128)} %broadcast_in_dim_reshape.4.held_ref, bf16[128,1664]{1,0:T(8,128)(2,1)} %bitcast.34, ...), custom_call_target="tpu_custom_call" | custom-call | bytes 11070000 | tf_op jit(solution)/shard_map/pallas_call | solution.py:432
  158.9 11.9 %shard_map.167 = (bf16[384,4096]{1,0:T(8,128)(2,1)}, bf16[128,512]{1,0:T(8,128)(2,1)}, bf16[128,512]{1,0:T(8,128)(2,1)}, f32[128,512]{1,0:T(8,128)}) custom-call(s32[3]{0:T(128)} %pad_add_fusion.at_ref, bf16[1024,128]{1,0:T(8,128)(2,1)} %get-tuple-element.48.cotm_ref, bf16[128,1536]{1,0:T(8,128)(2,1)} %get-tuple-element.49.hidden_ref, ...), custom_call_target="tpu_custom_call" | custom-call | bytes 369000 | tf_op jit(solution)/shard_map/pallas_call | solution.py:446
  170.8 2.1 %collective-permute-start.12 = (bf16[128,512]{1,0:T(8,128)(2,1)}, bf16[128,512]{1,0:T(8,128)(2,1)S(1)}, u32[]{:S(2)}, u32[]{:S(2)}) collective-permute-start(bf16[128,512]{1,0:T(8,128)(2,1)} %get-tuple-element.58), channel_id=1, source_target_pairs={{2,0},{3,1},{4,2},{5,3},{6,4},{7,5},{8,6},{9,7},{10,8},{11,9},{12,... | collective-permute-start | bytes 393224 | tf_op jit(solution)/shard_map/ppermute | solution.py:345
  172.8 2.2 %collective-permute-start.11 = (bf16[128,512]{1,0:T(8,128)(2,1)}, bf16[128,512]{1,0:T(8,128)(2,1)S(1)}, u32[]{:S(2)}, u32[]{:S(2)}) collective-permute-start(bf16[128,512]{1,0:T(8,128)(2,1)} %get-tuple-element.57), channel_id=1, source_target_pairs={{1,0},{2,1},{3,2},{4,3},{5,4},{6,5},{7,6},{8,7},{9,8},{10,9},{11,1... | collective-permute-start | bytes 393224 | tf_op jit(solution)/shard_map/ppermute | solution.py:345
  175.6 4.8 %shard_map.168 = (bf16[128,2048]{1,0:T(8,128)(2,1)}, bf16[1440,128]{1,0:T(8,128)(2,1)}) custom-call(bf16[384,4096]{1,0:T(8,128)(2,1)} %get-tuple-element.52.sg_ref, bf16[256,384]{1,0:T(8,128)(2,1)} %get-tuple-element.53.kt_ref, bf16[128,1536]{1,0:T(8,128)(2,1)} %get-tuple-element.54.src_ref, s32[1,1536]{1,0:T(1,128)} %compare_select_fusion.place_ref), custom_call_target="tpu_custom_call" | custom-call | bytes 369000 | tf_op jit(solution)/shard_map/pallas_call | solution.py:470
  180.4 9.5 %collective-permute-done.12 = bf16[128,512]{1,0:T(8,128)(2,1)S(1)} collective-permute-done((bf16[128,512]{1,0:T(8,128)(2,1)}, bf16[128,512]{1,0:T(8,128)(2,1)S(1)}, u32[]{:S(2)}, u32[]{:S(2)}) %collective-permute-start.12) | collective-permute-done | bytes 131104 | tf_op jit(solution)/shard_map/ppermute | solution.py:345
  189.9 1.2 collective-permute-done.11
  191.1 0.7 fusion.13
  192.1 0.7 slice_bitcast_fusion
  (45 shorter events, 3.1 us)
Async XLA Ops:
  7.2 27.7 %copy-start.11 = (s32[128]{0:T(128)S(1)}, s32[128]{0:T(128)}, u32[]{:S(2)}) copy-start(s32[128]{0:T(128)} %param.15) | copy-start | bytes 1540
  7.2 32.7 %copy-start.8 = (bf16[128,256]{1,0:T(8,128)(2,1)S(1)}, bf16[128,256]{1,0:T(8,128)(2,1)}, u32[]{:S(2)}) copy-start(bf16[128,256]{1,0:T(8,128)(2,1)} %param.14) | copy-start | bytes 196612
  7.2 32.7 %copy-start.9 = (bf16[128,256]{1,0:T(8,128)(2,1)S(1)}, bf16[128,256]{1,0:T(8,128)(2,1)}, u32[]{:S(2)}) copy-start(bf16[128,256]{1,0:T(8,128)(2,1)} %param.13) | copy-start | bytes 196612
  7.2 77.3 %all-gather.3.cloned.1.call-start = ((), (), s32[]{:S(2)}) async-start(), calls=%async_computation.2 | async-start | bytes 2654208 | tf_op jit(solution)/shard_map/all_gather | solution.py:353
  8.2 8.1 %collective-permute-start = (bf16[48,1536]{1,0:T(8,128)(2,1)S(1)}, bf16[48,1536]{1,0:T(8,128)(2,1)S(1)}, u32[]{:S(2)}, u32[]{:S(2)}) collective-permute-start(bf16[48,1536]{1,0:T(8,128)(2,1)S(1)} %pad.8), channel_id=1, source_target_pairs={{0,2},{2,0},{1,3},{3,1},{4,6},{6,4},{5,7},{7,5},{8,10},{10,8},{9,1... | collective-permute-start | bytes 442376 | tf_op jit(solution)/shard_map/ppermute | solution.py:336
  27.0 52.4 %all-to-all-start = ((bf16[16,8,3072]{2,1,0:T(8,128)(2,1)}), bf16[16,8,3072]{2,1,0:T(8,128)(2,1)S(1)}, u32[]{:S(2)}, u32[]{:S(2)}) async-start(bf16[16,8,3072]{2,1,0:T(8,128)(2,1)} %bitcast.35), calls=%async_computation | async-start | bytes 1572864 | tf_op jit(solution)/shard_map/all_to_all | solution.py:378
  34.8 114.8 %all-gather.5.cloned.1.call-start = ((), (), s32[]{:S(2)}) async-start(), calls=%async_computation.3 | async-start | bytes 3538944 | tf_op jit(solution)/shard_map/all_gather | solution.py:406
  35.5 33.6 %collective-permute-start.3 = (bf16[64,1536]{1,0:T(8,128)(2,1)}, bf16[64,1536]{1,0:T(8,128)(2,1)S(1)}, u32[]{:S(2)}, u32[]{:S(2)}) collective-permute-start(bf16[64,1536]{1,0:T(8,128)(2,1)} %get-tuple-element.37), channel_id=1, source_target_pairs={{0,2},{2,0},{1,3},{3,1},{4,6},{6,4},{5,7},{7,5},{8,10},{10,8},{9,1... | collective-permute-start | bytes 589832 | tf_op jit(solution)/shard_map/ppermute | solution.py:382
  39.9 29.2 %copy-start.4 = (bf16[128,640]{1,0:T(8,128)(2,1)}, bf16[128,640]{1,0:T(8,128)(2,1)S(1)}, u32[]{:S(2)}) copy-start(bf16[128,640]{1,0:T(8,128)(2,1)S(1)} %fusion.5.own_ref) | copy-start | bytes 491524
  39.9 13.2 %collective-permute-start.1 = (bf16[128,640]{1,0:T(8,128)(2,1)S(1)}, bf16[128,640]{1,0:T(8,128)(2,1)S(1)}, u32[]{:S(2)}, u32[]{:S(2)}) collective-permute-start(bf16[128,640]{1,0:T(8,128)(2,1)S(1)} %fusion.5.own_ref), channel_id=1, source_target_pairs={{0,1},{1,2},{2,3},{3,4},{4,5},{5,6},{6,7},{7,8},{8,9},{9,10},{10,1... | collective-permute-start | bytes 491528 | tf_op jit(solution)/shard_map/ppermute | solution.py:345
  45.0 24.1 %collective-permute-start.2 = (bf16[128,640]{1,0:T(8,128)(2,1)S(1)}, bf16[128,640]{1,0:T(8,128)(2,1)S(1)}, u32[]{:S(2)}, u32[]{:S(2)}) collective-permute-start(bf16[128,640]{1,0:T(8,128)(2,1)S(1)} %fusion.5.own_ref), channel_id=1, source_target_pairs={{0,2},{1,3},{2,4},{3,5},{4,6},{5,7},{6,8},{7,9},{8,10},{9,11},{10,... | collective-permute-start | bytes 491528 | tf_op jit(solution)/shard_map/ppermute | solution.py:345
  53.1 16.0 %copy-start.6 = (bf16[128,640]{1,0:T(8,128)(2,1)}, bf16[128,640]{1,0:T(8,128)(2,1)S(1)}, u32[]{:S(2)}) copy-start(bf16[128,640]{1,0:T(8,128)(2,1)S(1)} %collective-permute-done.1.near_ref) | copy-start | bytes 491524
  69.1 0.7 copy-start.7
  79.4 11.7 %copy-start = (bf16[16,8,3072]{2,1,0:T(8,128)(2,1)}, bf16[16,8,3072]{2,1,0:T(8,128)(2,1)S(1)}, u32[]{:S(2)}) copy-start(bf16[16,8,3072]{2,1,0:T(8,128)(2,1)S(1)} %all-to-all-done) | copy-start | bytes 2359300
  79.4 4.2 %collective-permute-start.4 = (bf16[128,3072]{1,0:T(8,128)(2,1)S(1)}, bf16[128,3072]{1,0:T(8,128)(2,1)S(1)}, u32[]{:S(2)}, u32[]{:S(2)}) collective-permute-start(bf16[128,3072]{1,0:T(8,128)(2,1)S(1)} %bitcast.28), channel_id=1, source_target_pairs={{0,1},{1,0},{2,3},{3,2},{4,5},{5,4},{6,7},{7,6},{8,9},{9,8},{10,11... | collective-permute-start | bytes 2359304 | tf_op jit(solution)/shard_map/ppermute | solution.py:404
  82.3 0.8 copy-start.2
  83.6 0.9 copy-start.3
  84.5 6.6 %collective-permute-start.5 = (bf16[768,1536]{1,0:T(8,128)(2,1)}, bf16[768,1536]{1,0:T(8,128)(2,1)S(1)}, u32[]{:S(2)}, u32[]{:S(2)}) collective-permute-start(bf16[768,1536]{1,0:T(8,128)(2,1)} %all-gather.3.cloned.1.call-done.wm_any), channel_id=1, source_target_pairs={{0,1},{1,0},{2,3},{3,2},{4,5},{5,4},{6,7},{7,6},{8,9},{9,8},{10,11... | collective-permute-start | bytes 7077896 | tf_op jit(solution)/shard_map/ppermute | solution.py:408
  91.1 1.4 copy-start.1
  102.1 8.7 %collective-permute-start.6 = (bf16[8,1,8,1664]{3,2,1,0:T(8,128)(2,1)S(1)}, bf16[8,1,8,1664]{3,2,1,0:T(8,128)(2,1)S(1)}, u32[]{:S(2)}, u32[]{:S(2)}) collective-permute-start(bf16[8,1,8,1664]{3,2,1,0:T(8,128)(2,1)S(1)} %fusion.3), channel_id=1, source_target_pairs={{0,32},{32,0},{1,33},{33,1},{2,34},{34,2},{3,35},{35,3},{4,36},{36... | collective-permute-start | bytes 638984 | tf_op jit(solution)/shard_map/ppermute | solution.py:322
  112.1 7.9 %collective-permute-start.7 = (bf16[2,2,1,16,1664]{4,3,2,1,0:T(8,128)(2,1)S(1)}, bf16[2,2,1,16,1664]{4,3,2,1,0:T(8,128)(2,1)S(1)}, u32[]{:S(2)}, u32[]{:S(2)}) collective-permute-start(bf16[2,2,1,16,1664]{4,3,2,1,0:T(8,128)(2,1)S(1)} %get-tuple-element.71), channel_id=1, source_target_pairs={{0,64},{64,128},{128,192},{192,256},{256,320},{320,384},{384,448},... | collective-permute-start | bytes 638984 | tf_op jit(solution)/shard_map/ppermute | solution.py:330
  120.1 14.5 %collective-permute-start.8 = (bf16[2,1,2,16,1664]{4,3,2,1,0:T(8,128)(2,1)S(1)}, bf16[2,1,2,16,1664]{4,3,2,1,0:T(8,128)(2,1)S(1)}, u32[]{:S(2)}, u32[]{:S(2)}) collective-permute-start(bf16[2,1,2,16,1664]{4,3,2,1,0:T(8,128)(2,1)S(1)} %get-tuple-element.69), channel_id=1, source_target_pairs={{0,128},{64,192},{128,256},{192,320},{256,384},{320,448},{384,0},{... | collective-permute-start | bytes 638984 | tf_op jit(solution)/shard_map/ppermute | solution.py:330
  126.6 65.2 %all-to-all-start.1 = ((bf16[16,48,1536]{2,1,0:T(8,128)(2,1)}), bf16[16,48,1536]{2,1,0:T(8,128)(2,1)S(1)}, u32[]{:S(2)}, u32[]{:S(2)}) async-start(bf16[16,48,1536]{2,1,0:T(8,128)(2,1)} %bitcast.30), calls=%async_computation.1 | async-start | bytes 4718592 | tf_op jit(solution)/shard_map/all_to_all | solution.py:424
  134.7 14.1 %collective-permute-start.9 = (bf16[1,2,2,16,1664]{4,3,2,1,0:T(8,128)(2,1)S(1)}, bf16[1,2,2,16,1664]{4,3,2,1,0:T(8,128)(2,1)S(1)}, u32[]{:S(2)}, u32[]{:S(2)}) collective-permute-start(bf16[1,2,2,16,1664]{4,3,2,1,0:T(8,128)(2,1)S(1)} %get-tuple-element.67), channel_id=1, source_target_pairs={{0,256},{64,320},{128,384},{192,448},{256,0},{320,64},{384,128},{4... | collective-permute-start | bytes 638984 | tf_op jit(solution)/shard_map/ppermute | solution.py:330
  149.5 9.3 %collective-permute-start.10 = (bf16[1024,1536]{1,0:T(8,128)(2,1)}, bf16[1024,1536]{1,0:T(8,128)(2,1)}, u32[]{:S(2)}, u32[]{:S(2)}) collective-permute-start(bf16[1024,1536]{1,0:T(8,128)(2,1)} %all-gather.5.cloned.1.call-done.om_any), channel_id=1, source_target_pairs={{0,1},{1,0},{2,3},{3,2},{4,5},{5,4},{6,7},{7,6},{8,9},{9,8},{10,11... | collective-permute-start | bytes 9437192 | tf_op jit(solution)/shard_map/ppermute | solution.py:429
  158.9 16.1 %copy-start.10 = (f32[4,128]{1,0:T(4,128)S(1)}, f32[4,128]{1,0:T(4,128)}, u32[]{:S(2)}) copy-start(f32[4,128]{1,0:T(4,128)} %get-tuple-element.60) | copy-start | bytes 6148
  170.7 20.3 %copy-start.5 = (f32[128,512]{1,0:T(8,128)S(1)}, f32[128,512]{1,0:T(8,128)}, u32[]{:S(2)}) copy-start(f32[128,512]{1,0:T(8,128)} %get-tuple-element.56) | copy-start | bytes 786436
  170.8 19.1 %collective-permute-start.12 = (bf16[128,512]{1,0:T(8,128)(2,1)}, bf16[128,512]{1,0:T(8,128)(2,1)S(1)}, u32[]{:S(2)}, u32[]{:S(2)}) collective-permute-start(bf16[128,512]{1,0:T(8,128)(2,1)} %get-tuple-element.58), channel_id=1, source_target_pairs={{2,0},{3,1},{4,2},{5,3},{6,4},{7,5},{8,6},{9,7},{10,8},{11,9},{12,... | collective-permute-start | bytes 393224 | tf_op jit(solution)/shard_map/ppermute | solution.py:345
  172.8 18.2 %collective-permute-start.11 = (bf16[128,512]{1,0:T(8,128)(2,1)}, bf16[128,512]{1,0:T(8,128)(2,1)S(1)}, u32[]{:S(2)}, u32[]{:S(2)}) collective-permute-start(bf16[128,512]{1,0:T(8,128)(2,1)} %get-tuple-element.57), channel_id=1, source_target_pairs={{1,0},{2,1},{3,2},{4,3},{5,4},{6,5},{7,6},{8,7},{9,8},{10,9},{11,1... | collective-permute-start | bytes 393224 | tf_op jit(solution)/shard_map/ppermute | solution.py:345
Sparse Core Ops, SparseCore 0:
  18.1 47.1 all-gather.2
  83.2 42.8 all-gather.4

commit v6 on v5

--- a/solution.py
+++ b/solution.py
@@ -154,13 +154,16 @@
 
 
 def expert_kernel(
-    got_ref, got2_ref, wo_ref, wm_any, back_any, part_any,
-    wm_ref, back_ref, pg_ref, pre_ref, part_ref, sems,
+    got_ref, got2_ref, wo_ref, wm_any, back_any, pg_any, x_any,
+    wm_ref, back_ref, pg_ref, x_ref, pre_ref, sems,
 ):
     load = pltpu.make_async_copy(wm_any, wm_ref, sems.at[0])
     load.start()
     x_mine = jnp.concatenate([got_ref[:, :HALF], got2_ref[:, HALF:DP]], axis=0)
     x_other = jnp.concatenate([got_ref[:, HALF:DP], got2_ref[:, :HALF]], axis=0)
+    x_ref[...] = x_mine
+    stores = [pltpu.make_async_copy(x_ref, x_any, sems.at[1])]
+    stores[0].start()
     load.wait()
     step = 512
     for lo in range(0, DP, step):
@@ -179,15 +182,8 @@
         total = total + jnp.sum(grad * (pre * sig), axis=1, keepdims=True)
         slope = sig * (1.0 + pre * (1.0 - sig))
         pg_ref[:, lo : lo + step] = (gate * grad * slope).astype(BF)
-    pg = pg_ref[...]
-    stores = []
-    for c in range(HALF // 256):
-        r = slice(c * 256, (c + 1) * 256)
-        part_ref[r, :] = dot(x_mine[:, r], pg, ((0,), (0,))).astype(BF)
-        stores.append(
-            pltpu.make_async_copy(part_ref.at[r, :], part_any.at[r, :], sems.at[2 + c])
-        )
-        stores[-1].start()
+    stores.append(pltpu.make_async_copy(pg_ref, pg_any, sems.at[2]))
+    stores[1].start()
     pg = pg_ref[:ROWS, :]
     for c in range(HALF // 256):
         r = slice(c * 256, (c + 1) * 256)
@@ -196,30 +192,41 @@
             pg, wo_ref[r, :], ((1,), (1,))
         ).astype(BF)
     back_ref[:, DP:] = jnp.broadcast_to(total[:ROWS], (ROWS, BACK - DP)).astype(BF)
-    stores.append(pltpu.make_async_copy(back_ref, back_any, sems.at[5]))
-    stores[-1].start()
+    stores.append(pltpu.make_async_copy(back_ref, back_any, sems.at[3]))
+    stores[2].start()
     for copy in stores:
         copy.wait()
 
 
+def map_kernel(x_any, pg_any, part_any, x_ref, pg_ref, part_ref, sems):
+    loads = copies_of(((x_any, x_ref), (pg_any, pg_ref)), sems)
+    for copy in loads:
+        copy.start()
+    for copy in loads:
+        copy.wait()
+    stores = []
+    for c in range(HALF // 256):
+        r = slice(c * 256, (c + 1) * 256)
+        part_ref[r, :] = dot(x_ref[:, r], pg_ref[...], ((0,), (0,))).astype(BF)
+        stores.append(
+            pltpu.make_async_copy(part_ref.at[r, :], part_any.at[r, :], sems.at[2 + c])
+        )
+        stores[-1].start()
+    for copy in stores:
+        copy.wait()
+
+
 def combine_kernel(
-    at_ref, picked_ref, held_ref, back_any, sent_any, skip_any, om_any,
+    picked_ref, held_ref, back_any, sent_any, skip_any, om_any,
     gate_ref, src_ref, hidden_ref, cot_ref, back_ref, sent_ref, skip_ref, om_ref, sems,
 ):
-    pairs = ((sent_any, sent_ref), (skip_any, skip_ref), (om_any, om_ref))
+    pairs = (
+        (sent_any, sent_ref), (skip_any, skip_ref), (om_any, om_ref), (back_any, back_ref)
+    )
     copies = copies_of(pairs, sems)
-    arrived = []
-    for k in range(8):
-        rows = pl.ds(pl.multiple_of(((at_ref[2] + 8 - k) % 8) * 16, 16), 16)
-        arrived.append(
-            pltpu.make_async_copy(
-                back_any.at[k * 16 : (k + 1) * 16, :], back_ref.at[rows, :], sems.at[3 + k]
-            )
-        )
-    for copy in arrived + copies:
+    for copy in copies:
         copy.start()
-    for copy in arrived:
-        copy.wait()
+    copies[3].wait()
     copies[0].wait()
     sent_bf = sent_ref[...]
     sent = sent_bf.astype(F32) > 0.5
@@ -311,25 +318,6 @@
         pick = jnp.where(feature == place_ref[:, at], 1.0, 0.0).astype(BF)
         total = total + dot(pick, src_ref[:, at], ((1,), (1,)))
     out_ref[...] = total.astype(BF)
-
-
-def give_back(back):
-    y, xl = lax.axis_index("y"), lax.axis_index("xl")
-    grid = back.reshape(8, 2, CAPP, BACK)
-    turned = jnp.concatenate([grid, grid], axis=0)
-    keep = lax.dynamic_slice(turned, (y, xl, 0, 0), (8, 1, CAPP, BACK))
-    give = lax.dynamic_slice(turned, (y, 1 - xl, 0, 0), (8, 1, CAPP, BACK))
-    got = lax.ppermute(give, "xl", SWAP)
-    both = jnp.concatenate(
-        [jnp.where(xl == 0, keep, got), jnp.where(xl == 0, got, keep)], axis=1
-    )
-    both = both.reshape(2, 2, 2, 2 * CAPP, BACK)
-    for bit, axis in ((1, 2), (2, 1), (4, 0)):
-        stay = lax.slice_in_dim(both, 0, 1, axis=axis)
-        move = lax.slice_in_dim(both, 1, 2, axis=axis)
-        move = lax.ppermute(move, "y", [(i, (i + bit) % 8) for i in range(8)])
-        both = jnp.concatenate([stay, move], axis=axis)
-    return both.reshape(ROWS, BACK)
 
 
 def both_xh(piece):
@@ -406,32 +394,47 @@
     o_mine = lax.all_gather(o_pair, "z", axis=0, tiled=True)
     w_mine = order(w_mine, got_other, o_pair)
     w_other = lax.ppermute(w_mine, "core", SWAP)
-    back, partial = call(
+    back, pg, x_mine = call(
         expert_kernel,
         "vvvh",
-        [out((ROWS, BACK)), out((HALF, DP))],
-        "hh",
+        [out((ROWS, BACK)), out((2 * ROWS, DP)), out((2 * ROWS, HALF))],
+        "hhh",
         [
             pltpu.VMEM((HALF, DP), BF),
             pltpu.VMEM((ROWS, BACK), BF),
             pltpu.VMEM((2 * ROWS, DP), BF),
+            pltpu.VMEM((2 * ROWS, HALF), BF),
             pltpu.VMEM((2 * ROWS, DP), F32),
-            pltpu.VMEM((HALF, DP), BF),
-            dma((6,)),
+            dma((4,)),
         ],
         3,
     )(got, got_other, w_other, w_mine)
+    returned = lax.all_to_all(back.reshape(EXPERTS, CAPP, BACK), CTX, 0, 0, tiled=True)
+    returned = returned.reshape(ROWS, BACK)
+    partial = call(
+        map_kernel,
+        "hh",
+        [out((HALF, DP))],
+        "h",
+        [
+            pltpu.VMEM((2 * ROWS, HALF), BF),
+            pltpu.VMEM((2 * ROWS, DP), BF),
+            pltpu.VMEM((HALF, DP), BF),
+            dma((5,)),
+        ],
+        3,
+    )(x_mine, pg)[0]
+    partial = order(partial, returned)
     terms = lax.all_to_all(partial.reshape(16, SEG, DP), ("z", "xh"), 0, 0, tiled=True)
     map_grad = jnp.sum(terms.astype(F32), axis=0)[None, :SHARD, :F].astype(BF)
 
-    returned = give_back(back)
     o_mine = order(o_mine, returned)
     o_other = lax.ppermute(o_mine, "core", SWAP)
-    spot = jnp.stack([core, xh, lax.axis_index("y")]).astype(jnp.int32)
+    spot = jnp.stack([core, xh]).astype(jnp.int32)
     half_shape = (16 * HD, DP)
     gate_t, src, hidden, cot_mine = call(
         combine_kernel,
-        "svvhhhh",
+        "vvhhhh",
         [out((4, TOK), F32), out((TOK, DP)), out((TOK, DP)), out((16 * HD, TOK))],
         "vvvv",
         [
@@ -439,10 +442,10 @@
             pltpu.VMEM((ROWS, TOK), BF),
             pltpu.VMEM((TOK, DP), BF),
             pltpu.VMEM(half_shape, BF),
-            dma((11,)),
+            dma((4,)),
         ],
         3,
-    )(spot, picked_t, held, returned, sent, skip_placed, o_mine)
+    )(picked_t, held, returned, sent, skip_placed, o_mine)
     sg, far_g, near_g, own_g = call(
         late_kernel,
         "svvhhhh",

time: 201 us -> 196 us (0.975)
  the two profiles are of different devices: /device:TPU:17 before, /device:TPU:4 now
where the time goes in v6:
time: 196 us; the launch traced here: 195 us
  waiting for transfers between devices  63.1 us (32%)
  starting transfers between devices  56 us (29%)
  Pallas kernels  47.9 us (24%)
  between operations  14.3 us (7%)
  local copies, waits for them, and re-layouts  7.01 us (4%)
  other arithmetic  6.44 us (3%)
    ppermute x4, waiting for transfers between devices, shift_blocks(): lax.ppermute(value, ALL, [(i, i + steps) for i in range(first, last)])  31.9 us
    all_to_all x1, waiting for transfers between devices, shards(): lax.all_to_all(back.reshape(EXPERTS, CAPP, BACK), CTX, 0, 0, tiled=True)  12.7 us
    all_to_all x1, starting transfers between devices, shards(): lax.all_to_all(partial.reshape(16, SEG, DP), ('z', 'xh'), 0, 0, tiled=True)  12.7 us
    pallas_call x1, Pallas kernels, shards(): call(late_kernel, 'svvhhhh', [out(shares_shape), out((TOK, 2 * KV)), out(...  11.9 us
    ppermute x4, starting transfers between devices, shift_blocks(): lax.ppermute(value, ALL, [(i, i + steps) for i in range(first, last)])  10.5 us
    pallas_call x1, Pallas kernels, shards(): call(shares_kernel, 'vvvvv', [out(shares_shape), out(qt_shape), out(kt_sh...  9.67 us
    all_to_all x1, starting transfers between devices, shards(): lax.all_to_all(back.reshape(EXPERTS, CAPP, BACK), CTX, 0, 0, tiled=True)  8.79 us
    ppermute x1, waiting for transfers between devices, shards(): o_across = lax.ppermute(o_placed, 'xh', SWAP)  8.75 us
  transfers between devices with their start and end apart: 14, of which 8 were waited for; matrix products, arithmetic and copies ran while one was open for 4% of the time, Pallas kernels for 25%

profile of v6, /device:TPU:4, one launch (start us, length us, event | category | flops | bytes accessed | tf_op | source)
XLA Modules:
  0.0 194.8 jit_solution(5194641963474613061)
XLA Ops:
  7.2 0.0 all-gather.3.cloned.1.call-start
  7.2 0.9 pad.8
  8.2 7.8 %collective-permute-start = (bf16[48,1536]{1,0:T(8,128)(2,1)S(1)}, bf16[48,1536]{1,0:T(8,128)(2,1)S(1)}, u32[]{:S(2)}, u32[]{:S(2)}) collective-permute-start(bf16[48,1536]{1,0:T(8,128)(2,1)S(1)} %pad.8), channel_id=1, source_target_pairs={{0,2},{2,0},{1,3},{3,1},{4,6},{6,4},{5,7},{7,5},{8,10},{10,8},{9,1... | collective-permute-start | bytes 442376 | tf_op jit(solution)/shard_map/ppermute | solution.py:324
  16.0 3.1 %collective-permute-done = bf16[48,1536]{1,0:T(8,128)(2,1)S(1)} collective-permute-done((bf16[48,1536]{1,0:T(8,128)(2,1)S(1)}, bf16[48,1536]{1,0:T(8,128)(2,1)S(1)}, u32[]{:S(2)}, u32[]{:S(2)}) %collective-permute-start) | collective-permute-done | bytes 147488 | tf_op jit(solution)/shard_map/ppermute | solution.py:324
  19.1 1.0 broadcast_select_fusion.1
  20.0 0.7 pad_maximum_fusion
  20.8 0.0 all-gather.3.cloned.1.call-update
  20.8 0.7 broadcast_in_dim.10
  21.5 0.7 broadcast_in_dim_reshape.4.held_ref
  22.2 1.2 convert_bitcast_fusion.3
  23.4 0.1 copy.27
  23.6 1.3 convert_bitcast_fusion.gate_ref
  24.8 0.7 compare_select_fusion.place_ref
  25.6 5.5 %shard_map.163 = (bf16[128,3072]{1,0:T(8,128)(2,1)}, bf16[64,1536]{1,0:T(8,128)(2,1)}, bf16[128,128]{1,0:T(8,128)(2,1)}, bf16[128,1536]{1,0:T(8,128)(2,1)}) custom-call(s32[4,128]{1,0:T(4,128)} %bitcast.37, s32[128,1]{1,0:T(8,128)} %broadcast_in_dim_reshape.4.held_ref, f32[4,128]{1,0:T(4,128)} %convert_bitcast_fusion.gate_ref, ...), custom_call_target="tpu_custom_call" | custom-call | bytes 7380000 | tf_op jit(solution)/shard_map/pallas_call | solution.py:358
  31.0 5.9 %all-to-all-start = ((bf16[16,8,3072]{2,1,0:T(8,128)(2,1)}), bf16[16,8,3072]{2,1,0:T(8,128)(2,1)S(1)}, u32[]{:S(2)}, u32[]{:S(2)}) async-start(bf16[16,8,3072]{2,1,0:T(8,128)(2,1)} %bitcast.30), calls=%async_computation | async-start | bytes 1572864 | tf_op jit(solution)/shard_map/all_to_all | solution.py:366
  37.0 0.0 all-gather.5.cloned.1.call-start
  37.1 1.9 collective-permute-start.1
  39.0 4.5 %collective-permute-start.2 = (bf16[128,640]{1,0:T(8,128)(2,1)S(1)}, bf16[128,640]{1,0:T(8,128)(2,1)S(1)}, u32[]{:S(2)}, u32[]{:S(2)}) collective-permute-start(bf16[128,640]{1,0:T(8,128)(2,1)S(1)} %fusion.1.own_ref), channel_id=1, source_target_pairs={{0,2},{1,3},{2,4},{3,5},{4,6},{5,7},{6,8},{7,9},{8,10},{9,11},{10,... | collective-permute-start | bytes 491528 | tf_op jit(solution)/shard_map/ppermute | solution.py:333
  43.5 2.9 %collective-permute-start.3 = (bf16[64,1536]{1,0:T(8,128)(2,1)}, bf16[64,1536]{1,0:T(8,128)(2,1)S(1)}, u32[]{:S(2)}, u32[]{:S(2)}) collective-permute-start(bf16[64,1536]{1,0:T(8,128)(2,1)} %get-tuple-element.39), channel_id=1, source_target_pairs={{0,2},{2,0},{1,3},{3,1},{4,6},{6,4},{5,7},{7,5},{8,10},{10,8},{9,1... | collective-permute-start | bytes 589832 | tf_op jit(solution)/shard_map/ppermute | solution.py:370
  46.4 1.0 constant_dynamic-update-slice_fusion.1
  47.4 3.4 %collective-permute-done.2.far_ref = bf16[128,640]{1,0:T(8,128)(2,1)S(1)} collective-permute-done((bf16[128,640]{1,0:T(8,128)(2,1)S(1)}, bf16[128,640]{1,0:T(8,128)(2,1)S(1)}, u32[]{:S(2)}, u32[]{:S(2)}) %collective-permute-start.2) | collective-permute-done | bytes 163872 | tf_op jit(solution)/shard_map/ppermute | solution.py:333
  50.7 8.7 %collective-permute-done.3 = bf16[64,1536]{1,0:T(8,128)(2,1)S(1)} collective-permute-done((bf16[64,1536]{1,0:T(8,128)(2,1)}, bf16[64,1536]{1,0:T(8,128)(2,1)S(1)}, u32[]{:S(2)}, u32[]{:S(2)}) %collective-permute-start.3) | collective-permute-done | bytes 196640 | tf_op jit(solution)/shard_map/ppermute | solution.py:370
  59.5 0.8 copy-done.3
  60.3 0.0 all-gather.5.cloned.1.call-update
  60.3 9.7 %shard_map.164 = (bf16[384,4096]{1,0:T(8,128)(2,1)}, bf16[2048,128]{1,0:T(8,128)(2,1)}, bf16[256,384]{1,0:T(8,128)(2,1)}, bf16[384,256]{1,0:T(8,128)(2,1)}) custom-call(bf16[128,2048]{1,0:T(8,128)(2,1)} %q_ref.1, bf16[128,640]{1,0:T(8,128)(2,1)} %copy-done.7, bf16[128,640]{1,0:T(8,128)(2,1)} %copy-done.6, bf16[128,640]{1,0:T(8,128)(2,1)} %copy-done.4, ...), custom_call_target="tpu_custom_call" | custom-call | bytes 29520000 | tf_op jit(solution)/shard_map/pallas_call | solution.py:374
  70.0 3.0 %collective-permute-start.4 = (bf16[128,3072]{1,0:T(8,128)(2,1)S(1)}, bf16[128,3072]{1,0:T(8,128)(2,1)}, u32[]{:S(2)}, u32[]{:S(2)}) collective-permute-start(bf16[128,3072]{1,0:T(8,128)(2,1)S(1)} %bitcast.27), channel_id=1, source_target_pairs={{0,1},{1,0},{2,3},{3,2},{4,5},{5,4},{6,7},{7,6},{8,9},{9,8},{10,11... | collective-permute-start | bytes 2359304 | tf_op jit(solution)/shard_map/ppermute | solution.py:392
  73.0 2.0 %collective-permute-done.4.got2_ref = bf16[128,3072]{1,0:T(8,128)(2,1)} collective-permute-done((bf16[128,3072]{1,0:T(8,128)(2,1)S(1)}, bf16[128,3072]{1,0:T(8,128)(2,1)}, u32[]{:S(2)}, u32[]{:S(2)}) %collective-permute-start.4) | collective-permute-done | bytes 786464 | tf_op jit(solution)/shard_map/ppermute | solution.py:392
  75.1 2.3 %collective-permute-start.5 = (bf16[768,1536]{1,0:T(8,128)(2,1)}, bf16[768,1536]{1,0:T(8,128)(2,1)S(1)}, u32[]{:S(2)}, u32[]{:S(2)}) collective-permute-start(bf16[768,1536]{1,0:T(8,128)(2,1)} %all-gather.3.cloned.1.call-done.wm_any), channel_id=1, source_target_pairs={{0,1},{1,0},{2,3},{3,2},{4,5},{5,4},{6,7},{7,6},{8,9},{9,8},{10,11... | collective-permute-start | bytes 7077896 | tf_op jit(solution)/shard_map/ppermute | solution.py:396
  77.3 4.3 %collective-permute-done.5.wo_ref = bf16[768,1536]{1,0:T(8,128)(2,1)S(1)} collective-permute-done((bf16[768,1536]{1,0:T(8,128)(2,1)}, bf16[768,1536]{1,0:T(8,128)(2,1)S(1)}, u32[]{:S(2)}, u32[]{:S(2)}) %collective-permute-start.5) | collective-permute-done | bytes 2359328 | tf_op jit(solution)/shard_map/ppermute | solution.py:396
  81.7 1.4 copy-done.1
  83.1 7.9 %shard_map.165 = (bf16[128,1664]{1,0:T(8,128)(2,1)}, bf16[256,1536]{1,0:T(8,128)(2,1)}, bf16[256,768]{1,0:T(8,128)(2,1)}) custom-call(bf16[128,3072]{1,0:T(8,128)(2,1)} %bitcast.28, bf16[128,3072]{1,0:T(8,128)(2,1)} %collective-permute-done.4.got2_ref, bf16[768,1536]{1,0:T(8,128)(2,1)} %copy-done.1, bf16[768,1536]{1,0:T(8,128)(2,1)} %all-gather.3.cloned.1.call-done.wm_any), custom_call_target="tpu_custom_call" | custom-call | bytes 11070000 | tf_op jit(solution)/shard_map/pallas_call | solution.py:397
  91.0 8.8 %all-to-all-start.1 = ((bf16[16,8,1664]{2,1,0:T(8,128)(2,1)}), bf16[16,8,1664]{2,1,0:T(8,128)(2,1)S(1)}, u32[]{:S(2)}, u32[]{:S(2)}) async-start(bf16[16,8,1664]{2,1,0:T(8,128)(2,1)} %bitcast.33), calls=%async_computation.1 | async-start | bytes 851968 | tf_op jit(solution)/shard_map/all_to_all | solution.py:412
  99.8 3.1 %shard_map.169 = bf16[768,1536]{1,0:T(8,128)(2,1)} custom-call(bf16[256,768]{1,0:T(8,128)(2,1)} %get-tuple-element.63.x_any, bf16[256,1536]{1,0:T(8,128)(2,1)} %get-tuple-element.64.pg_any), custom_call_target="tpu_custom_call" | custom-call | bytes 11070000 | tf_op jit(solution)/shard_map/pallas_call | solution.py:414
  102.9 12.7 %all-to-all-done.1 = bf16[16,8,1664]{2,1,0:T(8,128)(2,1)S(1)} async-done(((bf16[16,8,1664]{2,1,0:T(8,128)(2,1)}), bf16[16,8,1664]{2,1,0:T(8,128)(2,1)S(1)}, u32[]{:S(2)}, u32[]{:S(2)}) %all-to-all-start.1) | async-done | bytes 426016 | tf_op jit(solution)/shard_map/all_to_all | solution.py:412
  115.6 12.7 %all-to-all-start.2 = ((bf16[16,48,1536]{2,1,0:T(8,128)(2,1)}), bf16[16,48,1536]{2,1,0:T(8,128)(2,1)S(1)}, u32[]{:S(2)}, u32[]{:S(2)}) async-start(bf16[16,48,1536]{2,1,0:T(8,128)(2,1)} %bitcast.26), calls=%async_computation.2 | async-start | bytes 4718592 | tf_op jit(solution)/shard_map/all_to_all | solution.py:428
  128.4 2.1 %collective-permute-start.6 = (bf16[1024,1536]{1,0:T(8,128)(2,1)}, bf16[1024,1536]{1,0:T(8,128)(2,1)}, u32[]{:S(2)}, u32[]{:S(2)}) collective-permute-start(bf16[1024,1536]{1,0:T(8,128)(2,1)} %all-gather.5.cloned.1.call-done.om_any), channel_id=1, source_target_pairs={{0,1},{1,0},{2,3},{3,2},{4,5},{5,4},{6,7},{7,6},{8,9},{9,8},{10,11... | collective-permute-start | bytes 9437192 | tf_op jit(solution)/shard_map/ppermute | solution.py:432
  130.5 0.6 pad_add_fusion.at_ref
  131.1 5.0 %shard_map.166 = (f32[4,128]{1,0:T(4,128)}, bf16[128,1536]{1,0:T(8,128)(2,1)}, bf16[128,1536]{1,0:T(8,128)(2,1)}, bf16[1024,128]{1,0:T(8,128)(2,1)}) custom-call(s32[4,128]{1,0:T(4,128)} %bitcast.38, s32[128,1]{1,0:T(8,128)} %broadcast_in_dim_reshape.4.held_ref, bf16[128,1664]{1,0:T(8,128)(2,1)} %bitcast.29, bf16[128,128]{1,0:T(8,128)(2,1)} %get-tuple-element.47.sent_any, ...), custom_call_target="tpu_custom_call" | custom-call | bytes 11070000 | tf_op jit(solution)/shard_map/pallas_call | solution.py:435
  136.2 0.1 collective-permute-done.6.oo_any
  136.3 11.9 %shard_map.167 = (bf16[384,4096]{1,0:T(8,128)(2,1)}, bf16[128,512]{1,0:T(8,128)(2,1)}, bf16[128,512]{1,0:T(8,128)(2,1)}, f32[128,512]{1,0:T(8,128)}) custom-call(s32[2]{0:T(128)} %pad_add_fusion.at_ref, bf16[1024,128]{1,0:T(8,128)(2,1)} %get-tuple-element.50.cotm_ref, bf16[128,1536]{1,0:T(8,128)(2,1)} %get-tuple-element.51.hidden_ref, ...), custom_call_target="tpu_custom_call" | custom-call | bytes 369000 | tf_op jit(solution)/shard_map/pallas_call | solution.py:449
  148.2 2.1 %collective-permute-start.7 = (bf16[128,512]{1,0:T(8,128)(2,1)}, bf16[128,512]{1,0:T(8,128)(2,1)S(1)}, u32[]{:S(2)}, u32[]{:S(2)}) collective-permute-start(bf16[128,512]{1,0:T(8,128)(2,1)} %get-tuple-element.59), channel_id=1, source_target_pairs={{1,0},{2,1},{3,2},{4,3},{5,4},{6,5},{7,6},{8,7},{9,8},{10,9},{11,1... | collective-permute-start | bytes 393224 | tf_op jit(solution)/shard_map/ppermute | solution.py:333
  150.3 1.9 collective-permute-start.8
  152.3 0.6 convert_bitcast_fusion.1
  152.8 4.8 %shard_map.168 = (bf16[128,2048]{1,0:T(8,128)(2,1)}, bf16[1440,128]{1,0:T(8,128)(2,1)}) custom-call(bf16[384,4096]{1,0:T(8,128)(2,1)} %get-tuple-element.54.sg_ref, bf16[256,384]{1,0:T(8,128)(2,1)} %get-tuple-element.55.kt_ref, bf16[128,1536]{1,0:T(8,128)(2,1)} %get-tuple-element.56.src_ref, s32[1,1536]{1,0:T(1,128)} %compare_select_fusion.place_ref), custom_call_target="tpu_custom_call" | custom-call | bytes 369000 | tf_op jit(solution)/shard_map/pallas_call | solution.py:473
  157.7 28.5 %collective-permute-done.8 = bf16[128,512]{1,0:T(8,128)(2,1)S(1)} collective-permute-done((bf16[128,512]{1,0:T(8,128)(2,1)}, bf16[128,512]{1,0:T(8,128)(2,1)S(1)}, u32[]{:S(2)}, u32[]{:S(2)}) %collective-permute-start.8) | collective-permute-done | bytes 131104 | tf_op jit(solution)/shard_map/ppermute | solution.py:333
  186.2 0.7 fusion.8
  186.9 0.3 reduce
  187.3 0.7 slice_bitcast_fusion
  (31 shorter events, 0.2 us)
Async XLA Ops:
  7.2 29.9 %copy-start.9 = (bf16[128,256]{1,0:T(8,128)(2,1)S(1)}, bf16[128,256]{1,0:T(8,128)(2,1)}, u32[]{:S(2)}) copy-start(bf16[128,256]{1,0:T(8,128)(2,1)} %param.13) | copy-start | bytes 196612
  7.2 29.9 %copy-start.8 = (bf16[128,256]{1,0:T(8,128)(2,1)S(1)}, bf16[128,256]{1,0:T(8,128)(2,1)}, u32[]{:S(2)}) copy-start(bf16[128,256]{1,0:T(8,128)(2,1)} %param.14) | copy-start | bytes 196612
  7.2 67.9 %all-gather.3.cloned.1.call-start = ((), (), s32[]{:S(2)}) async-start(), calls=%async_computation.3 | async-start | bytes 2654208 | tf_op jit(solution)/shard_map/all_gather | solution.py:341
  8.2 10.9 %collective-permute-start = (bf16[48,1536]{1,0:T(8,128)(2,1)S(1)}, bf16[48,1536]{1,0:T(8,128)(2,1)S(1)}, u32[]{:S(2)}, u32[]{:S(2)}) collective-permute-start(bf16[48,1536]{1,0:T(8,128)(2,1)S(1)} %pad.8), channel_id=1, source_target_pairs={{0,2},{2,0},{1,3},{3,1},{4,6},{6,4},{5,7},{7,5},{8,10},{10,8},{9,1... | collective-permute-start | bytes 442376 | tf_op jit(solution)/shard_map/ppermute | solution.py:324
  31.0 38.9 %all-to-all-start = ((bf16[16,8,3072]{2,1,0:T(8,128)(2,1)}), bf16[16,8,3072]{2,1,0:T(8,128)(2,1)S(1)}, u32[]{:S(2)}, u32[]{:S(2)}) async-start(bf16[16,8,3072]{2,1,0:T(8,128)(2,1)} %bitcast.30), calls=%async_computation | async-start | bytes 1572864 | tf_op jit(solution)/shard_map/all_to_all | solution.py:366
  37.0 91.4 %all-gather.5.cloned.1.call-start = ((), (), s32[]{:S(2)}) async-start(), calls=%async_computation.4 | async-start | bytes 3538944 | tf_op jit(solution)/shard_map/all_gather | solution.py:394
  37.1 23.2 %copy-start.4 = (bf16[128,640]{1,0:T(8,128)(2,1)}, bf16[128,640]{1,0:T(8,128)(2,1)S(1)}, u32[]{:S(2)}) copy-start(bf16[128,640]{1,0:T(8,128)(2,1)S(1)} %fusion.1.own_ref) | copy-start | bytes 491524
  37.1 10.3 %collective-permute-start.1 = (bf16[128,640]{1,0:T(8,128)(2,1)S(1)}, bf16[128,640]{1,0:T(8,128)(2,1)S(1)}, u32[]{:S(2)}, u32[]{:S(2)}) collective-permute-start(bf16[128,640]{1,0:T(8,128)(2,1)S(1)} %fusion.1.own_ref), channel_id=1, source_target_pairs={{0,1},{1,2},{2,3},{3,4},{4,5},{5,6},{6,7},{7,8},{8,9},{9,10},{10,1... | collective-permute-start | bytes 491528 | tf_op jit(solution)/shard_map/ppermute | solution.py:333
  39.0 11.7 %collective-permute-start.2 = (bf16[128,640]{1,0:T(8,128)(2,1)S(1)}, bf16[128,640]{1,0:T(8,128)(2,1)S(1)}, u32[]{:S(2)}, u32[]{:S(2)}) collective-permute-start(bf16[128,640]{1,0:T(8,128)(2,1)S(1)} %fusion.1.own_ref), channel_id=1, source_target_pairs={{0,2},{1,3},{2,4},{3,5},{4,6},{5,7},{6,8},{7,9},{8,10},{9,11},{10,... | collective-permute-start | bytes 491528 | tf_op jit(solution)/shard_map/ppermute | solution.py:333
  43.5 16.0 %collective-permute-start.3 = (bf16[64,1536]{1,0:T(8,128)(2,1)}, bf16[64,1536]{1,0:T(8,128)(2,1)S(1)}, u32[]{:S(2)}, u32[]{:S(2)}) collective-permute-start(bf16[64,1536]{1,0:T(8,128)(2,1)} %get-tuple-element.39), channel_id=1, source_target_pairs={{0,2},{2,0},{1,3},{3,1},{4,6},{6,4},{5,7},{7,5},{8,10},{10,8},{9,1... | collective-permute-start | bytes 589832 | tf_op jit(solution)/shard_map/ppermute | solution.py:370
  47.4 12.9 %copy-start.6 = (bf16[128,640]{1,0:T(8,128)(2,1)}, bf16[128,640]{1,0:T(8,128)(2,1)S(1)}, u32[]{:S(2)}) copy-start(bf16[128,640]{1,0:T(8,128)(2,1)S(1)} %collective-permute-done.1.near_ref) | copy-start | bytes 491524
  50.7 9.6 %copy-start.7 = (bf16[128,640]{1,0:T(8,128)(2,1)}, bf16[128,640]{1,0:T(8,128)(2,1)S(1)}, u32[]{:S(2)}) copy-start(bf16[128,640]{1,0:T(8,128)(2,1)S(1)} %collective-permute-done.2.far_ref) | copy-start | bytes 491524
  59.5 0.8 copy-start.3
  70.0 11.7 %copy-start = (bf16[16,8,3072]{2,1,0:T(8,128)(2,1)}, bf16[16,8,3072]{2,1,0:T(8,128)(2,1)S(1)}, u32[]{:S(2)}) copy-start(bf16[16,8,3072]{2,1,0:T(8,128)(2,1)S(1)} %all-to-all-done) | copy-start | bytes 2359300
  70.0 5.0 %collective-permute-start.4 = (bf16[128,3072]{1,0:T(8,128)(2,1)S(1)}, bf16[128,3072]{1,0:T(8,128)(2,1)}, u32[]{:S(2)}, u32[]{:S(2)}) collective-permute-start(bf16[128,3072]{1,0:T(8,128)(2,1)S(1)} %bitcast.27), channel_id=1, source_target_pairs={{0,1},{1,0},{2,3},{3,2},{4,5},{5,4},{6,7},{7,6},{8,9},{9,8},{10,11... | collective-permute-start | bytes 2359304 | tf_op jit(solution)/shard_map/ppermute | solution.py:392
  75.1 6.6 %collective-permute-start.5 = (bf16[768,1536]{1,0:T(8,128)(2,1)}, bf16[768,1536]{1,0:T(8,128)(2,1)S(1)}, u32[]{:S(2)}, u32[]{:S(2)}) collective-permute-start(bf16[768,1536]{1,0:T(8,128)(2,1)} %all-gather.3.cloned.1.call-done.wm_any), channel_id=1, source_target_pairs={{0,1},{1,0},{2,3},{3,2},{4,5},{5,4},{6,7},{7,6},{8,9},{9,8},{10,11... | collective-permute-start | bytes 7077896 | tf_op jit(solution)/shard_map/ppermute | solution.py:396
  81.7 1.4 copy-start.1
  91.0 24.6 %all-to-all-start.1 = ((bf16[16,8,1664]{2,1,0:T(8,128)(2,1)}), bf16[16,8,1664]{2,1,0:T(8,128)(2,1)S(1)}, u32[]{:S(2)}, u32[]{:S(2)}) async-start(bf16[16,8,1664]{2,1,0:T(8,128)(2,1)} %bitcast.33), calls=%async_computation.1 | async-start | bytes 851968 | tf_op jit(solution)/shard_map/all_to_all | solution.py:412
  115.6 15.5 %copy-start.2 = (bf16[16,8,1664]{2,1,0:T(8,128)(2,1)}, bf16[16,8,1664]{2,1,0:T(8,128)(2,1)S(1)}, u32[]{:S(2)}) copy-start(bf16[16,8,1664]{2,1,0:T(8,128)(2,1)S(1)} %all-to-all-done.1) | copy-start | bytes 1277956
  115.6 71.3 %all-to-all-start.2 = ((bf16[16,48,1536]{2,1,0:T(8,128)(2,1)}), bf16[16,48,1536]{2,1,0:T(8,128)(2,1)S(1)}, u32[]{:S(2)}, u32[]{:S(2)}) async-start(bf16[16,48,1536]{2,1,0:T(8,128)(2,1)} %bitcast.26), calls=%async_computation.2 | async-start | bytes 4718592 | tf_op jit(solution)/shard_map/all_to_all | solution.py:428
  128.4 7.9 %collective-permute-start.6 = (bf16[1024,1536]{1,0:T(8,128)(2,1)}, bf16[1024,1536]{1,0:T(8,128)(2,1)}, u32[]{:S(2)}, u32[]{:S(2)}) collective-permute-start(bf16[1024,1536]{1,0:T(8,128)(2,1)} %all-gather.5.cloned.1.call-done.om_any), channel_id=1, source_target_pairs={{0,1},{1,0},{2,3},{3,2},{4,5},{5,4},{6,7},{7,6},{8,9},{9,8},{10,11... | collective-permute-start | bytes 9437192 | tf_op jit(solution)/shard_map/ppermute | solution.py:432
  136.3 16.0 %copy-start.10 = (f32[4,128]{1,0:T(4,128)S(1)}, f32[4,128]{1,0:T(4,128)}, u32[]{:S(2)}) copy-start(f32[4,128]{1,0:T(4,128)} %get-tuple-element.62) | copy-start | bytes 6148
  148.2 38.0 %copy-start.5 = (f32[128,512]{1,0:T(8,128)S(1)}, f32[128,512]{1,0:T(8,128)}, u32[]{:S(2)}) copy-start(f32[128,512]{1,0:T(8,128)} %get-tuple-element.58) | copy-start | bytes 786436
  148.2 9.5 %collective-permute-start.7 = (bf16[128,512]{1,0:T(8,128)(2,1)}, bf16[128,512]{1,0:T(8,128)(2,1)S(1)}, u32[]{:S(2)}, u32[]{:S(2)}) collective-permute-start(bf16[128,512]{1,0:T(8,128)(2,1)} %get-tuple-element.59), channel_id=1, source_target_pairs={{1,0},{2,1},{3,2},{4,3},{5,4},{6,5},{7,6},{8,7},{9,8},{10,9},{11,1... | collective-permute-start | bytes 393224 | tf_op jit(solution)/shard_map/ppermute | solution.py:333
  150.3 35.9 %collective-permute-start.8 = (bf16[128,512]{1,0:T(8,128)(2,1)}, bf16[128,512]{1,0:T(8,128)(2,1)S(1)}, u32[]{:S(2)}, u32[]{:S(2)}) collective-permute-start(bf16[128,512]{1,0:T(8,128)(2,1)} %get-tuple-element.60), channel_id=1, source_target_pairs={{2,0},{3,1},{4,2},{5,3},{6,4},{7,5},{8,6},{9,7},{10,8},{11,9},{12,... | collective-permute-start | bytes 393224 | tf_op jit(solution)/shard_map/ppermute | solution.py:333
Sparse Core Ops, SparseCore 0:
  20.9 51.3 all-gather.2
  74.4 50.0 all-gather.4

commit v7 on v6

--- a/solution.py
+++ b/solution.py
@@ -25,7 +25,8 @@
 WIDE = 640
 BF = jnp.bfloat16
 F32 = jnp.float32
-ALL = ("y", "xl", "z", "xh", "core")
+ALL = ("y", "xl", "zh", "zl", "xh", "core")
+Z = ("zh", "zl")
 CTX = ("y", "xl")
 SWAP = ((0, 1), (1, 0))
 
@@ -153,63 +154,91 @@
         copy.wait()
 
 
-def expert_kernel(
-    got_ref, got2_ref, wo_ref, wm_any, back_any, pg_any, x_any,
-    wm_ref, back_ref, pg_ref, x_ref, pre_ref, sems,
-):
-    load = pltpu.make_async_copy(wm_any, wm_ref, sems.at[0])
-    load.start()
-    x_mine = jnp.concatenate([got_ref[:, :HALF], got2_ref[:, HALF:DP]], axis=0)
-    x_other = jnp.concatenate([got_ref[:, HALF:DP], got2_ref[:, :HALF]], axis=0)
-    x_ref[...] = x_mine
-    stores = [pltpu.make_async_copy(x_ref, x_any, sems.at[1])]
-    stores[0].start()
-    load.wait()
+def activation_grads(pre_ref, grads, gate, pg_ref):
     step = 512
-    for lo in range(0, DP, step):
-        at = slice(lo, lo + step)
-        pre_ref[:, at] = dot(x_mine, wm_ref[:, at], ((1,), (0,))) + dot(
-            x_other, wo_ref[:, at], ((1,), (0,))
-        )
-    gate_at = slice(DP + F, DP + F + 1)
-    gate = jnp.concatenate([got_ref[:, gate_at], got2_ref[:, gate_at]], axis=0).astype(F32)
-    total = jnp.zeros((2 * ROWS, 1), F32)
+    total = jnp.zeros((pre_ref.shape[0], 1), F32)
     for lo in range(0, DP, step):
         pre = pre_ref[:, lo : lo + step]
-        at = slice(DP + lo, DP + lo + step)
-        grad = jnp.concatenate([got_ref[:, at], got2_ref[:, at]], axis=0).astype(F32)
+        grad = grads(DP + lo, DP + lo + step).astype(F32)
         sig = 1.0 / (1.0 + jnp.exp(-pre))
         total = total + jnp.sum(grad * (pre * sig), axis=1, keepdims=True)
         slope = sig * (1.0 + pre * (1.0 - sig))
         pg_ref[:, lo : lo + step] = (gate * grad * slope).astype(BF)
-    stores.append(pltpu.make_async_copy(pg_ref, pg_any, sems.at[2]))
-    stores[1].start()
-    pg = pg_ref[:ROWS, :]
+    return total
+
+
+def expert_kernel(
+    got_ref, wo_ref, wm_any, back_any, pg_any, wm_ref, back_ref, pg_ref, pre_ref, sems
+):
+    load = pltpu.make_async_copy(wm_any, wm_ref, sems.at[0])
+    load.start()
+    load.wait()
+    for lo in range(0, DP, 512):
+        at = slice(lo, lo + 512)
+        pre_ref[:, at] = dot(got_ref[:, :HALF], wm_ref[:, at], ((1,), (0,))) + dot(
+            got_ref[:, HALF:DP], wo_ref[:, at], ((1,), (0,))
+        )
+    gate = got_ref[:, DP + F : DP + F + 1].astype(F32)
+    total = activation_grads(pre_ref, lambda lo, hi: got_ref[:, lo:hi], gate, pg_ref)
+    stores = [pltpu.make_async_copy(pg_ref, pg_any, sems.at[1])]
+    stores[0].start()
+    pg = pg_ref[...]
     for c in range(HALF // 256):
         r = slice(c * 256, (c + 1) * 256)
         back_ref[:, c * 256 : (c + 1) * 256] = dot(pg, wm_ref[r, :], ((1,), (1,))).astype(BF)
         back_ref[:, HALF + c * 256 : HALF + (c + 1) * 256] = dot(
             pg, wo_ref[r, :], ((1,), (1,))
         ).astype(BF)
-    back_ref[:, DP:] = jnp.broadcast_to(total[:ROWS], (ROWS, BACK - DP)).astype(BF)
-    stores.append(pltpu.make_async_copy(back_ref, back_any, sems.at[3]))
-    stores[2].start()
+    back_ref[:, DP:] = jnp.broadcast_to(total, (ROWS, BACK - DP)).astype(BF)
+    stores.append(pltpu.make_async_copy(back_ref, back_any, sems.at[2]))
+    stores[1].start()
     for copy in stores:
         copy.wait()
 
 
-def map_kernel(x_any, pg_any, part_any, x_ref, pg_ref, part_ref, sems):
-    loads = copies_of(((x_any, x_ref), (pg_any, pg_ref)), sems)
+def map_kernel(
+    at_ref, wm_any, wo_any, own_any, near_any, core_any, far_any, pg_any, part_any,
+    wm_ref, wo_ref, own_ref, near_ref, core_ref, far_ref, own_pg_ref, pg_ref, pre_ref, part_ref,
+    sems,
+):
+    pairs = (
+        (near_any, near_ref), (core_any, core_ref), (far_any, far_ref), (wm_any, wm_ref),
+        (wo_any, wo_ref), (own_any, own_ref), (pg_any, own_pg_ref),
+    )
+    loads = copies_of(pairs, sems)
     for copy in loads:
         copy.start()
     for copy in loads:
         copy.wait()
-    stores = []
+
+    def columns(lo, hi):
+        return jnp.concatenate(
+            [near_ref[:, lo:hi], core_ref[:, lo:hi], far_ref[:, lo:hi]], axis=0
+        )
+
+    first, second = slice(0, HALF), slice(HALF, DP)
+    x_mine = jnp.concatenate([near_ref[:, first], core_ref[:, second], far_ref[:, second]], axis=0)
+    x_other = jnp.concatenate([near_ref[:, second], core_ref[:, first], far_ref[:, first]], axis=0)
+    for lo in range(0, DP, 512):
+        at = slice(lo, lo + 512)
+        pre_ref[:, at] = dot(x_mine, wm_ref[:, at], ((1,), (0,))) + dot(
+            x_other, wo_ref[:, at], ((1,), (0,))
+        )
+    gate = columns(DP + F, DP + F + 1).astype(F32)
+    activation_grads(pre_ref, columns, gate, pg_ref)
+    pg = jnp.concatenate([own_pg_ref[...], pg_ref[...]], axis=0)
     for c in range(HALF // 256):
         r = slice(c * 256, (c + 1) * 256)
-        part_ref[r, :] = dot(x_ref[:, r], pg_ref[...], ((0,), (0,))).astype(BF)
+        x = jnp.concatenate([own_ref[:, r], x_mine[:, r]], axis=0)
+        part_ref[r, :] = dot(x, pg, ((0,), (0,))).astype(BF)
+    stores = []
+    for k in range(4):
+        rows = pl.ds(pl.multiple_of((2 * k + at_ref[2]) * 2 * SEG, 2 * SEG), 2 * SEG)
         stores.append(
-            pltpu.make_async_copy(part_ref.at[r, :], part_any.at[r, :], sems.at[2 + c])
+            pltpu.make_async_copy(
+                part_ref.at[rows, :], part_any.at[k * 2 * SEG : (k + 1) * 2 * SEG, :],
+                sems.at[7 + k],
+            )
         )
         stores[-1].start()
     for copy in stores:
@@ -338,7 +367,7 @@
     xh = lax.axis_index("xh")
     w_pad = jnp.pad(weights[0], ((0, SEG - SHARD), (0, DP - F)))
     w_pair = both_xh(w_pad)
-    w_mine = lax.all_gather(w_pair, "z", axis=0, tiled=True)
+    w_mine = lax.all_gather(w_pair, Z, axis=0, tiled=True)
 
     plus = (label + 1).astype(jnp.int32)
     marks = jnp.stack([plus // 16, plus % 16], axis=1).astype(BF)
@@ -368,7 +397,7 @@
     near = shift_blocks(own, 1)
     far = shift_blocks(own, 2)
     o_across = lax.ppermute(o_placed, "xh", SWAP)
-    near, far, o_across = lax.optimization_barrier((near, far, o_across))
+    near, far, o_across, got = lax.optimization_barrier((near, far, o_across, got))
     shares_shape, qt_shape = (3 * TOK, HEADS * TOK), (HEADS * HD, TOK)
     kt_shape, v_shape = (KV, 3 * TOK), (3 * TOK, KV)
     shares, q_t, k_t, v_win = call(
@@ -388,49 +417,55 @@
         8,
     )(q, far, near, own, plus.astype(F32)[None, :])
 
-    got = order(got, v_win).reshape(ROWS, SEND)
-    got_other = lax.ppermute(got, "core", SWAP)
+    got = got.reshape(ROWS, SEND)
+    got_near = lax.ppermute(got, "zl", SWAP)
+    got_core = lax.ppermute(order(got, v_win), "core", SWAP)
     o_pair = jnp.concatenate([o_placed, o_across], axis=0)
-    o_mine = lax.all_gather(o_pair, "z", axis=0, tiled=True)
-    w_mine = order(w_mine, got_other, o_pair)
+    o_mine = lax.all_gather(o_pair, Z, axis=0, tiled=True)
+    w_mine = order(w_mine, got_core, o_pair)
     w_other = lax.ppermute(w_mine, "core", SWAP)
-    back, pg, x_mine = call(
+    spot = jnp.stack([core, xh, lax.axis_index("zl")]).astype(jnp.int32)
+    back, pg = call(
         expert_kernel,
-        "vvvh",
-        [out((ROWS, BACK)), out((2 * ROWS, DP)), out((2 * ROWS, HALF))],
-        "hhh",
+        "vvh",
+        [out((ROWS, BACK)), out((ROWS, DP))],
+        "hh",
         [
             pltpu.VMEM((HALF, DP), BF),
             pltpu.VMEM((ROWS, BACK), BF),
-            pltpu.VMEM((2 * ROWS, DP), BF),
-            pltpu.VMEM((2 * ROWS, HALF), BF),
-            pltpu.VMEM((2 * ROWS, DP), F32),
-            dma((4,)),
+            pltpu.VMEM((ROWS, DP), BF),
+            pltpu.VMEM((ROWS, DP), F32),
+            dma((3,)),
         ],
         3,
-    )(got, got_other, w_other, w_mine)
+    )(got, w_other, w_mine)
+    got_far = lax.ppermute(order(got_near, pg), "core", SWAP)
     returned = lax.all_to_all(back.reshape(EXPERTS, CAPP, BACK), CTX, 0, 0, tiled=True)
     returned = returned.reshape(ROWS, BACK)
     partial = call(
         map_kernel,
-        "hh",
-        [out((HALF, DP))],
+        "shhhhhhh",
+        [out((HALF // 2, DP))],
         "h",
         [
-            pltpu.VMEM((2 * ROWS, HALF), BF),
-            pltpu.VMEM((2 * ROWS, DP), BF),
             pltpu.VMEM((HALF, DP), BF),
-            dma((5,)),
+            pltpu.VMEM((HALF, DP), BF),
+            pltpu.VMEM((ROWS, SEND), BF),
+            pltpu.VMEM((ROWS, SEND), BF),
+            pltpu.VMEM((ROWS, SEND), BF),
+            pltpu.VMEM((ROWS, SEND), BF),
+            pltpu.VMEM((ROWS, DP), BF),
+            pltpu.VMEM((3 * ROWS, DP), BF),
+            pltpu.VMEM((3 * ROWS, DP), F32),
+            pltpu.VMEM((HALF, DP), BF),
+            dma((11,)),
         ],
-        3,
-    )(x_mine, pg)[0]
+        8,
+    )(spot, w_mine, w_other, got, got_near, got_core, got_far, pg)[0]
     partial = order(partial, returned)
-    terms = lax.all_to_all(partial.reshape(16, SEG, DP), ("z", "xh"), 0, 0, tiled=True)
-    map_grad = jnp.sum(terms.astype(F32), axis=0)[None, :SHARD, :F].astype(BF)
-
-    o_mine = order(o_mine, returned)
+    terms = lax.all_to_all(partial.reshape(8, SEG, DP), ("zh", "xh"), 0, 0, tiled=True)
+    o_mine = order(o_mine, returned, partial)
     o_other = lax.ppermute(o_mine, "core", SWAP)
-    spot = jnp.stack([core, xh]).astype(jnp.int32)
     half_shape = (16 * HD, DP)
     gate_t, src, hidden, cot_mine = call(
         combine_kernel,
@@ -468,12 +503,14 @@
         ],
         0.1,
     )(spot, cot_mine, hidden, v_win, o_other, q_t, shares)
-    got_near = shift_blocks(near_g, -1)
-    got_far = shift_blocks(far_g, -2)
+    got_next = shift_blocks(near_g, -1)
+    got_last = shift_blocks(far_g, -2)
+    terms = order(terms, got_next, got_last)
+    map_grad = jnp.sum(terms.astype(F32), axis=0)[None, :SHARD, :F].astype(BF)
     q_grad, src_t = call(
         query_kernel, "vvvv", [out((TOK, HEADS * HD)), out((D, TOK))], "vv", [], 0.1
     )(sg, k_t, src, place)
-    kv_grad = (own_g + got_near.astype(F32) + got_far.astype(F32)).astype(BF)
+    kv_grad = (own_g + got_next.astype(F32) + got_last.astype(F32)).astype(BF)
     return (
         q_grad,
         kv_grad[:, :KV],
@@ -485,9 +522,9 @@
 
 
 def solution(mesh):
-    fine = Mesh(mesh.devices.reshape(8, 2, 8, 2, 2), ALL)
+    fine = Mesh(mesh.devices.reshape(8, 2, 4, 2, 2, 2), ALL)
     rows = P(ALL, None)
-    fsdp = ("z", "xh", "core")
+    fsdp = ("zh", "zl", "xh", "core")
     return jax.shard_map(
         shards,
         mesh=fine,

time: 196 us -> 188 us (0.959)
  the two profiles are of different devices: /device:TPU:4 before, /device:TPU:49 now
where the time goes in v7:
time: 188 us; the launch traced here: 187 us
  starting transfers between devices  56.9 us (30%)
  Pallas kernels  52.4 us (28%)
  waiting for transfers between devices  49.5 us (26%)
  between operations  14.4 us (8%)
  local copies, waits for them, and re-layouts  7.95 us (4%)
  other arithmetic  5.69 us (3%)
    ppermute x4, waiting for transfers between devices, shift_blocks(): lax.ppermute(value, ALL, [(i, i + steps) for i in range(first, last)])  20.2 us
    ppermute x1, waiting for transfers between devices, shards(): got_near = lax.ppermute(got, 'zl', SWAP)  19.9 us
    ppermute x4, starting transfers between devices, shift_blocks(): lax.ppermute(value, ALL, [(i, i + steps) for i in range(first, last)])  19.8 us
    pallas_call x1, Pallas kernels, shards(): call(late_kernel, 'svvhhhh', [out(shares_shape), out((TOK, 2 * KV)), out(...  11.9 us
    pallas_call x1, Pallas kernels, shards(): call(shares_kernel, 'vvvvv', [out(shares_shape), out(qt_shape), out(kt_sh...  9.66 us
    pallas_call x1, Pallas kernels, shards(): call(map_kernel, 'shhhhhhh', [out((HALF // 2, DP))], 'h', [pltpu.VMEM((HA...  8.56 us
    all_to_all x1, starting transfers between devices, shards(): lax.all_to_all(send.reshape(EXPERTS, CAPP, SEND), CTX, 0, 0, tiled=True)  7.38 us
    pallas_call x1, Pallas kernels, shards(): call(expert_kernel, 'vvh', [out((ROWS, BACK)), out((ROWS, DP))], 'hh', [p...  6.95 us
  transfers between devices with their start and end apart: 16, of which 8 were waited for; matrix products, arithmetic and copies ran while one was open for 3% of the time, Pallas kernels for 28%

profile of v7, /device:TPU:49, one launch (start us, length us, event | category | flops | bytes accessed | tf_op | source)
XLA Modules:
  0.0 186.9 jit_solution(529838240571025018)
XLA Ops:
  7.2 0.0 all-gather.3.cloned.1.call-start
  7.2 0.9 pad.8
  8.2 4.7 %collective-permute-start = (bf16[48,1536]{1,0:T(8,128)(2,1)S(1)}, bf16[48,1536]{1,0:T(8,128)(2,1)S(1)}, u32[]{:S(2)}, u32[]{:S(2)}) collective-permute-start(bf16[48,1536]{1,0:T(8,128)(2,1)S(1)} %pad.8), channel_id=1, source_target_pairs={{0,2},{2,0},{1,3},{3,1},{4,6},{6,4},{5,7},{7,5},{8,10},{10,8},{9,1... | collective-permute-start | bytes 442376 | tf_op jit(solution)/shard_map/ppermute | solution.py:353
  12.8 3.4 %collective-permute-done = bf16[48,1536]{1,0:T(8,128)(2,1)S(1)} collective-permute-done((bf16[48,1536]{1,0:T(8,128)(2,1)S(1)}, bf16[48,1536]{1,0:T(8,128)(2,1)S(1)}, u32[]{:S(2)}, u32[]{:S(2)}) %collective-permute-start) | collective-permute-done | bytes 147488 | tf_op jit(solution)/shard_map/ppermute | solution.py:353
  16.3 1.0 broadcast_select_fusion.1
  17.3 0.7 pad_maximum_fusion
  18.0 0.7 broadcast_in_dim.10
  18.7 0.7 broadcast_in_dim_reshape.4.held_ref
  19.5 1.3 convert_bitcast_fusion.gate_ref
  20.7 0.7 compare_select_fusion.place_ref
  21.4 5.5 %shard_map.163 = (bf16[128,3072]{1,0:T(8,128)(2,1)}, bf16[64,1536]{1,0:T(8,128)(2,1)}, bf16[128,128]{1,0:T(8,128)(2,1)}, bf16[128,1536]{1,0:T(8,128)(2,1)}) custom-call(s32[4,128]{1,0:T(4,128)} %bitcast.40, s32[128,1]{1,0:T(8,128)} %broadcast_in_dim_reshape.4.held_ref, f32[4,128]{1,0:T(4,128)} %convert_bitcast_fusion.gate_ref, ...), custom_call_target="tpu_custom_call" | custom-call | bytes 7380000 | tf_op jit(solution)/shard_map/pallas_call | solution.py:387
  26.9 7.4 %all-to-all-start = ((bf16[16,8,3072]{2,1,0:T(8,128)(2,1)}), bf16[16,8,3072]{2,1,0:T(8,128)(2,1)S(1)}, u32[]{:S(2)}, u32[]{:S(2)}) async-start(bf16[16,8,3072]{2,1,0:T(8,128)(2,1)} %bitcast.33), calls=%async_computation | async-start | bytes 1572864 | tf_op jit(solution)/shard_map/all_to_all | solution.py:395
  34.4 0.5 convert_bitcast_fusion.3
  34.9 0.1 copy.26
  35.1 6.4 %collective-permute-start.1 = (bf16[128,640]{1,0:T(8,128)(2,1)S(1)}, bf16[128,640]{1,0:T(8,128)(2,1)S(1)}, u32[]{:S(2)}, u32[]{:S(2)}) collective-permute-start(bf16[128,640]{1,0:T(8,128)(2,1)S(1)} %fusion.1.own_ref), channel_id=1, source_target_pairs={{0,1},{1,2},{2,3},{3,4},{4,5},{5,6},{6,7},{7,8},{8,9},{9,10},{10,1... | collective-permute-start | bytes 491528 | tf_op jit(solution)/shard_map/ppermute | solution.py:362
  41.5 4.2 %collective-permute-start.2 = (bf16[128,640]{1,0:T(8,128)(2,1)S(1)}, bf16[128,640]{1,0:T(8,128)(2,1)S(1)}, u32[]{:S(2)}, u32[]{:S(2)}) collective-permute-start(bf16[128,640]{1,0:T(8,128)(2,1)S(1)} %fusion.1.own_ref), channel_id=1, source_target_pairs={{0,2},{1,3},{2,4},{3,5},{4,6},{5,7},{6,8},{7,9},{8,10},{9,11},{10,... | collective-permute-start | bytes 491528 | tf_op jit(solution)/shard_map/ppermute | solution.py:362
  45.7 4.4 %collective-permute-start.3 = (bf16[64,1536]{1,0:T(8,128)(2,1)}, bf16[64,1536]{1,0:T(8,128)(2,1)S(1)}, u32[]{:S(2)}, u32[]{:S(2)}) collective-permute-start(bf16[64,1536]{1,0:T(8,128)(2,1)} %get-tuple-element.41), channel_id=1, source_target_pairs={{0,2},{2,0},{1,3},{3,1},{4,6},{6,4},{5,7},{7,5},{8,10},{10,8},{9,1... | collective-permute-start | bytes 589832 | tf_op jit(solution)/shard_map/ppermute | solution.py:399
  50.1 1.0 constant_dynamic-update-slice_fusion.1
  51.0 18.7 %collective-permute-done.2.far_ref = bf16[128,640]{1,0:T(8,128)(2,1)S(1)} collective-permute-done((bf16[128,640]{1,0:T(8,128)(2,1)S(1)}, bf16[128,640]{1,0:T(8,128)(2,1)S(1)}, u32[]{:S(2)}, u32[]{:S(2)}) %collective-permute-start.2) | collective-permute-done | bytes 163872 | tf_op jit(solution)/shard_map/ppermute | solution.py:362
  69.8 0.8 copy-done.3
  70.6 9.7 %shard_map.164 = (bf16[384,4096]{1,0:T(8,128)(2,1)}, bf16[2048,128]{1,0:T(8,128)(2,1)}, bf16[256,384]{1,0:T(8,128)(2,1)}, bf16[384,256]{1,0:T(8,128)(2,1)}) custom-call(bf16[128,2048]{1,0:T(8,128)(2,1)} %q_ref.1, bf16[128,640]{1,0:T(8,128)(2,1)} %copy-done.8, bf16[128,640]{1,0:T(8,128)(2,1)} %copy-done.7, bf16[128,640]{1,0:T(8,128)(2,1)} %copy-done.5, ...), custom_call_target="tpu_custom_call" | custom-call | bytes 29520000 | tf_op jit(solution)/shard_map/pallas_call | solution.py:403
  80.3 2.4 %collective-permute-start.4 = (bf16[128,3072]{1,0:T(8,128)(2,1)S(1)}, bf16[128,3072]{1,0:T(8,128)(2,1)}, u32[]{:S(2)}, u32[]{:S(2)}) collective-permute-start(bf16[128,3072]{1,0:T(8,128)(2,1)S(1)} %bitcast.27), channel_id=1, source_target_pairs={{0,1},{1,0},{2,3},{3,2},{4,5},{5,4},{6,7},{7,6},{8,9},{9,8},{10,11... | collective-permute-start | bytes 2359304 | tf_op jit(solution)/shard_map/ppermute | solution.py:422
  82.7 2.0 %collective-permute-done.4.core_any = bf16[128,3072]{1,0:T(8,128)(2,1)} collective-permute-done((bf16[128,3072]{1,0:T(8,128)(2,1)S(1)}, bf16[128,3072]{1,0:T(8,128)(2,1)}, u32[]{:S(2)}, u32[]{:S(2)}) %collective-permute-start.4) | collective-permute-done | bytes 786464 | tf_op jit(solution)/shard_map/ppermute | solution.py:422
  84.7 2.3 %collective-permute-start.5 = (bf16[768,1536]{1,0:T(8,128)(2,1)}, bf16[768,1536]{1,0:T(8,128)(2,1)S(1)}, u32[]{:S(2)}, u32[]{:S(2)}) collective-permute-start(bf16[768,1536]{1,0:T(8,128)(2,1)} %all-gather.3.cloned.1.call-done.wm_any), channel_id=1, source_target_pairs={{0,1},{1,0},{2,3},{3,2},{4,5},{5,4},{6,7},{7,6},{8,9},{9,8},{10,11... | collective-permute-start | bytes 7077896 | tf_op jit(solution)/shard_map/ppermute | solution.py:426
  87.0 1.9 %collective-permute-start.6 = (bf16[128,3072]{1,0:T(8,128)(2,1)S(1)}, bf16[128,3072]{1,0:T(8,128)(2,1)}, u32[]{:S(2)}, u32[]{:S(2)}) collective-permute-start(bf16[128,3072]{1,0:T(8,128)(2,1)S(1)} %bitcast.28), channel_id=1, source_target_pairs={{0,4},{4,0},{1,5},{5,1},{2,6},{6,2},{3,7},{7,3},{8,12},{12,8},{9,1... | collective-permute-start | bytes 2359304 | tf_op jit(solution)/shard_map/ppermute | solution.py:421
  88.9 2.4 %collective-permute-done.5.wo_ref.wo_any = bf16[768,1536]{1,0:T(8,128)(2,1)S(1)} collective-permute-done((bf16[768,1536]{1,0:T(8,128)(2,1)}, bf16[768,1536]{1,0:T(8,128)(2,1)S(1)}, u32[]{:S(2)}, u32[]{:S(2)}) %collective-permute-start.5) | collective-permute-done | bytes 2359328 | tf_op jit(solution)/shard_map/ppermute | solution.py:426
  91.3 1.4 copy-done
  92.7 7.0 %shard_map.165 = (bf16[128,1664]{1,0:T(8,128)(2,1)}, bf16[128,1536]{1,0:T(8,128)(2,1)}) custom-call(bf16[128,3072]{1,0:T(8,128)(2,1)} %bitcast.29, bf16[768,1536]{1,0:T(8,128)(2,1)} %copy-done, bf16[768,1536]{1,0:T(8,128)(2,1)} %all-gather.3.cloned.1.call-done.wm_any), custom_call_target="tpu_custom_call" | custom-call | bytes 11070000 | tf_op jit(solution)/shard_map/pallas_call | solution.py:428
  99.7 5.6 %all-to-all-start.1 = ((bf16[16,8,1664]{2,1,0:T(8,128)(2,1)}), bf16[16,8,1664]{2,1,0:T(8,128)(2,1)S(1)}, u32[]{:S(2)}, u32[]{:S(2)}) async-start(bf16[16,8,1664]{2,1,0:T(8,128)(2,1)} %bitcast.36), calls=%async_computation.1 | async-start | bytes 851968 | tf_op jit(solution)/shard_map/all_to_all | solution.py:443
  105.2 19.9 %collective-permute-done.6.near_any = bf16[128,3072]{1,0:T(8,128)(2,1)} collective-permute-done((bf16[128,3072]{1,0:T(8,128)(2,1)S(1)}, bf16[128,3072]{1,0:T(8,128)(2,1)}, u32[]{:S(2)}, u32[]{:S(2)}) %collective-permute-start.6) | collective-permute-done | bytes 786464 | tf_op jit(solution)/shard_map/ppermute | solution.py:421
  125.1 2.5 %collective-permute-start.7 = (bf16[128,3072]{1,0:T(8,128)(2,1)}, bf16[128,3072]{1,0:T(8,128)(2,1)S(1)}, u32[]{:S(2)}, u32[]{:S(2)}) collective-permute-start(bf16[128,3072]{1,0:T(8,128)(2,1)} %collective-permute-done.6.near_any), channel_id=1, source_target_pairs={{0,1},{1,0},{2,3},{3,2},{4,5},{5,4},{6,7},{7,6},{8,9},{9,8},{10,11... | collective-permute-start | bytes 2359304 | tf_op jit(solution)/shard_map/ppermute | solution.py:442
  127.7 0.7 pad_add_fusion.at_ref
  128.3 1.4 collective-permute-done.7.far_any
  129.8 0.9 copy-done.4
  130.7 8.6 %shard_map.166 = bf16[384,1536]{1,0:T(8,128)(2,1)} custom-call(s32[3]{0:T(128)} %pad_add_fusion.at_ref, bf16[768,1536]{1,0:T(8,128)(2,1)} %all-gather.3.cloned.1.call-done.wm_any, bf16[768,1536]{1,0:T(8,128)(2,1)} %copy-done, bf16[128,3072]{1,0:T(8,128)(2,1)} %bitcast.30, bf16[128,3072]{1,0:T(8,128)(2,1)} %collective-permute-done.6.near_any, ...), custom_call_target="tpu_custom_call" | custom-call | bytes 29520000 | tf_op jit(solution)/shard_map/pallas_call | solution.py:445
  139.3 2.3 %collective-permute-start.8 = (bf16[1024,1536]{1,0:T(8,128)(2,1)}, bf16[1024,1536]{1,0:T(8,128)(2,1)}, u32[]{:S(2)}, u32[]{:S(2)}) collective-permute-start(bf16[1024,1536]{1,0:T(8,128)(2,1)} %all-gather.5.cloned.1.call-done.om_any), channel_id=1, source_target_pairs={{0,1},{1,0},{2,3},{3,2},{4,5},{5,4},{6,7},{7,6},{8,9},{9,8},{10,11... | collective-permute-start | bytes 9437192 | tf_op jit(solution)/shard_map/ppermute | solution.py:468
  141.6 3.8 %all-to-all-start.2 = ((bf16[8,48,1536]{2,1,0:T(8,128)(2,1)}), bf16[8,48,1536]{2,1,0:T(8,128)(2,1)S(1)}, u32[]{:S(2)}, u32[]{:S(2)}) async-start(bf16[8,48,1536]{2,1,0:T(8,128)(2,1)} %bitcast.31), calls=%async_computation.2 | async-start | bytes 2359296 | tf_op jit(solution)/shard_map/all_to_all | solution.py:466
  145.3 5.1 %shard_map.167 = (f32[4,128]{1,0:T(4,128)}, bf16[128,1536]{1,0:T(8,128)(2,1)}, bf16[128,1536]{1,0:T(8,128)(2,1)}, bf16[1024,128]{1,0:T(8,128)(2,1)}) custom-call(s32[4,128]{1,0:T(4,128)} %bitcast.41, s32[128,1]{1,0:T(8,128)} %broadcast_in_dim_reshape.4.held_ref, bf16[128,1664]{1,0:T(8,128)(2,1)} %bitcast.32, bf16[128,128]{1,0:T(8,128)(2,1)} %get-tuple-element.50.sent_any, ...), custom_call_target="tpu_custom_call" | custom-call | bytes 11070000 | tf_op jit(solution)/shard_map/pallas_call | solution.py:470
  150.4 11.9 %shard_map.168 = (bf16[384,4096]{1,0:T(8,128)(2,1)}, bf16[128,512]{1,0:T(8,128)(2,1)}, bf16[128,512]{1,0:T(8,128)(2,1)}, f32[128,512]{1,0:T(8,128)}) custom-call(s32[3]{0:T(128)} %pad_add_fusion.at_ref, bf16[1024,128]{1,0:T(8,128)(2,1)} %get-tuple-element.56.cotm_ref, bf16[128,1536]{1,0:T(8,128)(2,1)} %get-tuple-element.57.hidden_ref, ...), custom_call_target="tpu_custom_call" | custom-call | bytes 369000 | tf_op jit(solution)/shard_map/pallas_call | solution.py:484
  162.3 6.4 %collective-permute-start.10 = (bf16[128,512]{1,0:T(8,128)(2,1)}, bf16[128,512]{1,0:T(8,128)(2,1)S(1)}, u32[]{:S(2)}, u32[]{:S(2)}) collective-permute-start(bf16[128,512]{1,0:T(8,128)(2,1)} %get-tuple-element.66), channel_id=1, source_target_pairs={{2,0},{3,1},{4,2},{5,3},{6,4},{7,5},{8,6},{9,7},{10,8},{11,9},{12,... | collective-permute-start | bytes 393224 | tf_op jit(solution)/shard_map/ppermute | solution.py:362
  168.7 2.8 %collective-permute-start.9 = (bf16[128,512]{1,0:T(8,128)(2,1)}, bf16[128,512]{1,0:T(8,128)(2,1)S(1)}, u32[]{:S(2)}, u32[]{:S(2)}) collective-permute-start(bf16[128,512]{1,0:T(8,128)(2,1)} %get-tuple-element.65), channel_id=1, source_target_pairs={{1,0},{2,1},{3,2},{4,3},{5,4},{6,5},{7,6},{8,7},{9,8},{10,9},{11,1... | collective-permute-start | bytes 393224 | tf_op jit(solution)/shard_map/ppermute | solution.py:362
  171.6 0.6 convert_bitcast_fusion.1
  172.1 4.8 %shard_map.169 = (bf16[128,2048]{1,0:T(8,128)(2,1)}, bf16[1440,128]{1,0:T(8,128)(2,1)}) custom-call(bf16[384,4096]{1,0:T(8,128)(2,1)} %get-tuple-element.60.sg_ref, bf16[256,384]{1,0:T(8,128)(2,1)} %get-tuple-element.61.kt_ref, bf16[128,1536]{1,0:T(8,128)(2,1)} %get-tuple-element.62.src_ref, s32[1,1536]{1,0:T(1,128)} %compare_select_fusion.place_ref), custom_call_target="tpu_custom_call" | custom-call | bytes 369000 | tf_op jit(solution)/shard_map/pallas_call | solution.py:510
  177.0 0.3 collective-permute-done.10
  177.3 1.3 collective-permute-done.9
  178.5 0.2 reduce
  178.7 0.7 slice_bitcast_fusion
  179.4 0.7 fusion.8
  (39 shorter events, 0.2 us)
Async XLA Ops:
  7.2 27.2 %copy-start.12 = (s32[128]{0:T(128)S(1)}, s32[128]{0:T(128)}, u32[]{:S(2)}) copy-start(s32[128]{0:T(128)} %param.15) | copy-start | bytes 1540
  7.2 27.9 %copy-start.10 = (bf16[128,256]{1,0:T(8,128)(2,1)S(1)}, bf16[128,256]{1,0:T(8,128)(2,1)}, u32[]{:S(2)}) copy-start(bf16[128,256]{1,0:T(8,128)(2,1)} %param.13) | copy-start | bytes 196612
  7.2 27.9 %copy-start.9 = (bf16[128,256]{1,0:T(8,128)(2,1)S(1)}, bf16[128,256]{1,0:T(8,128)(2,1)}, u32[]{:S(2)}) copy-start(bf16[128,256]{1,0:T(8,128)(2,1)} %param.14) | copy-start | bytes 196612
  7.2 77.5 %all-gather.3.cloned.1.call-start = ((), (), s32[]{:S(2)}) async-start(), calls=%async_computation.3 | async-start | bytes 2654208 | tf_op jit(solution)/shard_map/all_gather | solution.py:370
  8.2 8.1 %collective-permute-start = (bf16[48,1536]{1,0:T(8,128)(2,1)S(1)}, bf16[48,1536]{1,0:T(8,128)(2,1)S(1)}, u32[]{:S(2)}, u32[]{:S(2)}) collective-permute-start(bf16[48,1536]{1,0:T(8,128)(2,1)S(1)} %pad.8), channel_id=1, source_target_pairs={{0,2},{2,0},{1,3},{3,1},{4,6},{6,4},{5,7},{7,5},{8,10},{10,8},{9,1... | collective-permute-start | bytes 442376 | tf_op jit(solution)/shard_map/ppermute | solution.py:353
  26.9 42.8 %all-to-all-start = ((bf16[16,8,3072]{2,1,0:T(8,128)(2,1)}), bf16[16,8,3072]{2,1,0:T(8,128)(2,1)S(1)}, u32[]{:S(2)}, u32[]{:S(2)}) async-start(bf16[16,8,3072]{2,1,0:T(8,128)(2,1)} %bitcast.33), calls=%async_computation | async-start | bytes 1572864 | tf_op jit(solution)/shard_map/all_to_all | solution.py:395
  34.3 104.9 %all-gather.5.cloned.1.call-start = ((), (), s32[]{:S(2)}) async-start(), calls=%async_computation.4 | async-start | bytes 3538944 | tf_op jit(solution)/shard_map/all_gather | solution.py:424
  35.1 35.5 %copy-start.5 = (bf16[128,640]{1,0:T(8,128)(2,1)}, bf16[128,640]{1,0:T(8,128)(2,1)S(1)}, u32[]{:S(2)}) copy-start(bf16[128,640]{1,0:T(8,128)(2,1)S(1)} %fusion.1.own_ref) | copy-start | bytes 491524
  35.1 15.9 %collective-permute-start.1 = (bf16[128,640]{1,0:T(8,128)(2,1)S(1)}, bf16[128,640]{1,0:T(8,128)(2,1)S(1)}, u32[]{:S(2)}, u32[]{:S(2)}) collective-permute-start(bf16[128,640]{1,0:T(8,128)(2,1)S(1)} %fusion.1.own_ref), channel_id=1, source_target_pairs={{0,1},{1,2},{2,3},{3,4},{4,5},{5,6},{6,7},{7,8},{8,9},{9,10},{10,1... | collective-permute-start | bytes 491528 | tf_op jit(solution)/shard_map/ppermute | solution.py:362
  41.5 28.2 %collective-permute-start.2 = (bf16[128,640]{1,0:T(8,128)(2,1)S(1)}, bf16[128,640]{1,0:T(8,128)(2,1)S(1)}, u32[]{:S(2)}, u32[]{:S(2)}) collective-permute-start(bf16[128,640]{1,0:T(8,128)(2,1)S(1)} %fusion.1.own_ref), channel_id=1, source_target_pairs={{0,2},{1,3},{2,4},{3,5},{4,6},{5,7},{6,8},{7,9},{8,10},{9,11},{10,... | collective-permute-start | bytes 491528 | tf_op jit(solution)/shard_map/ppermute | solution.py:362
  45.7 24.0 %collective-permute-start.3 = (bf16[64,1536]{1,0:T(8,128)(2,1)}, bf16[64,1536]{1,0:T(8,128)(2,1)S(1)}, u32[]{:S(2)}, u32[]{:S(2)}) collective-permute-start(bf16[64,1536]{1,0:T(8,128)(2,1)} %get-tuple-element.41), channel_id=1, source_target_pairs={{0,2},{2,0},{1,3},{3,1},{4,6},{6,4},{5,7},{7,5},{8,10},{10,8},{9,1... | collective-permute-start | bytes 589832 | tf_op jit(solution)/shard_map/ppermute | solution.py:399
  51.0 19.6 %copy-start.7 = (bf16[128,640]{1,0:T(8,128)(2,1)}, bf16[128,640]{1,0:T(8,128)(2,1)S(1)}, u32[]{:S(2)}) copy-start(bf16[128,640]{1,0:T(8,128)(2,1)S(1)} %collective-permute-done.1.near_ref) | copy-start | bytes 491524
  69.7 0.9 copy-start.8
  69.7 21.6 %copy-start.1 = (bf16[16,8,3072]{2,1,0:T(8,128)(2,1)}, bf16[16,8,3072]{2,1,0:T(8,128)(2,1)S(1)}, u32[]{:S(2)}) copy-start(bf16[16,8,3072]{2,1,0:T(8,128)(2,1)S(1)} %all-to-all-done) | copy-start | bytes 2359300
  69.7 0.8 copy-start.3
  80.3 4.4 %collective-permute-start.4 = (bf16[128,3072]{1,0:T(8,128)(2,1)S(1)}, bf16[128,3072]{1,0:T(8,128)(2,1)}, u32[]{:S(2)}, u32[]{:S(2)}) collective-permute-start(bf16[128,3072]{1,0:T(8,128)(2,1)S(1)} %bitcast.27), channel_id=1, source_target_pairs={{0,1},{1,0},{2,3},{3,2},{4,5},{5,4},{6,7},{7,6},{8,9},{9,8},{10,11... | collective-permute-start | bytes 2359304 | tf_op jit(solution)/shard_map/ppermute | solution.py:422
  84.7 6.6 %collective-permute-start.5 = (bf16[768,1536]{1,0:T(8,128)(2,1)}, bf16[768,1536]{1,0:T(8,128)(2,1)S(1)}, u32[]{:S(2)}, u32[]{:S(2)}) collective-permute-start(bf16[768,1536]{1,0:T(8,128)(2,1)} %all-gather.3.cloned.1.call-done.wm_any), channel_id=1, source_target_pairs={{0,1},{1,0},{2,3},{3,2},{4,5},{5,4},{6,7},{7,6},{8,9},{9,8},{10,11... | collective-permute-start | bytes 7077896 | tf_op jit(solution)/shard_map/ppermute | solution.py:426
  87.0 38.2 %collective-permute-start.6 = (bf16[128,3072]{1,0:T(8,128)(2,1)S(1)}, bf16[128,3072]{1,0:T(8,128)(2,1)}, u32[]{:S(2)}, u32[]{:S(2)}) collective-permute-start(bf16[128,3072]{1,0:T(8,128)(2,1)S(1)} %bitcast.28), channel_id=1, source_target_pairs={{0,4},{4,0},{1,5},{5,1},{2,6},{6,2},{3,7},{7,3},{8,12},{12,8},{9,1... | collective-permute-start | bytes 2359304 | tf_op jit(solution)/shard_map/ppermute | solution.py:421
  91.3 1.4 copy-start
  99.7 39.6 %all-to-all-start.1 = ((bf16[16,8,1664]{2,1,0:T(8,128)(2,1)}), bf16[16,8,1664]{2,1,0:T(8,128)(2,1)S(1)}, u32[]{:S(2)}, u32[]{:S(2)}) async-start(bf16[16,8,1664]{2,1,0:T(8,128)(2,1)} %bitcast.36), calls=%async_computation.1 | async-start | bytes 851968 | tf_op jit(solution)/shard_map/all_to_all | solution.py:443
  125.1 4.6 %collective-permute-start.7 = (bf16[128,3072]{1,0:T(8,128)(2,1)}, bf16[128,3072]{1,0:T(8,128)(2,1)S(1)}, u32[]{:S(2)}, u32[]{:S(2)}) collective-permute-start(bf16[128,3072]{1,0:T(8,128)(2,1)} %collective-permute-done.6.near_any), channel_id=1, source_target_pairs={{0,1},{1,0},{2,3},{3,2},{4,5},{5,4},{6,7},{7,6},{8,9},{9,8},{10,11... | collective-permute-start | bytes 2359304 | tf_op jit(solution)/shard_map/ppermute | solution.py:442
  129.8 0.9 copy-start.4
  139.2 6.1 %copy-start.2 = (bf16[16,8,1664]{2,1,0:T(8,128)(2,1)}, bf16[16,8,1664]{2,1,0:T(8,128)(2,1)S(1)}, u32[]{:S(2)}) copy-start(bf16[16,8,1664]{2,1,0:T(8,128)(2,1)S(1)} %all-to-all-done.1) | copy-start | bytes 1277956
  139.3 11.1 %collective-permute-start.8 = (bf16[1024,1536]{1,0:T(8,128)(2,1)}, bf16[1024,1536]{1,0:T(8,128)(2,1)}, u32[]{:S(2)}, u32[]{:S(2)}) collective-permute-start(bf16[1024,1536]{1,0:T(8,128)(2,1)} %all-gather.5.cloned.1.call-done.om_any), channel_id=1, source_target_pairs={{0,1},{1,0},{2,3},{3,2},{4,5},{5,4},{6,7},{7,6},{8,9},{9,8},{10,11... | collective-permute-start | bytes 9437192 | tf_op jit(solution)/shard_map/ppermute | solution.py:468
  141.6 35.4 %all-to-all-start.2 = ((bf16[8,48,1536]{2,1,0:T(8,128)(2,1)}), bf16[8,48,1536]{2,1,0:T(8,128)(2,1)S(1)}, u32[]{:S(2)}, u32[]{:S(2)}) async-start(bf16[8,48,1536]{2,1,0:T(8,128)(2,1)} %bitcast.31), calls=%async_computation.2 | async-start | bytes 2359296 | tf_op jit(solution)/shard_map/all_to_all | solution.py:466
  150.4 21.1 %copy-start.11 = (f32[4,128]{1,0:T(4,128)S(1)}, f32[4,128]{1,0:T(4,128)}, u32[]{:S(2)}) copy-start(f32[4,128]{1,0:T(4,128)} %get-tuple-element.68) | copy-start | bytes 6148
  162.3 17.0 %copy-start.6 = (f32[128,512]{1,0:T(8,128)S(1)}, f32[128,512]{1,0:T(8,128)}, u32[]{:S(2)}) copy-start(f32[128,512]{1,0:T(8,128)} %get-tuple-element.64) | copy-start | bytes 786436
  162.3 14.9 %collective-permute-start.10 = (bf16[128,512]{1,0:T(8,128)(2,1)}, bf16[128,512]{1,0:T(8,128)(2,1)S(1)}, u32[]{:S(2)}, u32[]{:S(2)}) collective-permute-start(bf16[128,512]{1,0:T(8,128)(2,1)} %get-tuple-element.66), channel_id=1, source_target_pairs={{2,0},{3,1},{4,2},{5,3},{6,4},{7,5},{8,6},{9,7},{10,8},{11,9},{12,... | collective-permute-start | bytes 393224 | tf_op jit(solution)/shard_map/ppermute | solution.py:362
  168.7 9.8 %collective-permute-start.9 = (bf16[128,512]{1,0:T(8,128)(2,1)}, bf16[128,512]{1,0:T(8,128)(2,1)S(1)}, u32[]{:S(2)}, u32[]{:S(2)}) collective-permute-start(bf16[128,512]{1,0:T(8,128)(2,1)} %get-tuple-element.65), channel_id=1, source_target_pairs={{1,0},{2,1},{3,2},{4,3},{5,4},{6,5},{7,6},{8,7},{9,8},{10,9},{11,1... | collective-permute-start | bytes 393224 | tf_op jit(solution)/shard_map/ppermute | solution.py:362
Sparse Core Ops, SparseCore 0:
  18.1 46.8 all-gather.2
  70.7 67.5 all-gather.4
